TPU v7x, 32 devices: a whole 2x2x4 slice. The times are simulated.
32 devices in a mesh: seq: 2 (over x), fsdp: 16 (over z, y, core).
Axes of the slice: x: 2, y: 2, z: 4, core: 2. Of those that a mesh axis runs over, the one named last changes fastest.
Arguments:
- inputs: bfloat16 [16, 4096, 1024], P('fsdp', 'seq'), may hold values from -6 to 6
- targets: bfloat16 [16, 4096, 1024], P('fsdp', 'seq'), may hold values from -6 to 6
- valid_count: int32 [16], replicated, may hold values from 1024 to 4096, as said below
- gain_mix: bfloat16 [1024], P(('seq', 'fsdp')), may hold values from 0.5 to 1.5
- w_query: bfloat16 [1024, 256], P(('seq', 'fsdp')), may hold values from -0.1875 to 0.1875
- w_key: bfloat16 [1024, 256], P(('seq', 'fsdp')), may hold values from -0.1875 to 0.1875
- w_value: bfloat16 [1024, 1024], P(('seq', 'fsdp')), may hold values from -0.1875 to 0.1875
- w_out: bfloat16 [1024, 1024], P(('seq', 'fsdp')), may hold values from -3 to 3
- gain_ffn: bfloat16 [1024], P(('seq', 'fsdp')), may hold values from 0.5 to 1.5
- w_gate: bfloat16 [1024, 2752], P(('seq', 'fsdp')), may hold values from -0.1875 to 0.1875
- w_up: bfloat16 [1024, 2752], P(('seq', 'fsdp')), may hold values from -0.1875 to 0.1875
- w_down: bfloat16 [1024, 2752], P(('seq', 'fsdp')), may hold values from -0.109375 to 0.109375
Outputs:
- result: bfloat16 [16, 4096, 1024], P('fsdp', 'seq')
- loss: float32 [], replicated
- input_grad: float32 [16, 4096, 1024], P('fsdp', 'seq')
- grad_gain_mix: float32 [1024], P(('seq', 'fsdp'))
- grad_query: float32 [1024, 256], P(('seq', 'fsdp'))
- grad_key: float32 [1024, 256], P(('seq', 'fsdp'))
- grad_value: float32 [1024, 1024], P(('seq', 'fsdp'))
- grad_out: float32 [1024, 1024], P(('seq', 'fsdp'))
- grad_gain_ffn: float32 [1024], P(('seq', 'fsdp'))
- grad_gate: float32 [1024, 2752], P(('seq', 'fsdp'))
- grad_up: float32 [1024, 2752], P(('seq', 'fsdp'))
- grad_down: float32 [1024, 2752], P(('seq', 'fsdp'))
Inputs may be any that keep to these rules, and one draw needn't show every extreme that they name: Tokens of sequence s from position valid_count[s] on carry no target; one sequence has all 4096 and one has 1024.
All inputs are finite; a program needn't handle non-finite values.
Results may differ from a plain program's by a relative error of at most 0.012.
The roundings to bfloat16 on the way count: a program that leaves them out, or rounds other values in their place, can miss the bound.
Values may be sent and summed in bfloat16 or wider, within the bound.
A program may use at most 384 MiB of HBM per device.

v0:
```python
import math

import jax
import jax.numpy as jnp
import numpy as np
from jax import lax
from jax.sharding import PartitionSpec as P

HEADS = 16
FEAT = 16
HEAD_DIM = 64
BLK = 512
PHI = 153


epsilon = 1e-05
highest = lax.Precision.HIGHEST


def pair_tables(width):
    upper_rows, upper_cols = np.triu_indices(width, 1)
    count_pairs = upper_rows.size
    left = np.zeros((width, count_pairs), np.float32)
    right = np.zeros((width, count_pairs), np.float32)
    left[upper_rows, np.arange(count_pairs)] = 1.0
    right[upper_cols, np.arange(count_pairs)] = 1.0
    return (jnp.asarray(left), jnp.asarray(right))


def features(values):
    width = values.shape[-1]
    left, right = pair_tables(width)
    square = values * values * (1.0 / math.sqrt(2.0 * width))
    cross = (
        jnp.dot(values, left, precision=highest)
        * jnp.dot(values, right, precision=highest)
        * (1.0 / math.sqrt(width))
    )
    linear = values * width ** (-0.25)
    ones = jnp.ones(values.shape[:-1] + (1,), values.dtype)
    return jnp.concatenate([ones, linear, square, cross], -1)


def inner_rows(left, right):
    return lax.dot_general(
        left, right, (((0,), (0,)), ((), ())), preferred_element_type=jnp.float32
    )


def times_transposed(left, right):
    return lax.dot_general(
        left, right, (((1,), (1,)), ((), ())), preferred_element_type=jnp.float32
    )


def blocked(array):
    return array.reshape((array.shape[0] // BLK, BLK) + array.shape[1:])


def block_forward(query, key, value, state, total):
    length = query.shape[0]
    factor = 1.0 / math.sqrt(query.shape[-1])
    scores = jnp.einsum("thf,shf->hts", query, key, preferred_element_type=jnp.float32) * factor
    causal = (jnp.arange(length)[:, None] >= jnp.arange(length)[None, :]).astype(jnp.float32)
    weights = (1.0 + scores + 0.5 * scores * scores) * causal
    numerator = jnp.einsum(
        "hts,she->the", weights.astype(jnp.bfloat16), value, preferred_element_type=jnp.float32
    )
    query_feat = features(query.astype(jnp.float32))
    numerator = numerator + jnp.einsum("thp,hpe->the", query_feat, state, precision=highest)
    denominator = jnp.sum(weights, -1).T + jnp.einsum(
        "thp,hp->th", query_feat, total, precision=highest
    )
    return (numerator, denominator, scores, weights, query_feat, causal)


def mixer_forward(query, key, value, state, total):
    rows = query.shape[0]

    def step(carry, pieces):
        state_now, total_now = carry
        q_blk, k_blk, v_blk = pieces
        numerator, denominator, scores, weights, query_feat, causal = block_forward(
            q_blk, k_blk, v_blk, state_now, total_now
        )
        output = numerator / denominator[..., None]
        key_feat = features(k_blk.astype(jnp.float32))
        state_now = state_now + jnp.einsum(
            "shp,she->hpe", key_feat, v_blk.astype(jnp.float32), precision=highest
        )
        total_now = total_now + jnp.sum(key_feat, 0)
        return ((state_now, total_now), output)

    _, outputs = lax.scan(step, (state, total), (blocked(query), blocked(key), blocked(value)))
    return outputs.reshape((rows,) + outputs.shape[2:])


def mixer_backward(query, key, value, state, total, grad_mixed, later_fn):
    rows = query.shape[0]
    factor = 1.0 / math.sqrt(query.shape[-1])

    def step(carry, pieces):
        state_now, total_now = carry
        q_blk, k_blk, v_blk, g_blk = pieces
        numerator, denominator, scores, weights, query_feat, causal = block_forward(
            q_blk, k_blk, v_blk, state_now, total_now
        )
        output = numerator / denominator[..., None]
        numer_back = (g_blk / denominator[..., None]).astype(jnp.bfloat16)
        numer_wide = numer_back.astype(jnp.float32)
        denom_back = -jnp.sum(g_blk * output, -1) / denominator
        weight_back = (
            jnp.einsum("the,she->hts", numer_back, v_blk, preferred_element_type=jnp.float32)
            + denom_back.T[:, :, None]
        )
        score_back = (weight_back * (1.0 + scores) * causal).astype(jnp.bfloat16)
        query_back = (
            jnp.einsum("hts,shf->thf", score_back, k_blk, preferred_element_type=jnp.float32)
            * factor
        )
        key_back = (
            jnp.einsum("hts,thf->shf", score_back, q_blk, preferred_element_type=jnp.float32)
            * factor
        )
        value_back = jnp.einsum(
            "hts,the->she",
            weights.astype(jnp.bfloat16),
            numer_back,
            preferred_element_type=jnp.float32,
        )
        qfeat_back = (
            jnp.einsum("the,hpe->thp", numer_wide, state_now, precision=highest)
            + denom_back[..., None] * total_now[None]
        )
        _, pull = jax.vjp(features, q_blk.astype(jnp.float32))
        query_back = query_back + pull(qfeat_back)[0]
        state_back = jnp.einsum("thp,the->hpe", query_feat, numer_wide, precision=highest)
        total_back = jnp.einsum("thp,th->hp", query_feat, denom_back, precision=highest)
        key_feat = features(k_blk.astype(jnp.float32))
        state_now = state_now + jnp.einsum(
            "shp,she->hpe", key_feat, v_blk.astype(jnp.float32), precision=highest
        )
        total_now = total_now + jnp.sum(key_feat, 0)
        return ((state_now, total_now), (query_back, key_back, value_back, state_back, total_back))

    key_blocks = blocked(key)
    value_blocks = blocked(value)
    _, (query_back, key_back, value_back, state_back, total_back) = lax.scan(
        step, (state, total), (blocked(query), key_blocks, value_blocks, blocked(grad_mixed))
    )
    local_state = jnp.sum(state_back, 0)
    local_total = jnp.sum(total_back, 0)
    later_state, later_total = later_fn(local_state, local_total)
    after_state = later_state[None] + (local_state[None] - jnp.cumsum(state_back, 0))
    after_total = later_total[None] + (local_total[None] - jnp.cumsum(total_back, 0))
    key_wide = key_blocks.astype(jnp.float32)
    value_wide = value_blocks.astype(jnp.float32)
    key_feat = features(key_wide)
    kfeat_back = (
        jnp.einsum("nshe,nhpe->nshp", value_wide, after_state, precision=highest)
        + after_total[:, None]
    )
    value_back = value_back + jnp.einsum(
        "nshp,nhpe->nshe", key_feat, after_state, precision=highest
    )
    _, pull = jax.vjp(features, key_wide)
    key_back = key_back + pull(kfeat_back)[0]
    shaped = (rows, query.shape[1] * query.shape[2])
    return (
        query_back.reshape(shaped).astype(jnp.bfloat16),
        key_back.reshape(shaped).astype(jnp.bfloat16),
        value_back.reshape(rows, value.shape[1] * value.shape[2]).astype(jnp.bfloat16),
    )


def no_later(state_sum, total_sum):
    return (jnp.zeros_like(state_sum), jnp.zeros_like(total_sum))


def body(
    inputs,
    targets,
    valid_count,
    gain_mix,
    w_query,
    w_key,
    w_value,
    w_out,
    gain_ffn,
    w_gate,
    w_up,
    w_down,
):
    seq_parts = lax.axis_size("seq")
    fsdp_parts = lax.axis_size("fsdp")
    seq_index = lax.axis_index("seq")
    batch_index = lax.axis_index("fsdp")
    rows = inputs.shape[1]
    tokens = inputs[0].astype(jnp.float32)
    target = targets[0].astype(jnp.float32)
    owners = jnp.arange(valid_count.shape[0])
    count = jnp.sum(jnp.where(owners == batch_index, valid_count, 0))
    total_valid = jnp.sum(valid_count).astype(jnp.float32)
    positions = seq_index * rows + jnp.arange(rows)
    valid = (positions < count).astype(jnp.float32)[:, None]
    gathered = (
        lax.all_gather(gain_mix, ("seq", "fsdp"), axis=0, tiled=True),
        lax.all_gather(w_query, ("seq", "fsdp"), axis=0, tiled=True),
        lax.all_gather(w_key, ("seq", "fsdp"), axis=0, tiled=True),
        lax.all_gather(w_value, ("seq", "fsdp"), axis=0, tiled=True),
        lax.all_gather(w_out, ("seq", "fsdp"), axis=0, tiled=True),
        lax.all_gather(gain_ffn, ("seq", "fsdp"), axis=0, tiled=True),
        lax.all_gather(w_gate, ("seq", "fsdp"), axis=0, tiled=True),
        lax.all_gather(w_up, ("seq", "fsdp"), axis=0, tiled=True),
        lax.all_gather(w_down, ("seq", "fsdp"), axis=0, tiled=True),
    )
    (
        full_mix,
        full_query,
        full_key,
        full_value,
        full_out,
        full_ffn,
        full_gate,
        full_up,
        full_down,
    ) = gathered
    gain_one = full_mix.astype(jnp.float32)
    gain_two = full_ffn.astype(jnp.float32)
    scale_mix = lax.rsqrt(jnp.mean(tokens * tokens, -1, keepdims=True) + epsilon)
    unit_mix = tokens * scale_mix
    normed = (unit_mix * gain_one).astype(jnp.bfloat16)
    query = jnp.dot(normed, full_query, preferred_element_type=jnp.float32).astype(jnp.bfloat16)
    key = jnp.dot(normed, full_key, preferred_element_type=jnp.float32).astype(jnp.bfloat16)
    value = jnp.dot(normed, full_value, preferred_element_type=jnp.float32).astype(jnp.bfloat16)
    head_query, head_key, head_value = (
        lax.all_to_all(query, "seq", split_axis=1, concat_axis=0, tiled=True),
        lax.all_to_all(key, "seq", split_axis=1, concat_axis=0, tiled=True),
        lax.all_to_all(value, "seq", split_axis=1, concat_axis=0, tiled=True),
    )
    local_heads = HEADS // seq_parts
    shaped = (
        head_query.reshape(-1, local_heads, FEAT),
        head_key.reshape(-1, local_heads, FEAT),
        head_value.reshape(-1, local_heads, HEAD_DIM),
    )
    state_start = jnp.zeros((local_heads, PHI, HEAD_DIM), jnp.float32)
    total_start = jnp.zeros((local_heads, PHI), jnp.float32)
    head_out = mixer_forward(shaped[0], shaped[1], shaped[2], state_start, total_start)
    head_low = head_out.reshape(head_out.shape[0], -1).astype(jnp.bfloat16)
    mixed = lax.all_to_all(head_low, "seq", split_axis=0, concat_axis=1, tiled=True)
    resid = tokens + jnp.dot(mixed, full_out, preferred_element_type=jnp.float32)
    scale_ffn = lax.rsqrt(jnp.mean(resid * resid, -1, keepdims=True) + epsilon)
    unit_ffn = resid * scale_ffn
    normed_ffn = (unit_ffn * gain_two).astype(jnp.bfloat16)
    gate = jnp.dot(normed_ffn, full_gate, preferred_element_type=jnp.float32)
    upward = jnp.dot(normed_ffn, full_up, preferred_element_type=jnp.float32)
    sigmoid = jax.nn.sigmoid(gate)
    activated = gate * sigmoid
    hidden = (activated * upward).astype(jnp.bfloat16)
    full_result = resid + times_transposed(hidden, full_down)
    difference = valid * (full_result - target)
    local_error = 0.5 * jnp.sum(difference * difference)
    error = lax.psum(local_error, ("seq", "fsdp"))
    loss = 2.0 * error / (inputs.shape[2] * total_valid)
    branch_back = difference.astype(jnp.bfloat16)
    grad_wdown = inner_rows(branch_back, hidden)
    hidden_back = (
        jnp.dot(branch_back, full_down, preferred_element_type=jnp.float32)
        .astype(jnp.bfloat16)
        .astype(jnp.float32)
    )
    gate_back = (hidden_back * upward * sigmoid * (1.0 + gate * (1.0 - sigmoid))).astype(
        jnp.bfloat16
    )
    up_back = (hidden_back * activated).astype(jnp.bfloat16)
    grad_wgate = inner_rows(normed_ffn, gate_back)
    grad_wup = inner_rows(normed_ffn, up_back)
    ffn_back = times_transposed(gate_back, full_gate) + times_transposed(up_back, full_up)
    grad_gain_two = jnp.sum(ffn_back * unit_ffn, 0)
    scaled_back = ffn_back * gain_two
    resid_back = difference + scale_ffn * (
        scaled_back - unit_ffn * jnp.mean(scaled_back * unit_ffn, -1, keepdims=True)
    )
    attended_back = resid_back.astype(jnp.bfloat16)
    grad_wout = inner_rows(mixed, attended_back)
    mixed_back = times_transposed(attended_back, full_out).astype(jnp.bfloat16)
    head_grad = lax.all_to_all(mixed_back, "seq", split_axis=1, concat_axis=0, tiled=True)
    head_grad = head_grad.reshape(-1, local_heads, HEAD_DIM).astype(jnp.float32)
    head_qb, head_kb, head_vb = mixer_backward(
        shaped[0], shaped[1], shaped[2], state_start, total_start, head_grad, no_later
    )
    query_back, key_back, value_back = (
        lax.all_to_all(head_qb, "seq", split_axis=0, concat_axis=1, tiled=True),
        lax.all_to_all(head_kb, "seq", split_axis=0, concat_axis=1, tiled=True),
        lax.all_to_all(head_vb, "seq", split_axis=0, concat_axis=1, tiled=True),
    )
    grad_wquery = inner_rows(normed, query_back)
    grad_wkey = inner_rows(normed, key_back)
    grad_wvalue = inner_rows(normed, value_back)
    normed_back = (
        times_transposed(query_back, full_query)
        + times_transposed(key_back, full_key)
        + times_transposed(value_back, full_value)
    )
    grad_gain_one = jnp.sum(normed_back * unit_mix, 0)
    mix_back = normed_back * gain_one
    input_back = resid_back + scale_mix * (
        mix_back - unit_mix * jnp.mean(mix_back * unit_mix, -1, keepdims=True)
    )
    terms = (
        grad_gain_one,
        grad_wquery,
        grad_wkey,
        grad_wvalue,
        grad_wout,
        grad_gain_two,
        grad_wgate,
        grad_wup,
        grad_wdown,
    )
    grouped = tuple((term.reshape((seq_parts, fsdp_parts, -1) + term.shape[1:]) for term in terms))
    arrived = (
        lax.all_to_all(
            grouped[0].astype(jnp.bfloat16), "fsdp", split_axis=1, concat_axis=1, tiled=True
        ).astype(jnp.float32),
        lax.all_to_all(
            grouped[1].astype(jnp.bfloat16), "fsdp", split_axis=1, concat_axis=1, tiled=True
        ).astype(jnp.float32),
        lax.all_to_all(
            grouped[2].astype(jnp.bfloat16), "fsdp", split_axis=1, concat_axis=1, tiled=True
        ).astype(jnp.float32),
        lax.all_to_all(
            grouped[3].astype(jnp.bfloat16), "fsdp", split_axis=1, concat_axis=1, tiled=True
        ).astype(jnp.float32),
        lax.all_to_all(
            grouped[4].astype(jnp.bfloat16), "fsdp", split_axis=1, concat_axis=1, tiled=True
        ).astype(jnp.float32),
        lax.all_to_all(
            grouped[5].astype(jnp.bfloat16), "fsdp", split_axis=1, concat_axis=1, tiled=True
        ).astype(jnp.float32),
        lax.all_to_all(
            grouped[6].astype(jnp.bfloat16), "fsdp", split_axis=1, concat_axis=1, tiled=True
        ).astype(jnp.float32),
        lax.all_to_all(
            grouped[7].astype(jnp.bfloat16), "fsdp", split_axis=1, concat_axis=1, tiled=True
        ).astype(jnp.float32),
        lax.all_to_all(
            grouped[8].astype(jnp.bfloat16), "fsdp", split_axis=1, concat_axis=1, tiled=True
        ).astype(jnp.float32),
    )
    summed = tuple((jnp.sum(piece, 1) for piece in arrived))
    shares = (
        lax.psum_scatter(
            summed[0].astype(jnp.bfloat16), "seq", scatter_dimension=0, tiled=True
        ).astype(jnp.float32),
        lax.psum_scatter(
            summed[1].astype(jnp.bfloat16), "seq", scatter_dimension=0, tiled=True
        ).astype(jnp.float32),
        lax.psum_scatter(
            summed[2].astype(jnp.bfloat16), "seq", scatter_dimension=0, tiled=True
        ).astype(jnp.float32),
        lax.psum_scatter(
            summed[3].astype(jnp.bfloat16), "seq", scatter_dimension=0, tiled=True
        ).astype(jnp.float32),
        lax.psum_scatter(
            summed[4].astype(jnp.bfloat16), "seq", scatter_dimension=0, tiled=True
        ).astype(jnp.float32),
        lax.psum_scatter(
            summed[5].astype(jnp.bfloat16), "seq", scatter_dimension=0, tiled=True
        ).astype(jnp.float32),
        lax.psum_scatter(
            summed[6].astype(jnp.bfloat16), "seq", scatter_dimension=0, tiled=True
        ).astype(jnp.float32),
        lax.psum_scatter(
            summed[7].astype(jnp.bfloat16), "seq", scatter_dimension=0, tiled=True
        ).astype(jnp.float32),
        lax.psum_scatter(
            summed[8].astype(jnp.bfloat16), "seq", scatter_dimension=0, tiled=True
        ).astype(jnp.float32),
    )
    shares = tuple((share.reshape((-1,) + share.shape[2:]) for share in shares))
    return (
        full_result.astype(jnp.bfloat16)[None],
        loss,
        input_back[None],
        shares[0],
        shares[1],
        shares[2],
        shares[3],
        shares[4],
        shares[5],
        shares[6],
        shares[7],
        shares[8],
    )


def solution(mesh):
    return jax.shard_map(
        body,
        mesh=mesh,
        in_specs=(
            P("fsdp", "seq", None),
            P("fsdp", "seq", None),
            P(),
            P(("seq", "fsdp")),
            P(("seq", "fsdp"), None),
            P(("seq", "fsdp"), None),
            P(("seq", "fsdp"), None),
            P(("seq", "fsdp"), None),
            P(("seq", "fsdp")),
            P(("seq", "fsdp"), None),
            P(("seq", "fsdp"), None),
            P(("seq", "fsdp"), None),
        ),
        out_specs=(
            P("fsdp", "seq", None),
            P(),
            P("fsdp", "seq", None),
            P(("seq", "fsdp")),
            P(("seq", "fsdp"), None),
            P(("seq", "fsdp"), None),
            P(("seq", "fsdp"), None),
            P(("seq", "fsdp"), None),
            P(("seq", "fsdp")),
            P(("seq", "fsdp"), None),
            P(("seq", "fsdp"), None),
            P(("seq", "fsdp"), None),
        ),
        check_vma=False,
    )
```

profile of v0, /device:TPU:0, one launch (start us, length us, event | category | flops | bytes accessed | tf_op | source)
XLA Modules:
  0.0 2080.3 jit_solution(110246368628591117)
XLA Ops:
  11.1 42.1 %all-reduce.4 = (bf16[1024]{0:T(1024)(128)(2,1)S(1)}, bf16[1024]{0:T(1024)(128)(2,1)}) all-reduce(bf16[1024]{0:T(1024)(128)(2,1)S(1)} %dynamic-update-slice, bf16[1024]{0:T(1024)(128)(2,1)S(1)} %dynamic-update-slice.1), channel_id=1, replica_groups=mesh['seq'=2,'fsdp'=16] {'seq','fsdp'}, use_global_device_ids=true, to_apply=%add | all-reduce | flops 2048 | bytes 8192
  63.0 42.1 %all_gather.28 = bf16[1024,256]{1,0:T(8,128)(2,1)S(1)} all-gather(bf16[32,256]{1,0:T(8,128)(2,1)S(1)} %copy-done.44), channel_id=1, replica_groups=mesh['seq'=2,'fsdp'=16] {'seq','fsdp'}, dimensions={0}, use_global_device_ids=true | all-gather | bytes 540672 | tf_op jit(solution)/shard_map/all_gather | solution.py:209
  113.9 39.0 %all_gather.30 = bf16[1024,256]{1,0:T(8,128)(2,1)S(1)} all-gather(bf16[32,256]{1,0:T(8,128)(2,1)S(1)} %copy-done.45), channel_id=1, replica_groups=mesh['seq'=2,'fsdp'=16] {'seq','fsdp'}, dimensions={0}, use_global_device_ids=true | all-gather | bytes 540672 | tf_op jit(solution)/shard_map/all_gather | solution.py:208
  161.8 9.5 convolution_convert_fusion.5
  192.4 47.8 %all-to-all-done.1 = bf16[2048,2,512]{0,2,1:T(8,128)(2,1)} async-done(((bf16[2048,2,512]{0,2,1:T(8,128)(2,1)}), bf16[2048,2,512]{0,2,1:T(8,128)(2,1)}, u32[]{:S(2)}, u32[]{:S(2)}) %all-to-all-start.1) | async-done | bytes 4194336 | tf_op jit(solution)/shard_map/all_to_all | solution.py:239
  240.2 8.7 copy.201
  261.6 221.2 %while.48 = (s32[]{:T(128)}, f32[8,153,64]{1,2,0:T(8,128)}, f32[8,153]{1,0:T(8,128)}, bf16[8,512,8,64]{1,3,2,0:T(8,128)(2,1)}, bf16[8,512,8,16]{1,3,2,0:T(8,128)...) while((s32[]{:T(128)}, f32[8,153,64]{1,2,0:T(8,128)}, ...), condition=%wide.region_4.5_spmd.clone.clone.clone.clone, body=%wide.region_1.4_spmd.sunk.clone.clone.clone.sunk.clone | while | flops 1724427008 | bytes 53687544 | solution.py:94
  517.5 45.3 %all-to-all-done.3 = bf16[2,2048,512]{1,2,0:T(8,128)(2,1)} async-done(((bf16[2,2048,512]{1,2,0:T(8,128)(2,1)}), bf16[2,2048,512]{1,2,0:T(8,128)(2,1)}, u32[]{:S(2)}, u32[]{:S(2)}) %all-to-all-start.3) | async-done | bytes 4194336 | tf_op jit(solution)/shard_map/all_to_all | solution.py:251
  562.8 10.0 multiply_reduce_fusion.3
  579.0 19.7 fusion.224
  598.7 27.8 %multiply_convert_fusion.1 = (bf16[2048,2752]{0,1:T(8,128)(2,1)}, f32[2048,2752]{0,1:T(8,128)}) fusion(f32[2048,2752]{0,1:T(8,128)} %fusion.224, bf16[2048,1024]{0,1:T(8,128)(2,1)} %multiply_convert_fusion.2, bf16[1024,2752]{1,0:T(8,128)(2,1)} %all-gather.12.cloned.1.call-done), kind=kOutput, calls=%fused_computation.188 | convolution fusion | flops 11576541184 | bytes 66191360 | tf_op jit(solution)/shard_map/dot_general | solution.py:257
  626.4 22.4 %fusion.192 = (bf16[2048,1024]{0,1:T(8,128)(2,1)}, f32[2048,1024]{0,1:T(8,128)}) fusion(bf16[1,2048,1024]{1,2,0:T(8,128)(2,1)} %copy.209, f32[2048]{0:T(1024)S(1)} %fusion.207, f32[2048,1024]{0,1:T(8,128)} %copy-done.8, bf16[1024,2752]{1,0:T(8,128)(2,1)} %all-gather.14.cloned.1.call-done, bf16[2048,2752]{0,1:T(8,128)(2,1)} %get-tuple-element.793), kind=kOutput, calls=%fused_computation.254 | convolution fusion | flops 11553210368 | bytes 42082304 | tf_op jit(solution)/shard_map/dot_general | solution.py:51
  648.8 33.7 %fusion.154 = (bf16[2048,2752]{0,1:T(8,128)(2,1)}, bf16[2048,2752]{0,1:T(8,128)(2,1)}) fusion(f32[2048,2752]{0,1:T(8,128)} %fusion.224, f32[2048,2752]{0,1:T(8,128)} %get-tuple-element.794, bf16[2048,1024]{0,1:T(8,128)(2,1)} %get-tuple-element.795, bf16[1024,2752]{1,0:T(8,128)(2,1)} %all-gather.14.cloned.1.call-done), kind=kOutput, calls=%fused_computation.187 | convolution fusion | flops 11627266048 | bytes 77463552 | tf_op jit(solution)/shard_map/dot_general | solution.py:269
  682.5 18.8 fusion.225
  701.3 23.0 %multiply_reduce_fusion = (bf16[1024]{0:T(1024)(128)(2,1)S(1)}, f32[2048]{0:T(1024)S(1)}, f32[2048,1024]{0,1:T(8,128)}) fusion(f32[2048,1024]{0,1:T(8,128)} %copy-done.8, f32[2048]{0:T(1024)S(1)} %copy-done.35, f32[1024]{0:T(1024)S(1)} %copy-done.39, f32[2048,1024]{0,1:T(8,128)} %fusion.225, bf16[1024,2752]{1,0:T(8,128)(2,1)} %all-gather.12.cloned.1.call-done, ...), kind=kOutput, calls=%fused_computation.227 | convolution fusion | flops 11557401600 | bytes 42096640 | tf_op jit(solution)/shard_map/dot_general | solution.py:51
  724.3 17.1 multiply_add_fusion
  741.4 9.2 convolution_convert_fusion.4
  756.4 10.2 fusion.217
  766.6 17.6 multiply_multiply_fusion.4
  784.9 18.6 all-to-all-done.4
  812.1 11.1 copy.212
  823.1 11.7 reshape.236
  834.8 417.9 %while.49 = (s32[]{:T(128)}, f32[8,153,64]{1,2,0:T(8,128)}, f32[8,153]{1,0:T(8,128)}, bf16[8,512,8,16]{1,3,2,0:T(8,128)(2,1)}, f32[8,512,8,16]{1,3,2,0:T(8,128)}...) while((s32[]{:T(128)}, f32[8,153,64]{1,2,0:T(8,128)}, ...), condition=%wide.region_15.16_spmd.clone.clone.clone.clone, body=%wide.region_11.15_spmd.sunk.clone.clone.clone.sunk.clone | while | flops 3592051968 | bytes 113944904 | solution.py:148
  1260.4 17.2 add_bitcast_fusion
  1277.6 17.0 fusion.163
  1294.6 19.4 fusion.195
  1345.1 9.3 all-to-all-done.5
  1378.7 19.7 fusion.181
  1423.1 9.2 fusion.202
  1433.8 37.5 %all-to-all-done.7 = bf16[2,2048,512]{1,2,0:T(8,128)(2,1)} async-done(((bf16[2,2048,512]{1,2,0:T(8,128)(2,1)}), bf16[2,2048,512]{1,2,0:T(8,128)(2,1)}, u32[]{:S(2)}, u32[]{:S(2)}) %all-to-all-start.7) | async-done | bytes 4194336 | tf_op jit(solution)/shard_map/all_to_all | solution.py:296
  1479.9 9.1 fusion.227
  1497.4 20.8 all-to-all-done.12
  1518.2 11.4 all-to-all-start.8
  1545.2 17.5 convolution_convert_fusion.1
  1576.5 9.9 all-to-all-done.11
  1586.4 11.5 all-to-all-start.16
  1597.9 17.6 convolution_convert_fusion.2
  1615.4 8.3 copy.242
  1629.4 73.5 %all-to-all-done.16 = bf16[2,16,32,2752]{3,2,0,1:T(8,128)(2,1)} async-done(((bf16[2,16,32,2752]{3,2,0,1:T(8,128)(2,1)}), bf16[2,16,32,2752]{3,2,0,1:T(8,128)(2,1)}, u32[]{:S(2)}, u32[]{:S(2)}) %all-to-all-start.16) | async-done | bytes 5636128 | tf_op jit(solution)/shard_map/all_to_all | solution.py:348
  1702.9 26.3 %all-to-all-start.15 = ((bf16[2,16,32,2752]{3,2,0,1:T(8,128)(2,1)}), bf16[2,16,32,2752]{3,2,0,1:T(8,128)(2,1)}, u32[]{:S(2)}, u32[]{:S(2)}) async-start(bf16[2,16,32,2752]{3,2,0,1:T(8,128)(2,1)} %copy.243), calls=%async_computation.20 | async-start | bytes 11534336 | tf_op jit(solution)/shard_map/all_to_all | solution.py:345
  1729.2 17.5 convolution_convert_fusion.3
  1746.7 8.3 copy.240
  1760.6 73.6 %all-to-all-done.15 = bf16[2,16,32,2752]{3,2,0,1:T(8,128)(2,1)} async-done(((bf16[2,16,32,2752]{3,2,0,1:T(8,128)(2,1)}), bf16[2,16,32,2752]{3,2,0,1:T(8,128)(2,1)}, u32[]{:S(2)}, u32[]{:S(2)}) %all-to-all-start.15) | async-done | bytes 5636128 | tf_op jit(solution)/shard_map/all_to_all | solution.py:345
  1834.2 26.0 %all-to-all-start.14 = ((bf16[2,16,32,2752]{3,2,0,1:T(8,128)(2,1)}), bf16[2,16,32,2752]{3,2,0,1:T(8,128)(2,1)}, u32[]{:S(2)}, u32[]{:S(2)}) async-start(bf16[2,16,32,2752]{3,2,0,1:T(8,128)(2,1)} %copy.241), calls=%async_computation.18 | async-start | bytes 11534336 | tf_op jit(solution)/shard_map/all_to_all | solution.py:342
  1872.0 135.2 %psum.7 = f32[]{:T(128)} all-reduce(f32[]{:T(128)S(6)} %mul.471), channel_id=1, replica_groups=mesh['seq'=2,'fsdp'=16] {'seq','fsdp'}, use_global_device_ids=true, to_apply=%region_8.9 | all-reduce | flops 1 | bytes 8 | tf_op jit(solution)/shard_map/psum | solution.py:264
  2022.4 11.3 fusion.177
  2033.7 9.3 copy.247
  2060.4 9.8 reduce-scatter.16.cloned.1.call-done
  (769 shorter events, 947.3 us)
Async XLA Ops:
  7.2 154.6 %all-gather.6.cloned.1.call-start = ((), (), s32[]{:S(2)}) async-start(), calls=%async_computation.24 | async-start | bytes 2162688 | tf_op jit(solution)/shard_map/all_gather | solution.py:210
  7.9 509.6 %all-gather.8.cloned.1.call-start = ((), (), s32[]{:S(2)}) async-start(), calls=%async_computation.25 | async-start | bytes 2162688 | tf_op jit(solution)/shard_map/all_gather | solution.py:211
  8.7 570.4 %all-gather.10.cloned.1.call-start = ((), (), s32[]{:S(2)}) async-start(), calls=%async_computation.26 | async-start | bytes 5947392 | tf_op jit(solution)/shard_map/all_gather | solution.py:213
  53.2 51.9 %copy-start.36 = (f32[1024]{0:T(1024)}, f32[1024]{0:T(1024)S(1)}, u32[]{:S(2)}) copy-start(f32[1024]{0:T(1024)S(1)} %convert_element_type.258) | copy-start | bytes 12292
  59.8 45.4 %copy-start = (bf16[1,2048,1024]{1,2,0:T(8,128)(2,1)S(1)}, bf16[1,2048,1024]{1,2,0:T(8,128)(2,1)}, u32[]{:S(2)}) copy-start(bf16[1,2048,1024]{1,2,0:T(8,128)(2,1)} %copy.199) | copy-start | bytes 12582916
  63.0 43.1 %copy-start.28 = (f32[2048]{0:T(1024)}, f32[2048]{0:T(1024)S(1)}, u32[]{:S(2)}) copy-start(f32[2048]{0:T(1024)S(1)} %add_rsqrt_fusion.1) | copy-start | bytes 24580
  110.3 47.9 %all-to-all-start = ((bf16[2048,2,128]{0,2,1:T(8,128)(2,1)}), bf16[2048,2,128]{0,2,1:T(8,128)(2,1)S(1)}, u32[]{:S(2)}, u32[]{:S(2)}) async-start(bf16[2048,2,128]{0,2,1:T(8,128)(2,1)} %bitcast.2), calls=%async_computation | async-start | bytes 2097152 | tf_op jit(solution)/shard_map/all_to_all | solution.py:238
  158.2 18.9 all-to-all-start.2
  177.1 63.0 %all-to-all-start.1 = ((bf16[2048,2,512]{0,2,1:T(8,128)(2,1)}), bf16[2048,2,512]{0,2,1:T(8,128)(2,1)}, u32[]{:S(2)}, u32[]{:S(2)}) async-start(bf16[2048,2,512]{0,2,1:T(8,128)(2,1)} %bitcast.547), calls=%async_computation.1 | async-start | bytes 8388608 | tf_op jit(solution)/shard_map/all_to_all | solution.py:239
  182.7 415.9 %all-gather.12.cloned.1.call-start = ((), (), s32[]{:S(2)}) async-start(), calls=%async_computation.27 | async-start | bytes 5947392 | tf_op jit(solution)/shard_map/all_gather | solution.py:214
  503.2 59.6 %all-to-all-start.3 = ((bf16[2,2048,512]{1,2,0:T(8,128)(2,1)}), bf16[2,2048,512]{1,2,0:T(8,128)(2,1)}, u32[]{:S(2)}, u32[]{:S(2)}) async-start(bf16[2,2048,512]{1,2,0:T(8,128)(2,1)} %copy.207), calls=%async_computation.3 | async-start | bytes 8388608 | tf_op jit(solution)/shard_map/all_to_all | solution.py:251
  509.0 117.5 %all-gather.14.cloned.1.call-start = ((), (), s32[]{:S(2)}) async-start(), calls=%async_computation.28 | async-start | bytes 5947392 | tf_op jit(solution)/shard_map/all_gather | solution.py:215
  509.6 63.3 %copy-start.38 = (f32[1024]{0:T(1024)}, f32[1024]{0:T(1024)S(1)}, u32[]{:S(2)}) copy-start(f32[1024]{0:T(1024)S(1)} %convert_element_type.265) | copy-start | bytes 12292
  682.5 18.8 copy-start.35
  682.5 18.8 copy-start.39
  701.3 23.0 %copy-start.9 = (bf16[1,2048,1024]{1,2,0:T(8,128)(2,1)S(1)}, bf16[1,2048,1024]{1,2,0:T(8,128)(2,1)}, u32[]{:S(2)}) copy-start(bf16[1,2048,1024]{1,2,0:T(8,128)(2,1)} %copy.209) | copy-start | bytes 12582916
  741.4 9.2 copy-start.7
  750.6 52.8 %all-to-all-start.4 = ((bf16[2048,2,512]{0,2,1:T(8,128)(2,1)}), bf16[2048,2,512]{0,2,1:T(8,128)(2,1)}, u32[]{:S(2)}, u32[]{:S(2)}) async-start(bf16[2048,2,512]{0,2,1:T(8,128)(2,1)} %bitcast.548), calls=%async_computation.4 | async-start | bytes 8388608 | tf_op jit(solution)/shard_map/all_to_all | solution.py:288
  756.4 10.2 copy-start.42
  803.4 515.0 %all-to-all-start.13 = ((bf16[2,16,32]{2,0,1:T(2,128)(2,1)}), bf16[2,16,32]{2,0,1:T(2,128)(2,1)}, u32[]{:S(2)}, u32[]{:S(2)}) async-start(bf16[2,16,32]{2,0,1:T(2,128)(2,1)} %copy.239), calls=%async_computation.17 | async-start | bytes 16384 | tf_op jit(solution)/shard_map/all_to_all | solution.py:339
  823.1 11.7 copy-start.6
  823.1 11.7 copy-start.15
  823.1 11.7 copy-start.17
  1260.4 17.2 copy-start.43
  1277.6 17.0 copy-start.4
  1277.6 17.0 copy-start.41
  1318.4 18.0 all-to-all-start.6
  1336.3 18.1 all-to-all-start.5
  1354.4 20.0 all-to-all-start.10
  1374.4 24.0 %copy-start.23 = (bf16[2,16,32,256]{3,2,0,1:T(8,128)(2,1)}, bf16[2,16,32,256]{3,2,0,1:T(8,128)(2,1)S(1)}, u32[]{:S(2)}) copy-start(bf16[2,16,32,256]{3,2,0,1:T(8,128)(2,1)S(1)} %all-to-all-done.10) | copy-start | bytes 1572868
  1374.4 41.9 %all-to-all-start.9 = ((bf16[2,16,32,256]{3,2,0,1:T(8,128)(2,1)}), bf16[2,16,32,256]{3,2,0,1:T(8,128)(2,1)S(1)}, u32[]{:S(2)}, u32[]{:S(2)}) async-start(bf16[2,16,32,256]{3,2,0,1:T(8,128)(2,1)} %copy.234), calls=%async_computation.9 | async-start | bytes 1048576 | tf_op jit(solution)/shard_map/all_to_all | solution.py:327
  1417.1 54.2 %all-to-all-start.7 = ((bf16[2,2048,512]{1,2,0:T(8,128)(2,1)}), bf16[2,2048,512]{1,2,0:T(8,128)(2,1)}, u32[]{:S(2)}, u32[]{:S(2)}) async-start(bf16[2,2048,512]{1,2,0:T(8,128)(2,1)} %copy.230), calls=%async_computation.7 | async-start | bytes 8388608 | tf_op jit(solution)/shard_map/all_to_all | solution.py:296
  1471.3 46.8 %all-to-all-start.12 = ((bf16[2,16,32,1024]{3,2,0,1:T(8,128)(2,1)}), bf16[2,16,32,1024]{3,2,0,1:T(8,128)(2,1)S(1)}, u32[]{:S(2)}, u32[]{:S(2)}) async-start(bf16[2,16,32,1024]{3,2,0,1:T(8,128)(2,1)} %copy.238), calls=%async_computation.15 | async-start | bytes 4194304 | tf_op jit(solution)/shard_map/all_to_all | solution.py:336
  1479.9 9.1 copy-start.1
  1518.2 20.9 %all-to-all-start.8 = ((bf16[2,16,32]{2,0,1:T(2,128)(2,1)}), bf16[2,16,32]{2,0,1:T(2,128)(2,1)S(1)}, u32[]{:S(2)}, u32[]{:S(2)}) async-start(bf16[2,16,32]{2,0,1:T(2,128)(2,1)} %copy.233), calls=%async_computation.8 | async-start | bytes 16384 | tf_op jit(solution)/shard_map/all_to_all | solution.py:324
  1539.0 47.3 %all-to-all-start.11 = ((bf16[2,16,32,1024]{3,2,0,1:T(8,128)(2,1)}), bf16[2,16,32,1024]{3,2,0,1:T(8,128)(2,1)}, u32[]{:S(2)}, u32[]{:S(2)}) async-start(bf16[2,16,32,1024]{3,2,0,1:T(8,128)(2,1)} %copy.236), calls=%async_computation.13 | async-start | bytes 4194304 | tf_op jit(solution)/shard_map/all_to_all | solution.py:333
  1586.4 116.5 %all-to-all-start.16 = ((bf16[2,16,32,2752]{3,2,0,1:T(8,128)(2,1)}), bf16[2,16,32,2752]{3,2,0,1:T(8,128)(2,1)}, u32[]{:S(2)}, u32[]{:S(2)}) async-start(bf16[2,16,32,2752]{3,2,0,1:T(8,128)(2,1)} %copy.245), calls=%async_computation.22 | async-start | bytes 11534336 | tf_op jit(solution)/shard_map/all_to_all | solution.py:348
  1702.9 131.3 %all-to-all-start.15 = ((bf16[2,16,32,2752]{3,2,0,1:T(8,128)(2,1)}), bf16[2,16,32,2752]{3,2,0,1:T(8,128)(2,1)}, u32[]{:S(2)}, u32[]{:S(2)}) async-start(bf16[2,16,32,2752]{3,2,0,1:T(8,128)(2,1)} %copy.243), calls=%async_computation.20 | async-start | bytes 11534336 | tf_op jit(solution)/shard_map/all_to_all | solution.py:345
  1760.6 99.7 %copy-start.24 = (bf16[2,16,32,256]{3,2,0,1:T(8,128)(2,1)S(1)}, bf16[2,16,32,256]{3,2,0,1:T(8,128)(2,1)}, u32[]{:S(2)}) copy-start(bf16[2,16,32,256]{3,2,0,1:T(8,128)(2,1)} %copy-done.23) | copy-start | bytes 1572868
  1760.6 100.4 %copy-start.26 = (bf16[2,16,32,256]{3,2,0,1:T(8,128)(2,1)S(1)}, bf16[2,16,32,256]{3,2,0,1:T(8,128)(2,1)}, u32[]{:S(2)}) copy-start(bf16[2,16,32,256]{3,2,0,1:T(8,128)(2,1)} %copy-done.25) | copy-start | bytes 1572868
  1834.2 218.4 %all-to-all-start.14 = ((bf16[2,16,32,2752]{3,2,0,1:T(8,128)(2,1)}), bf16[2,16,32,2752]{3,2,0,1:T(8,128)(2,1)}, u32[]{:S(2)}, u32[]{:S(2)}) async-start(bf16[2,16,32,2752]{3,2,0,1:T(8,128)(2,1)} %copy.241), calls=%async_computation.18 | async-start | bytes 11534336 | tf_op jit(solution)/shard_map/all_to_all | solution.py:342
  1860.2 154.8 %reduce-scatter.10.cloned.1.call-start = ((), (), s32[]{:S(2)}) async-start(), calls=%async_computation.30 | async-start | bytes 49152 | tf_op jit(solution)/shard_map/reduce_scatter | solution.py:360
  1861.0 155.4 %reduce-scatter.8.cloned.1.call-start = ((), (), s32[]{:S(2)}) async-start(), calls=%async_computation.29 | async-start | bytes 49152 | tf_op jit(solution)/shard_map/reduce_scatter | solution.py:357
  1861.8 181.2 %reduce-scatter.14.cloned.1.call-start = ((), (), s32[]{:S(2)}) async-start(), calls=%async_computation.32 | async-start | bytes 196608 | tf_op jit(solution)/shard_map/reduce_scatter | solution.py:366
  1862.9 188.2 %reduce-scatter.12.cloned.1.call-start = ((), (), s32[]{:S(2)}) async-start(), calls=%async_computation.31 | async-start | bytes 196608 | tf_op jit(solution)/shard_map/reduce_scatter | solution.py:363
  1865.7 191.3 %reduce-scatter.20.cloned.1.call-start = ((), (), s32[]{:S(2)}) async-start(), calls=%async_computation.35 | async-start | bytes 540672 | tf_op jit(solution)/shard_map/reduce_scatter | solution.py:378
  1870.1 188.6 %reduce-scatter.18.cloned.1.call-start = ((), (), s32[]{:S(2)}) async-start(), calls=%async_computation.34 | async-start | bytes 540672 | tf_op jit(solution)/shard_map/reduce_scatter | solution.py:375
  2022.1 48.1 %reduce-scatter.16.cloned.1.call-start = ((), (), s32[]{:S(2)}) async-start(), calls=%async_computation.33 | async-start | bytes 540672 | tf_op jit(solution)/shard_map/reduce_scatter | solution.py:372
  (119 other events, 372.2 us)
Sparse Core Ops, SparseCore 0:
  10.9 59.1 all-gather.5
  73.0 58.4 all-gather.7
  134.4 79.6 all-gather.9
  216.8 66.0 all-gather.11
  512.4 73.2 all-gather.13
  1863.5 10.1 reduce-scatter.9
  1876.5 9.8 reduce-scatter.7
  1889.1 10.2 reduce-scatter.13
  1902.2 10.2 reduce-scatter.11
  1915.1 12.7 reduce-scatter.19
  2022.2 13.6 reduce-scatter.17
  2057.1 13.0 reduce-scatter.15
where the time goes:
time: 2100 us; the launch traced here: 2080 us
  matrix products  879 us (42%)
  waiting for transfers between devices  369 us (18%)
  blocking collectives  264 us (13%)
  local copies, waits for them, and re-layouts  250 us (12%)
  other arithmetic  155 us (7%)
  starting transfers between devices  141 us (7%)
    psum x1, blocking collectives, body(): error = lax.psum(local_error, ('seq', 'fsdp'))  135 us
    dot_general x42, matrix products, features(): jnp.dot(values, left, precision=highest)  97.1 us
    dot_general x7, matrix products, times_transposed(): lax.dot_general(left, right, (((1,), (1,)), ((), ())), preferred_element_...  92.9 us
    dot_general x42, matrix products, features(): jnp.dot(values, right, precision=highest)  92.4 us
    dot_general x7, matrix products, inner_rows(): lax.dot_general(left, right, (((0,), (0,)), ((), ())), preferred_element_...  75.7 us
    all_to_all x1, waiting for transfers between devices, body(): lax.all_to_all(grouped[7].astype(jnp.bfloat16), 'fsdp', split_axis=1, con...  73.6 us
    all_to_all x1, waiting for transfers between devices, body(): lax.all_to_all(grouped[8].astype(jnp.bfloat16), 'fsdp', split_axis=1, con...  73.5 us
    dot_general x16, matrix products, block_forward(): jnp.einsum('thf,shf->hts', query, key, preferred_element_type=jnp.float32)  57.2 us
  transfers between devices with their start and end apart: 29, of which 13 were waited for; matrix products, arithmetic and copies ran while one was open for 54% of the time, Pallas kernels for 0%

commit v1 on v0

v1 whole, which is shorter than its diff:
```python
import functools
import math

import jax
import jax.numpy as jnp
import numpy as np
from jax import lax
from jax.experimental import pallas as pl
from jax.experimental.pallas import tpu as pltpu
from jax.sharding import PartitionSpec as P

HEADS = 16
FEAT = 16
HEAD_DIM = 64
HROWS = 2 * FEAT + HEAD_DIM
CUT = 256
GROUPS = 11
FROWS = GROUPS * FEAT
VROWS = HEAD_DIM + 16
HG = 4

epsilon = 1e-05
F32 = jnp.float32
BF16 = jnp.bfloat16
NN = (((1,), (0,)), ((), ()))
NT = (((1,), (1,)), ((), ()))
TN = (((0,), (0,)), ((), ()))


def dot(left, right, dims):
    return lax.dot_general(left, right, dims, preferred_element_type=F32)


def first_row(rows, cols, count=1):
    return (lax.broadcasted_iota(jnp.int32, (rows, cols), 0) < count).astype(F32)


def rolled(u, shift):
    return pltpu.roll(u, (FEAT - shift) % FEAT, 0)


def phi_rows(u, const):
    groups = [u * u]
    for d in range(1, 9):
        groups.append(u * rolled(u, d))
    groups.append(u)
    groups.append(const)
    return jnp.concatenate([g.astype(BF16) for g in groups], 0)


def phi_pull(grad, u):
    total = grad[9 * FEAT : 10 * FEAT] + 2.0 * grad[0:FEAT] * u
    for d in range(1, 9):
        g = grad[d * FEAT : (d + 1) * FEAT]
        total = total + g * rolled(u, d) + rolled(g * u, FEAT - d)
    return total


def lane_scale():
    group = lax.broadcasted_iota(jnp.int32, (1, FROWS), 1) // FEAT
    scale = jnp.where((group == 0) | (group == 8), 1.0 / 32.0, 1.0 / 16.0)
    scale = jnp.where(group == 9, 0.25, scale)
    return jnp.where(group == 10, 1.0, scale)


def causal_mask():
    s = lax.broadcasted_iota(jnp.int32, (CUT, CUT), 0)
    t = lax.broadcasted_iota(jnp.int32, (CUT, CUT), 1)
    return s <= t


def state_kernel(blocks, qkv_ref, out_ref):
    ones2 = first_row(16, CUT, 2).astype(BF16)
    const = first_row(FEAT, CUT)

    def step(b, sums):
        cols = pl.ds(pl.multiple_of(b * CUT, CUT), CUT)
        fresh = []
        for h in range(HG):
            base = h * HROWS
            k = qkv_ref[base + FEAT : base + 2 * FEAT, cols].astype(F32)
            v = qkv_ref[base + 2 * FEAT : base + HROWS, cols]
            v_aug = jnp.concatenate([v, ones2], 0)
            fresh.append(sums[h] + dot(v_aug, phi_rows(k, const), NT))
        return tuple(fresh)

    zero = jnp.zeros((VROWS, FROWS), F32)
    sums = lax.fori_loop(0, blocks, step, (zero,) * HG)
    for h in range(HG):
        out_ref[h] = sums[h]


def forward_kernel(blocks, qkv_ref, init_ref, mixed_ref, den_ref, saved_ref, state):
    ones2 = first_row(16, CUT, 2).astype(BF16)
    const = first_row(FEAT, CUT)
    one_low = const.astype(BF16)
    scale = 2.0 * lane_scale()
    mask = causal_mask()
    state[...] = init_ref[...]

    def step(b, carry):
        cols = pl.ds(pl.multiple_of(b * CUT, CUT), CUT)
        for h in range(HG):
            base = h * HROWS
            q = qkv_ref[base : base + FEAT, cols]
            k = qkv_ref[base + FEAT : base + 2 * FEAT, cols]
            v = qkv_ref[base + 2 * FEAT : base + HROWS, cols]
            v_aug = jnp.concatenate([v, ones2], 0)
            k_aug = jnp.concatenate([k, one_low], 0)
            q_aug = jnp.concatenate([q * 0.25, one_low], 0)
            u = dot(k_aug, q_aug, TN)
            weight = jnp.where(mask, u * u + 1.0, 0.0).astype(BF16)
            low = (state[h] * scale).astype(BF16)
            saved_ref[h, b] = low
            numer = dot(v_aug, weight, NN) + dot(low, phi_rows(q.astype(F32), const), NN)
            den = numer[HEAD_DIM : HEAD_DIM + 1]
            mixed_ref[h * HEAD_DIM : (h + 1) * HEAD_DIM, cols] = (
                numer[:HEAD_DIM] / den
            ).astype(BF16)
            den_ref[0, h : h + 1, cols] = 0.5 * den
            state[h] += dot(v_aug, phi_rows(k.astype(F32), const), NT)
        return carry

    lax.fori_loop(0, blocks, step, 0)


def back_state_kernel(blocks, qkv_ref, grad_ref, mixed_ref, den_ref, nb_ref, out_ref):
    const = first_row(FEAT, CUT)
    row = lax.broadcasted_iota(jnp.int32, (16, CUT), 0)

    def step(b, sums):
        cols = pl.ds(pl.multiple_of(b * CUT, CUT), CUT)
        fresh = []
        for h in range(HG):
            base = h * HROWS
            q = qkv_ref[base : base + FEAT, cols].astype(F32)
            rows = slice(h * HEAD_DIM, (h + 1) * HEAD_DIM)
            g = grad_ref[rows, cols].astype(F32)
            inverse = 1.0 / den_ref[0, h : h + 1, cols]
            db = -inverse * jnp.sum(
                g * mixed_ref[rows, cols].astype(F32), axis=0, keepdims=True
            )
            nb = (g * inverse).astype(BF16)
            high = db.astype(BF16).astype(F32)
            tail = jnp.where(row == 0, high, jnp.where(row == 1, db - high, 0.0)).astype(BF16)
            nb_aug = jnp.concatenate([nb, tail], 0)
            nb_ref[h, :, cols] = nb_aug
            fresh.append(sums[h] + dot(nb_aug, phi_rows(q, const), NT))
        return tuple(fresh)

    zero = jnp.zeros((VROWS, FROWS), F32)
    sums = lax.fori_loop(0, blocks, step, (zero,) * HG)
    for h in range(HG):
        out_ref[h] = sums[h]


def backward_kernel(blocks, qkv_ref, nb_ref, saved_ref, init_ref, out_ref, state):
    ones2 = first_row(16, CUT, 2).astype(BF16)
    const = first_row(FEAT, CUT)
    one_low = const.astype(BF16)
    scale = lane_scale()
    mask = causal_mask()
    state[...] = init_ref[...]

    def step(i, carry):
        b = blocks - 1 - i
        cols = pl.ds(pl.multiple_of(b * CUT, CUT), CUT)
        for h in range(HG):
            base = h * HROWS
            q = qkv_ref[base : base + FEAT, cols]
            k = qkv_ref[base + FEAT : base + 2 * FEAT, cols]
            v = qkv_ref[base + 2 * FEAT : base + HROWS, cols]
            qf = q.astype(F32)
            kf = k.astype(F32)
            q4 = q * 0.25
            nb = nb_ref[h, :, cols]
            v_aug = jnp.concatenate([v, ones2], 0)
            k_aug = jnp.concatenate([k, one_low], 0)
            q_aug = jnp.concatenate([q4, one_low], 0)
            u = dot(k_aug, q_aug, TN)
            weight = jnp.where(mask, u * u + 1.0, 0.0).astype(BF16)
            wb = dot(v_aug, nb, TN)
            sb = jnp.where(mask, wb * u, 0.0).astype(BF16)
            q_feat_back = dot(saved_ref[h, b], nb, TN)
            dq = 0.25 * dot(k, sb, NN) + 0.5 * phi_pull(q_feat_back, qf)
            low = (state[h] * scale).astype(BF16)
            k_feat_back = dot(low, v_aug, TN)
            dk = dot(q4, sb, NT) + phi_pull(k_feat_back, kf)
            dv = 0.5 * dot(nb[:HEAD_DIM], weight, NT) + dot(
                low[:HEAD_DIM], phi_rows(kf, const), NN
            )
            out_ref[base : base + FEAT, cols] = dq.astype(BF16)
            out_ref[base + FEAT : base + 2 * FEAT, cols] = dk.astype(BF16)
            out_ref[base + 2 * FEAT : base + HROWS, cols] = dv.astype(BF16)
            state[h] += dot(nb, phi_rows(qf, const), NT)
        return carry

    lax.fori_loop(0, blocks, step, 0)


def head_spec(rows, cols):
    return pl.BlockSpec((HG * rows, cols), lambda g: (g, 0))


def lead_spec(*tail):
    return pl.BlockSpec((HG,) + tail, lambda g: (g,) + (0,) * len(tail))


VMEM_LIMIT = pltpu.CompilerParams(vmem_limit_bytes=56 * 1024 * 1024)


def local_state(qkv):
    cols = qkv.shape[1]
    return pl.pallas_call(
        functools.partial(state_kernel, cols // CUT),
        grid=(HEADS // HG,),
        in_specs=[head_spec(HROWS, cols)],
        out_specs=lead_spec(VROWS, FROWS),
        out_shape=jax.ShapeDtypeStruct((HEADS, VROWS, FROWS), F32),
        compiler_params=VMEM_LIMIT,
        name="key_state",
    )(qkv)


def attention_forward(qkv, init):
    cols = qkv.shape[1]
    blocks = cols // CUT
    return pl.pallas_call(
        functools.partial(forward_kernel, blocks),
        grid=(HEADS // HG,),
        in_specs=[head_spec(HROWS, cols), lead_spec(VROWS, FROWS)],
        out_specs=[
            head_spec(HEAD_DIM, cols),
            pl.BlockSpec((1, HG, cols), lambda g: (g, 0, 0)),
            lead_spec(blocks, VROWS, FROWS),
        ],
        out_shape=[
            jax.ShapeDtypeStruct((HEADS * HEAD_DIM, cols), BF16),
            jax.ShapeDtypeStruct((HEADS // HG, HG, cols), F32),
            jax.ShapeDtypeStruct((HEADS, blocks, VROWS, FROWS), BF16),
        ],
        scratch_shapes=[pltpu.VMEM((HG, VROWS, FROWS), F32)],
        compiler_params=VMEM_LIMIT,
        name="attend",
    )(qkv, init)


def local_back_state(qkv, grad, mixed, den):
    cols = qkv.shape[1]
    return pl.pallas_call(
        functools.partial(back_state_kernel, cols // CUT),
        grid=(HEADS // HG,),
        in_specs=[
            head_spec(HROWS, cols),
            head_spec(HEAD_DIM, cols),
            head_spec(HEAD_DIM, cols),
            pl.BlockSpec((1, HG, cols), lambda g: (g, 0, 0)),
        ],
        out_specs=[lead_spec(VROWS, cols), lead_spec(VROWS, FROWS)],
        out_shape=[
            jax.ShapeDtypeStruct((HEADS, VROWS, cols), BF16),
            jax.ShapeDtypeStruct((HEADS, VROWS, FROWS), F32),
        ],
        compiler_params=VMEM_LIMIT,
        name="query_state",
    )(qkv, grad, mixed, den)


def attention_backward(qkv, nb, saved, init):
    cols = qkv.shape[1]
    blocks = cols // CUT
    return pl.pallas_call(
        functools.partial(backward_kernel, blocks),
        grid=(HEADS // HG,),
        in_specs=[
            head_spec(HROWS, cols),
            lead_spec(VROWS, cols),
            lead_spec(blocks, VROWS, FROWS),
            lead_spec(VROWS, FROWS),
        ],
        out_specs=head_spec(HROWS, cols),
        out_shape=jax.ShapeDtypeStruct((HEADS * HROWS, cols), BF16),
        scratch_shapes=[pltpu.VMEM((HG, VROWS, FROWS), F32)],
        compiler_params=VMEM_LIMIT,
        name="attend_back",
    )(qkv, nb, saved, init)


def shifted_sum(array, parts, sign):
    total = jnp.zeros_like(array)
    for shift in range(1, parts):
        if sign > 0:
            pairs = [(i, i + shift) for i in range(parts - shift)]
        else:
            pairs = [(i + shift, i) for i in range(parts - shift)]
        total = total + lax.ppermute(array, "seq", pairs)
    return total


def body(
    inputs,
    targets,
    valid_count,
    gain_mix,
    w_query,
    w_key,
    w_value,
    w_out,
    gain_ffn,
    w_gate,
    w_up,
    w_down,
):
    both = ("seq", "fsdp")
    seq_parts = lax.axis_size("seq")
    seq_index = lax.axis_index("seq")
    batch_index = lax.axis_index("fsdp")
    rows, width = inputs.shape[1:]
    hidden_units = w_gate.shape[1]
    tokens = inputs[0].astype(F32)
    target = targets[0].astype(F32)
    owners = jnp.arange(valid_count.shape[0])
    count = jnp.sum(jnp.where(owners == batch_index, valid_count, 0))
    total_valid = jnp.sum(valid_count).astype(F32)
    positions = seq_index * rows + jnp.arange(rows)
    valid = (positions < count).astype(F32)[:, None]
    gains = jnp.pad(jnp.stack([gain_mix, gain_ffn], 1), ((0, 0), (0, 126)))
    early = jnp.concatenate([gains, w_query, w_key, w_value], 1)
    early = lax.all_gather(early, both, axis=0, tiled=True)
    gain_one = early[:, 0].astype(F32)
    gain_two = early[:, 1].astype(F32)
    late = lax.all_gather(
        jnp.concatenate([w_out, w_gate, w_up, w_down], 1), both, axis=0, tiled=True
    )
    full_out = late[:, :width]
    full_gate = late[:, width : width + hidden_units]
    full_up = late[:, width + hidden_units : width + 2 * hidden_units]
    full_down = late[:, width + 2 * hidden_units :]
    lead = HEADS * FEAT
    w_qkv = jnp.concatenate(
        [
            early[:, 128 : 128 + lead].reshape(width, HEADS, FEAT),
            early[:, 128 + lead : 128 + 2 * lead].reshape(width, HEADS, FEAT),
            early[:, 128 + 2 * lead :].reshape(width, HEADS, HEAD_DIM),
        ],
        2,
    ).reshape(width, HEADS * HROWS)
    w_qkv_t = w_qkv.T
    scale_mix = lax.rsqrt(jnp.mean(tokens * tokens, -1, keepdims=True) + epsilon)
    unit_mix = tokens * scale_mix
    normed = (unit_mix * gain_one).astype(BF16)
    qkv = dot(w_qkv_t, normed, NT).astype(BF16)
    state = shifted_sum(local_state(qkv), seq_parts, 1)
    mixed, den, saved = attention_forward(qkv, state)
    resid = tokens + dot(mixed, full_out, TN)
    scale_ffn = lax.rsqrt(jnp.mean(resid * resid, -1, keepdims=True) + epsilon)
    unit_ffn = resid * scale_ffn
    normed_ffn = (unit_ffn * gain_two).astype(BF16)
    gate = dot(normed_ffn, full_gate, NN)
    upward = dot(normed_ffn, full_up, NN)
    sigmoid = jax.nn.sigmoid(gate)
    activated = gate * sigmoid
    hidden = (activated * upward).astype(BF16)
    full_result = resid + dot(hidden, full_down, NT)
    difference = valid * (full_result - target)
    local_error = 0.5 * jnp.sum(difference * difference)
    error = lax.psum(local_error, both)
    loss = 2.0 * error / (width * total_valid)
    branch_back = difference.astype(BF16)
    grad_down = dot(branch_back, hidden, TN)
    hidden_back = dot(branch_back, full_down, NN).astype(BF16).astype(F32)
    gate_back = (hidden_back * upward * sigmoid * (1.0 + gate * (1.0 - sigmoid))).astype(BF16)
    up_back = (hidden_back * activated).astype(BF16)
    grad_gate = dot(normed_ffn, gate_back, TN)
    grad_up = dot(normed_ffn, up_back, TN)
    ffn_back = dot(gate_back, full_gate, NT) + dot(up_back, full_up, NT)
    grad_gain_two = jnp.sum(ffn_back * unit_ffn, 0)
    scaled_back = ffn_back * gain_two
    resid_back = difference + scale_ffn * (
        scaled_back - unit_ffn * jnp.mean(scaled_back * unit_ffn, -1, keepdims=True)
    )
    attended_back = resid_back.astype(BF16)
    grad_out = dot(mixed, attended_back, NN)
    late_grads = jnp.concatenate(
        [g.astype(BF16) for g in (grad_out, grad_gate, grad_up, grad_down)], 1
    )
    late_sums = scatter(late_grads)
    mixed_back = dot(full_out, attended_back, NT).astype(BF16)
    nb, back = local_back_state(qkv, mixed_back, mixed, den)
    later = shifted_sum(back, seq_parts, -1)
    qkv_back = attention_backward(qkv, nb, saved, later)
    grad_qkv = dot(qkv_back, normed, NN)
    normed_back = dot(qkv_back, w_qkv_t, TN)
    grad_gain_one = jnp.sum(normed_back * unit_mix, 0)
    mix_back = normed_back * gain_one
    input_back = resid_back + scale_mix * (
        mix_back - unit_mix * jnp.mean(mix_back * unit_mix, -1, keepdims=True)
    )
    grad_gains = jnp.pad(jnp.stack([grad_gain_one, grad_gain_two], 1), ((0, 0), (0, 126)))
    early_grads = jnp.concatenate([grad_gains.astype(BF16), grad_qkv.astype(BF16).T], 1)
    early_sums = scatter(early_grads)
    qkv_sums = early_sums[:, 128:].reshape(-1, HEADS, HROWS)
    own = early_sums.shape[0]
    return (
        full_result.astype(BF16)[None],
        loss,
        input_back[None],
        early_sums[:, 0],
        qkv_sums[:, :, :FEAT].reshape(own, lead),
        qkv_sums[:, :, FEAT : 2 * FEAT].reshape(own, lead),
        qkv_sums[:, :, 2 * FEAT :].reshape(own, HEADS * HEAD_DIM),
        late_sums[:, :width],
        early_sums[:, 1],
        late_sums[:, width : width + hidden_units],
        late_sums[:, width + hidden_units : width + 2 * hidden_units],
        late_sums[:, width + 2 * hidden_units :],
    )


def scatter(grads):
    seq_parts = lax.axis_size("seq")
    fsdp_parts = lax.axis_size("fsdp")
    grouped = grads.reshape((seq_parts, fsdp_parts, -1) + grads.shape[1:])
    part = lax.psum_scatter(grouped, "seq", scatter_dimension=0, tiled=True)
    part = lax.psum_scatter(part, "fsdp", scatter_dimension=1, tiled=True)
    return part.reshape((-1,) + grads.shape[1:]).astype(F32)


def solution(mesh):
    both = P(("seq", "fsdp"))
    rows = P(("seq", "fsdp"), None)
    tokens = P("fsdp", "seq", None)
    return jax.shard_map(
        body,
        mesh=mesh,
        in_specs=(tokens, tokens, P(), both, rows, rows, rows, rows, both, rows, rows, rows),
        out_specs=(tokens, P(), tokens, both, rows, rows, rows, rows, both, rows, rows, rows),
        check_vma=False,
    )
```

time: 2100 us -> 1140 us (0.54)
  matrix products: 879 us -> 254 us
  blocking collectives: 264 us -> 39.4 us
  waiting for transfers between devices: 369 us -> 537 us
  local copies, waits for them, and re-layouts: 250 us -> 86.4 us
  starting transfers between devices: 141 us -> 5.1 us
  Pallas kernels: 0 us -> 113 us
  other arithmetic: 155 us -> 78.1 us
    dot_general x243 -> x15, matrix products: 879 us -> 254 us  [dot(): return lax.dot_general(left, right, dims, preferred_element_type=F32)]
    reduce_scatter x7 -> x4, waiting for transfers between devices: 9.86 us -> 408 us  [the longest x2 271 us: scatter(): part = lax.psum_scatter(grouped, 'seq', scatter_dimension=0, tiled=True)]
    all_to_all x17 -> x0, waiting for transfers between devices: 356 us -> none  [the longest x1 73.6 us: body(): lax.all_to_all(grouped[7].astype(jnp.bfloat16), 'fsdp', split_axis=1, con...]
    all_to_all x17 -> x0, starting transfers between devices: 140 us -> none  [the longest x1 26.3 us: body(): lax.all_to_all(grouped[7].astype(jnp.bfloat16), 'fsdp', split_axis=1, con...]
    convert_element_type x28 -> x0, local copies, waits for them, and re-layouts: 121 us -> none  [the longest x2 22.7 us: body(): head_grad = head_grad.reshape(-1, local_heads, HEAD_DIM).astype(jnp.float32)]
    pallas_call x0 -> x4, Pallas kernels: none -> 113 us  [the longest x1 53.2 us: attention_backward(): pl.pallas_call(functools.partial(backward_kernel, blocks), grid=(HEADS //...]
    psum x1, blocking collectives: 135 us -> 39.4 us  [body(): error = lax.psum(local_error, both)]
    all_gather x2 -> x0, blocking collectives: 81 us -> none  [the longest x1 42.1 us: body(): lax.all_gather(w_key, ('seq', 'fsdp'), axis=0, tiled=True)]
  transfers between devices with their start and end apart: 29 -> 8, of which waited for: 13 -> 8; matrix products, arithmetic and copies ran while one was open for 54% -> 16% of each run, Pallas kernels for 0% -> 4%
where the time goes in v1:
time: 1140 us; the launch traced here: 1130 us
  waiting for transfers between devices  537 us (47%)
  matrix products  254 us (22%)
  Pallas kernels  113 us (10%)
  local copies, waits for them, and re-layouts  86.4 us (8%)
  other arithmetic  78.1 us (7%)
  blocking collectives  39.4 us (3%)
  between operations  17.8 us (2%)
    reduce_scatter x2, waiting for transfers between devices, scatter(): part = lax.psum_scatter(grouped, 'seq', scatter_dimension=0, tiled=True)  271 us
    dot_general x15, matrix products, dot(): return lax.dot_general(left, right, dims, preferred_element_type=F32)  254 us
    reduce_scatter x2, waiting for transfers between devices, scatter(): part = lax.psum_scatter(part, 'fsdp', scatter_dimension=1, tiled=True)  137 us
    pallas_call x1, Pallas kernels, attention_backward(): pl.pallas_call(functools.partial(backward_kernel, blocks), grid=(HEADS //...  53.2 us
    all_gather x1, waiting for transfers between devices, body(): early = lax.all_gather(early, both, axis=0, tiled=True)  52.7 us
    ppermute x2, waiting for transfers between devices, shifted_sum(): total = total + lax.ppermute(array, 'seq', pairs)  48.2 us
    unnamed x62, local copies, waits for them, and re-layouts  42.7 us
    psum x1, blocking collectives, body(): error = lax.psum(local_error, both)  39.4 us
  transfers between devices with their start and end apart: 8, of which 8 were waited for; matrix products, arithmetic and copies ran while one was open for 16% of the time, Pallas kernels for 4%

profile of v1, /device:TPU:0, one launch (start us, length us, event | category | flops | bytes accessed | tf_op | source)
XLA Modules:
  0.0 1131.2 jit_solution(14010922150886998943)
XLA Ops:
  8.0 1.5 fusion.65
  9.6 2.0 concatenate.17
  11.7 6.5 copy.58
  18.2 3.1 fusion.19
  21.3 52.7 %all-gather.3.cloned.1.call-done = bf16[1024,1664]{1,0:T(8,128)(2,1)} async-done(((bf16[32,1664]{1,0:T(8,128)(2,1)}), bf16[1024,1664]{1,0:T(8,128)(2,1)}) %all-gather.3.cloned.1.call-update) | async-done | bytes 3407888 | tf_op jit(solution)/shard_map/all_gather | solution.py:329
  75.7 3.1 slice.78
  78.8 2.9 copy.84
  81.6 1.3 convert_reduce_fusion
  83.6 1.4 copy-done.9
  85.0 11.0 convolution_convert_fusion.1.qkv_ref
  96.0 11.0 key_state.1
  107.0 3.6 collective-permute-start
  110.6 6.6 copy.64
  118.4 33.2 %collective-permute-done.init_ref = f32[16,80,176]{2,1,0:T(8,128)S(1)} collective-permute-done((f32[16,80,176]{2,1,0:T(8,128)}, f32[16,80,176]{2,1,0:T(8,128)S(1)}, u32[]{:S(2)}, u32[]{:S(2)}) %collective-permute-start) | collective-permute-done | bytes 901152 | tf_op jit(solution)/shard_map/ppermute | solution.py:296
  152.6 35.7 %attend.1 = (bf16[1024,2048]{1,0:T(8,128)(2,1)}, f32[4,4,2048]{2,1,0:T(4,128)}, bf16[16,8,80,176]{3,2,1,0:T(8,128)(2,1)}) custom-call(bf16[1536,2048]{1,0:T(8,128)(2,1)} %convolution_convert_fusion.1.qkv_ref, f32[16,80,176]{2,1,0:T(8,128)} %copy-done.12), custom_call_target="tpu_custom_call" | custom-call | tf_op jit(solution)/shard_map/attend/pallas_call | solution.py:228
  188.3 27.7 %all-gather.5.cloned.1.call-done = bf16[1024,9280]{1,0:T(8,128)(2,1)} async-done(((bf16[32,9280]{1,0:T(8,128)(2,1)}), bf16[1024,9280]{1,0:T(8,128)(2,1)}) %all-gather.5.cloned.1.call-update) | async-done | bytes 19005456 | tf_op jit(solution)/shard_map/all_gather | solution.py:332
  216.0 9.6 multiply_reduce_fusion.3
  225.7 3.4 copy-done.2
  229.8 2.0 copy-done.7
  231.8 17.7 %fusion.30 = f32[2048,2752]{0,1:T(8,128)} fusion(bf16[2048,1024]{0,1:T(8,128)(2,1)S(1)} %multiply_convert_fusion.1, bf16[1024,9280]{1,0:T(8,128)(2,1)} %all-gather.5.cloned.1.call-done), kind=kOutput, calls=%fused_computation.50 | convolution fusion | flops 11542724608 | bytes 32505856 | tf_op jit(solution)/shard_map/dot_general | solution.py:31
  249.5 32.6 %multiply_convert_fusion = (bf16[2048,2752]{0,1:T(8,128)(2,1)}, f32[2048,2752]{0,1:T(8,128)}) fusion(f32[2048,2752]{0,1:T(8,128)} %fusion.30, bf16[2048,1024]{0,1:T(8,128)(2,1)} %copy-done.7, bf16[1024,9280]{1,0:T(8,128)(2,1)} %all-gather.5.cloned.1.call-done), kind=kOutput, calls=%fused_computation.6 | convolution fusion | flops 11576541184 | bytes 66322432 | tf_op jit(solution)/shard_map/dot_general | solution.py:31
  282.0 20.8 %fusion.53 = (bf16[2048,1024]{0,1:T(8,128)(2,1)}, f32[2048,1024]{0,1:T(8,128)}) fusion(bf16[1,2048,1024]{1,2,0:T(8,128)(2,1)S(1)} %copy-done.3, f32[2048]{0:T(1024)S(1)} %fusion.66, f32[2048,1024]{0,1:T(8,128)} %copy-done.2, bf16[2048,2752]{0,1:T(8,128)(2,1)} %get-tuple-element.82, bf16[1024,9280]{1,0:T(8,128)(2,1)} %all-gather.5.cloned.1.call-done), kind=kOutput, calls=%fused_computation.68 | convolution fusion | flops 11553210368 | bytes 42213376 | tf_op jit(solution)/shard_map/dot_general | solution.py:31
  302.8 33.9 %fusion.2 = (bf16[2048,2752]{0,1:T(8,128)(2,1)}, bf16[2048,2752]{0,1:T(8,128)(2,1)}) fusion(f32[2048,2752]{0,1:T(8,128)} %get-tuple-element.83, f32[2048,2752]{0,1:T(8,128)} %fusion.30, bf16[2048,1024]{0,1:T(8,128)(2,1)} %get-tuple-element.84, bf16[1024,9280]{1,0:T(8,128)(2,1)} %all-gather.5.cloned.1.call-done), kind=kOutput, calls=%fused_computation.4 | convolution fusion | flops 11627266048 | bytes 77594624 | tf_op jit(solution)/shard_map/dot_general | solution.py:31
  336.7 18.8 %fusion.24 = f32[2048,1024]{0,1:T(8,128)} fusion(bf16[2048,2752]{0,1:T(8,128)(2,1)} %get-tuple-element.67, bf16[1024,9280]{1,0:T(8,128)(2,1)} %all-gather.5.cloned.1.call-done), kind=kOutput, calls=%fused_computation.44 | convolution fusion | flops 11542724608 | bytes 25427968 | tf_op jit(solution)/shard_map/dot_general | solution.py:31
  355.5 24.0 %multiply_reduce_fusion = (bf16[1024]{0:T(1024)(128)(2,1)S(1)}, f32[2048]{0:T(1024)S(1)}, f32[2048,1024]{0,1:T(8,128)}) fusion(f32[2048,1024]{0,1:T(8,128)} %copy-done.2, f32[2048]{0:T(1024)S(1)} %copy-done.14, f32[1024]{0:T(1024)S(1)} %copy-done.16, f32[2048,1024]{0,1:T(8,128)} %fusion.24, bf16[2048,2752]{0,1:T(8,128)(2,1)} %get-tuple-element.66, ...), kind=kOutput, calls=%fused_computation.32 | convolution fusion | flops 11557401600 | bytes 42227712 | tf_op jit(solution)/shard_map/dot_general | solution.py:31
  379.5 17.0 %multiply_add_fusion = (f32[2048,1024]{0,1:T(8,128)S(1)}, f32[]{:T(128)}, bf16[1,2048,1024]{1,2,0:T(8,128)(2,1)}) fusion(f32[2048,1024]{0,1:T(8,128)} %get-tuple-element.86, f32[2048,1024]{0,1:T(8,128)} %copy-done.2, f32[2048]{0:T(1024)S(1)} %broadcast_multiply_fusion.1, f32[1024]{0:T(1024)S(1)} %copy-done.16, f32[2048]{0:T(1024)S(1)} %copy-done.14, ...), kind=kLoop, calls=%fused_computation.33 | loop fusion | flops 25165824 | bytes 41971716 | tf_op jit(solution)/shard_map/add | solution.py:379
  396.5 9.2 convolution_convert_fusion.5.grad_ref
  405.7 13.2 %query_state.1 = (bf16[16,80,2048]{2,1,0:T(8,128)(2,1)}, f32[16,80,176]{2,1,0:T(8,128)}) custom-call(bf16[1536,2048]{1,0:T(8,128)(2,1)} %convolution_convert_fusion.1.qkv_ref, bf16[1024,2048]{1,0:T(8,128)(2,1)} %convolution_convert_fusion.5.grad_ref, bf16[1024,2048]{1,0:T(8,128)(2,1)} %get-tuple-element.17.mixed_ref, f32[4,4,2048]{2,1,0:T(4,128)} %get-tuple-element.18.den_ref), custom_call_target="tpu_custom_call" | custom-call | tf_op jit(solution)/shard_map/query_state/pallas_call | solution.py:250
  420.2 16.6 %convolution_convert_fusion.2 = bf16[1024,2752]{0,1:T(8,128)(2,1)} fusion(bf16[2048,1024]{0,1:T(8,128)(2,1)S(1)} %copy-done.22, bf16[2048,2752]{0,1:T(8,128)(2,1)} %get-tuple-element.82), kind=kOutput, calls=%fused_computation.41 | convolution fusion | flops 11545542656 | bytes 21102592 | tf_op jit(solution)/shard_map/dot_general | solution.py:31
  436.8 15.1 %collective-permute-done.1.init_ref = f32[16,80,176]{2,1,0:T(8,128)S(1)} collective-permute-done((f32[16,80,176]{2,1,0:T(8,128)}, f32[16,80,176]{2,1,0:T(8,128)S(1)}, u32[]{:S(2)}, u32[]{:S(2)}) %collective-permute-start.1) | collective-permute-done | bytes 901152 | tf_op jit(solution)/shard_map/ppermute | solution.py:296
  453.0 53.2 %attend_back.1 = bf16[1536,2048]{1,0:T(8,128)(2,1)} custom-call(bf16[1536,2048]{1,0:T(8,128)(2,1)} %convolution_convert_fusion.1.qkv_ref, bf16[16,80,2048]{2,1,0:T(8,128)(2,1)} %get-tuple-element.19.nb_ref, bf16[16,8,80,176]{3,2,1,0:T(8,128)(2,1)} %get-tuple-element.20.saved_ref, f32[16,80,176]{2,1,0:T(8,128)} %copy-done.11), custom_call_target="tpu_custom_call" | custom-call | tf_op jit(solution)/shard_map/attend_back/pallas_call | solution.py:272
  506.2 12.4 %fusion.17 = (bf16[1024]{0:T(1024)(128)(2,1)S(1)}, f32[2048]{0:T(1024)S(1)}, f32[2048,1024]{0,1:T(8,128)}) fusion(bf16[1,2048,1024]{1,2,0:T(8,128)(2,1)S(1)} %copy-done, f32[2048]{0:T(1024)S(1)} %copy-done.18, f32[1024]{0:T(1024)S(1)} %copy-done.20, bf16[1536,2048]{1,0:T(8,128)(2,1)} %attend_back.1, bf16[1024,1536]{0,1:T(8,128)(2,1)S(1)} %bitcast.95), kind=kOutput, calls=%fused_computation.25 | convolution fusion | flops 6457127936 | bytes 22042624 | tf_op jit(solution)/shard_map/dot_general | solution.py:31
  518.7 8.3 fusion.49
  527.8 2.3 fusion.52
  530.1 9.8 copy.70
  540.1 17.7 %convolution_convert_fusion.3 = bf16[1024,2752]{0,1:T(8,128)(2,1)} fusion(bf16[2048,1024]{0,1:T(8,128)(2,1)} %copy-done.7, bf16[2048,2752]{0,1:T(8,128)(2,1)} %get-tuple-element.67), kind=kOutput, calls=%fused_computation.42 | convolution fusion | flops 11545542656 | bytes 21102592 | tf_op jit(solution)/shard_map/dot_general | solution.py:31
  557.8 8.4 fusion.57
  566.2 13.5 %convolution_convert_fusion.4 = bf16[1024,2752]{0,1:T(8,128)(2,1)} fusion(bf16[2048,1024]{0,1:T(8,128)(2,1)S(1)} %copy-done.8, bf16[2048,2752]{0,1:T(8,128)(2,1)S(1)} %bitcast.106), kind=kOutput, calls=%fused_computation.43 | convolution fusion | flops 11545542656 | bytes 21102592 | tf_op jit(solution)/shard_map/dot_general | solution.py:31
  579.7 36.2 %pad_maximum_fusion = bf16[1024,9280]{0,1:T(8,128)(2,1)} fusion(bf16[1024,2752]{0,1:T(8,128)(2,1)} %convolution_convert_fusion.2, bf16[1024,2752]{0,1:T(8,128)(2,1)} %convolution_convert_fusion.3, bf16[1024,2752]{0,1:T(8,128)(2,1)} %convolution_convert_fusion.4, bf16[1024,1024]{0,1:T(8,128)(2,1)S(1)} %fusion.57), kind=kLoop, calls=%fused_computation.9 | loop fusion | flops 76021760 | bytes 38010880 | tf_op jit(solution)/shard_map/concatenate | solution.py:384
  615.9 23.4 %copy.72 = bf16[1024,9280]{1,0:T(8,128)(2,1)} copy(bf16[1024,9280]{0,1:T(8,128)(2,1)} %pad_maximum_fusion) | data formatting | bytes 38010880 | tf_op jit(solution)/shard_map/concatenate | solution.py:384
  639.4 54.6 %reduce-scatter.5.cloned.1.call-done = bf16[1,16,32,1664]{2,3,1,0:T(8,128)(2,1)} async-done(((bf16[2,16,32,1664]{2,3,1,0:T(8,128)(2,1)}), bf16[1,16,32,1664]{2,3,1,0:T(8,128)(2,1)}) %reduce-scatter.5.cloned.1.call-update) | async-done | bytes 1703952 | tf_op jit(solution)/shard_map/reduce_scatter | solution.py:424
  694.1 216.6 %reduce-scatter.9.cloned.1.call-done = bf16[1,16,32,9280]{3,2,1,0:T(8,128)(2,1)} async-done(((bf16[2,16,32,9280]{3,2,1,0:T(8,128)(2,1)}), bf16[1,16,32,9280]{3,2,1,0:T(8,128)(2,1)}) %reduce-scatter.9.cloned.1.call-update) | async-done | bytes 9502736 | tf_op jit(solution)/shard_map/reduce_scatter | solution.py:424
  912.0 39.4 %psum.7 = f32[]{:T(128)} all-reduce(f32[]{:T(128)S(6)} %mul_shard_map.6), channel_id=1, replica_groups=mesh['seq'=2,'fsdp'=16] {'seq','fsdp'}, use_global_device_ids=true, to_apply=%region_4.5 | all-reduce | flops 1 | bytes 8 | tf_op jit(solution)/shard_map/psum | solution.py:367
  951.5 6.4 copy.73
  958.6 11.5 %fusion.16 = f32[1,2048,1024]{1,2,0:T(8,128)} fusion(f32[2048,1024]{0,1:T(8,128)} %copy-done.1, bf16[1,2048,1024]{1,2,0:T(8,128)(2,1)} %copy.58, f32[2048,1024]{0,1:T(8,128)} %get-tuple-element.87, f32[2048]{0:T(1024)S(1)} %broadcast_multiply_fusion, f32[1024]{0:T(1024)S(1)} %copy-done.20, f32[2048]{0:T(1024)S(1)} %copy-done.18), kind=kLoop, calls=%fused_computation.24 | loop fusion | flops 14680064 | bytes 29380608 | tf_op jit(solution)/shard_map/broadcast_in_dim | solution.py:407
  970.0 9.2 copy.74
  979.3 24.8 %reduce-scatter.7.cloned.1.call-done = bf16[1,1,32,1664]{2,3,1,0:T(8,128)(2,1)} async-done(((bf16[1,16,32,1664]{2,3,1,0:T(8,128)(2,1)}), bf16[1,1,32,1664]{2,3,1,0:T(8,128)(2,1)}) %reduce-scatter.7.cloned.1.call-update) | async-done | bytes 106512 | tf_op jit(solution)/shard_map/reduce_scatter | solution.py:425
  1008.0 112.0 %reduce-scatter.11.cloned.1.call-done = bf16[1,1,32,9280]{3,2,1,0:T(8,128)(2,1)} async-done(((bf16[1,16,32,9280]{3,2,1,0:T(8,128)(2,1)}), bf16[1,1,32,9280]{3,2,1,0:T(8,128)(2,1)}) %reduce-scatter.11.cloned.1.call-update) | async-done | bytes 593936 | tf_op jit(solution)/shard_map/reduce_scatter | solution.py:425
  (91 shorter events, 16.6 us)
Async XLA Ops:
  7.2 66.8 %all-gather.3.cloned.1.call-start = ((), (), s32[]{:S(2)}) async-start(), calls=%async_computation.4 | async-start | bytes 3514368 | tf_op jit(solution)/shard_map/all_gather | solution.py:329
  9.5 206.5 %all-gather.5.cloned.1.call-start = ((), (), s32[]{:S(2)}) async-start(), calls=%async_computation.5 | async-start | bytes 19734528 | tf_op jit(solution)/shard_map/all_gather | solution.py:332
  11.6 682.4 %reduce-scatter.5.cloned.1.call-start = ((), (), s32[]{:S(2)}) async-start(), calls=%async_computation.6 | async-start | bytes 20447232 | tf_op jit(solution)/shard_map/reduce_scatter | solution.py:424
  21.3 62.1 %copy-start.17 = (f32[2048]{0:T(1024)}, f32[2048]{0:T(1024)S(1)}, u32[]{:S(2)}) copy-start(f32[2048]{0:T(1024)S(1)} %add_rsqrt_fusion.1) | copy-start | bytes 24580
  83.0 0.6 copy-start.19
  83.0 142.7 %copy-start.15 = (f32[1024]{0:T(1024)}, f32[1024]{0:T(1024)S(1)}, u32[]{:S(2)}) copy-start(f32[1024]{0:T(1024)S(1)} %get-tuple-element.62) | copy-start | bytes 12292
  83.3 1.6 copy-start.9
  96.0 21.1 %copy-start.21 = (s32[16]{0:T(128)S(1)}, s32[16]{0:T(128)}, u32[]{:S(2)}) copy-start(s32[16]{0:T(128)} %param.14) | copy-start | bytes 196
  107.0 44.6 %collective-permute-start = (f32[16,80,176]{2,1,0:T(8,128)}, f32[16,80,176]{2,1,0:T(8,128)S(1)}, u32[]{:S(2)}, u32[]{:S(2)}) collective-permute-start(f32[16,80,176]{2,1,0:T(8,128)} %key_state.1), channel_id=1, source_target_pairs={{0,16},{1,17},{2,18},{3,19},{4,20},{5,21},{6,22},{7,23},{8,24},{9,... | collective-permute-start | bytes 2703368 | tf_op jit(solution)/shard_map/ppermute | solution.py:296
  151.6 1.1 copy-start.12
  225.6 3.4 copy-start.2
  225.7 3.4 copy-start.13
  229.8 2.0 copy-start.7
  249.5 32.6 %copy-start.3 = (bf16[1,2048,1024]{1,2,0:T(8,128)(2,1)S(1)}, bf16[1,2048,1024]{1,2,0:T(8,128)(2,1)}, u32[]{:S(2)}) copy-start(bf16[1,2048,1024]{1,2,0:T(8,128)(2,1)} %copy.64) | copy-start | bytes 12582916
  336.7 18.8 %copy-start.14 = (f32[2048]{0:T(1024)S(1)}, f32[2048]{0:T(1024)}, u32[]{:S(2)}) copy-start(f32[2048]{0:T(1024)} %copy-done.13) | copy-start | bytes 24580
  336.7 18.8 %copy-start.16 = (f32[1024]{0:T(1024)S(1)}, f32[1024]{0:T(1024)}, u32[]{:S(2)}) copy-start(f32[1024]{0:T(1024)} %copy-done.15) | copy-start | bytes 12292
  355.5 24.0 %copy-start.4 = (bf16[1,2048,1024]{1,2,0:T(8,128)(2,1)S(1)}, bf16[1,2048,1024]{1,2,0:T(8,128)(2,1)}, u32[]{:S(2)}) copy-start(bf16[1,2048,1024]{1,2,0:T(8,128)(2,1)} %copy.64) | copy-start | bytes 12582916
  396.5 9.2 copy-start.1
  405.7 14.5 %copy-start.22 = (bf16[2048,1024]{0,1:T(8,128)(2,1)S(1)}, bf16[2048,1024]{0,1:T(8,128)(2,1)}, u32[]{:S(2)}) copy-start(bf16[2048,1024]{0,1:T(8,128)(2,1)} %get-tuple-element.84) | copy-start | bytes 12582916
  418.9 33.0 %collective-permute-start.1 = (f32[16,80,176]{2,1,0:T(8,128)}, f32[16,80,176]{2,1,0:T(8,128)S(1)}, u32[]{:S(2)}, u32[]{:S(2)}) collective-permute-start(f32[16,80,176]{2,1,0:T(8,128)} %get-tuple-element.21), channel_id=1, source_target_pairs={{16,0},{17,1},{18,2},{19,3},{20,4},{21,5},{22,6},{23,7},{24,8},{25... | collective-permute-start | bytes 2703368 | tf_op jit(solution)/shard_map/ppermute | solution.py:296
  451.9 1.1 copy-start.11
  453.0 53.2 %copy-start = (bf16[1,2048,1024]{1,2,0:T(8,128)(2,1)S(1)}, bf16[1,2048,1024]{1,2,0:T(8,128)(2,1)}, u32[]{:S(2)}) copy-start(bf16[1,2048,1024]{1,2,0:T(8,128)(2,1)} %copy.58) | copy-start | bytes 12582916
  453.0 53.2 %copy-start.10 = (bf16[1024,16,96]{0,2,1:T(8,128)(2,1)S(1)}, bf16[1024,16,96]{0,2,1:T(8,128)(2,1)}, u32[]{:S(2)}) copy-start(bf16[1024,16,96]{0,2,1:T(8,128)(2,1)} %copy-done.9) | copy-start | bytes 9437188
  453.0 53.2 %copy-start.18 = (f32[2048]{0:T(1024)S(1)}, f32[2048]{0:T(1024)}, u32[]{:S(2)}) copy-start(f32[2048]{0:T(1024)} %copy-done.17) | copy-start | bytes 24580
  453.0 53.2 %copy-start.20 = (f32[1024]{0:T(1024)S(1)}, f32[1024]{0:T(1024)}, u32[]{:S(2)}) copy-start(f32[1024]{0:T(1024)} %copy-done.19) | copy-start | bytes 12292
  506.2 12.4 %copy-start.5 = (bf16[1536,2048]{1,0:T(8,128)(2,1)S(1)}, bf16[1536,2048]{1,0:T(8,128)(2,1)}, u32[]{:S(2)}) copy-start(bf16[1536,2048]{1,0:T(8,128)(2,1)} %attend_back.1) | copy-start | bytes 18874372
  540.0 370.7 %reduce-scatter.9.cloned.1.call-start = ((), (), s32[]{:S(2)}) async-start(), calls=%async_computation.8 | async-start | bytes 28704768 | tf_op jit(solution)/shard_map/reduce_scatter | solution.py:424
  540.0 17.7 %copy-start.6 = (bf16[1024,2048]{1,0:T(8,128)(2,1)S(1)}, bf16[1024,2048]{1,0:T(8,128)(2,1)}, u32[]{:S(2)}) copy-start(bf16[1024,2048]{1,0:T(8,128)(2,1)} %get-tuple-element.17.mixed_ref) | copy-start | bytes 12582916
  540.0 26.1 %slice-start = ((s8[11272192]{0:T(1024)(128)(4,1)}), s8[4194304]{0:T(1024)(128)(4,1)S(1)}, s32[]{:S(2)}) async-start(s8[11272192]{0:T(1024)(128)(4,1)} %bitcast.105), calls=%async_computation.10 | async-start | bytes 8388608
  540.1 26.1 %slice-start.1 = ((s8[11272192]{0:T(1024)(128)(4,1)}), s8[4194304]{0:T(1024)(128)(4,1)S(1)}, s32[]{:S(2)}) async-start(s8[11272192]{0:T(1024)(128)(4,1)} %bitcast.105), calls=%async_computation.11 | async-start | bytes 8388608
  557.8 8.4 copy-start.8
  557.8 8.4 slice-start.2
  639.4 364.8 %reduce-scatter.7.cloned.1.call-start = ((), (), s32[]{:S(2)}) async-start(), calls=%async_computation.7 | async-start | bytes 7241728 | tf_op jit(solution)/shard_map/reduce_scatter | solution.py:425
  694.1 426.0 %reduce-scatter.11.cloned.1.call-start = ((), (), s32[]{:S(2)}) async-start(), calls=%async_computation.9 | async-start | bytes 10166272 | tf_op jit(solution)/shard_map/reduce_scatter | solution.py:425
Sparse Core Ops, SparseCore 0:
  11.5 62.4 all-gather.2
  76.9 139.0 all-gather.4
  540.1 153.8 reduce-scatter.4
  696.2 214.4 reduce-scatter.8
  915.1 89.0 reduce-scatter.6
  1008.1 111.9 reduce-scatter.10

commit v2 on v1

--- a/solution.py
+++ b/solution.py
@@ -17,6 +17,7 @@
 GROUPS = 11
 FROWS = GROUPS * FEAT
 VROWS = HEAD_DIM + 16
+PAIR = 2 * VROWS
 HG = 4
 
 epsilon = 1e-05
@@ -67,6 +68,15 @@
     s = lax.broadcasted_iota(jnp.int32, (CUT, CUT), 0)
     t = lax.broadcasted_iota(jnp.int32, (CUT, CUT), 1)
     return s <= t
+
+
+def split_pair(wide):
+    high = wide.astype(BF16)
+    return jnp.concatenate([high, (wide - high.astype(F32)).astype(BF16)], 0)
+
+
+def twice(rows):
+    return jnp.concatenate([rows, rows], 0)
 
 
 def state_kernel(blocks, qkv_ref, out_ref):
@@ -110,9 +120,10 @@
             q_aug = jnp.concatenate([q * 0.25, one_low], 0)
             u = dot(k_aug, q_aug, TN)
             weight = jnp.where(mask, u * u + 1.0, 0.0).astype(BF16)
-            low = (state[h] * scale).astype(BF16)
+            low = split_pair(state[h] * scale)
             saved_ref[h, b] = low
-            numer = dot(v_aug, weight, NN) + dot(low, phi_rows(q.astype(F32), const), NN)
+            earlier = dot(low, phi_rows(q.astype(F32), const), NN)
+            numer = dot(v_aug, weight, NN) + (earlier[:VROWS] + earlier[VROWS:])
             den = numer[HEAD_DIM : HEAD_DIM + 1]
             mixed_ref[h * HEAD_DIM : (h + 1) * HEAD_DIM, cols] = (
                 numer[:HEAD_DIM] / den
@@ -181,13 +192,14 @@
             weight = jnp.where(mask, u * u + 1.0, 0.0).astype(BF16)
             wb = dot(v_aug, nb, TN)
             sb = jnp.where(mask, wb * u, 0.0).astype(BF16)
-            q_feat_back = dot(saved_ref[h, b], nb, TN)
+            q_feat_back = dot(saved_ref[h, b], twice(nb), TN)
             dq = 0.25 * dot(k, sb, NN) + 0.5 * phi_pull(q_feat_back, qf)
-            low = (state[h] * scale).astype(BF16)
-            k_feat_back = dot(low, v_aug, TN)
+            low = split_pair(state[h] * scale)
+            k_feat_back = dot(low, twice(v_aug), TN)
+            later = dot(low, phi_rows(kf, const), NN)
             dk = dot(q4, sb, NT) + phi_pull(k_feat_back, kf)
-            dv = 0.5 * dot(nb[:HEAD_DIM], weight, NT) + dot(
-                low[:HEAD_DIM], phi_rows(kf, const), NN
+            dv = 0.5 * dot(nb[:HEAD_DIM], weight, NT) + (
+                later[:HEAD_DIM] + later[VROWS : VROWS + HEAD_DIM]
             )
             out_ref[base : base + FEAT, cols] = dq.astype(BF16)
             out_ref[base + FEAT : base + 2 * FEAT, cols] = dk.astype(BF16)
@@ -196,6 +208,10 @@
         return carry
 
     lax.fori_loop(0, blocks, step, 0)
+
+
+def cost(flops):
+    return pl.CostEstimate(flops=int(flops), bytes_accessed=0, transcendentals=0)
 
 
 def head_spec(rows, cols):
@@ -218,6 +234,7 @@
         out_specs=lead_spec(VROWS, FROWS),
         out_shape=jax.ShapeDtypeStruct((HEADS, VROWS, FROWS), F32),
         compiler_params=VMEM_LIMIT,
+        cost_estimate=cost(10e9 * cols / 2048),
         name="key_state",
     )(qkv)
 
@@ -232,15 +249,16 @@
         out_specs=[
             head_spec(HEAD_DIM, cols),
             pl.BlockSpec((1, HG, cols), lambda g: (g, 0, 0)),
-            lead_spec(blocks, VROWS, FROWS),
+            lead_spec(blocks, PAIR, FROWS),
         ],
         out_shape=[
             jax.ShapeDtypeStruct((HEADS * HEAD_DIM, cols), BF16),
             jax.ShapeDtypeStruct((HEADS // HG, HG, cols), F32),
-            jax.ShapeDtypeStruct((HEADS, blocks, VROWS, FROWS), BF16),
+            jax.ShapeDtypeStruct((HEADS, blocks, PAIR, FROWS), BF16),
         ],
         scratch_shapes=[pltpu.VMEM((HG, VROWS, FROWS), F32)],
         compiler_params=VMEM_LIMIT,
+        cost_estimate=cost(36e9 * cols / 2048),
         name="attend",
     )(qkv, init)
 
@@ -262,6 +280,7 @@
             jax.ShapeDtypeStruct((HEADS, VROWS, FROWS), F32),
         ],
         compiler_params=VMEM_LIMIT,
+        cost_estimate=cost(13e9 * cols / 2048),
         name="query_state",
     )(qkv, grad, mixed, den)
 
@@ -275,15 +294,364 @@
         in_specs=[
             head_spec(HROWS, cols),
             lead_spec(VROWS, cols),
-            lead_spec(blocks, VROWS, FROWS),
+            lead_spec(blocks, PAIR, FROWS),
             lead_spec(VROWS, FROWS),
         ],
         out_specs=head_spec(HROWS, cols),
         out_shape=jax.ShapeDtypeStruct((HEADS * HROWS, cols), BF16),
         scratch_shapes=[pltpu.VMEM((HG, VROWS, FROWS), F32)],
         compiler_params=VMEM_LIMIT,
+        cost_estimate=cost(53e9 * cols / 2048),
         name="attend_back",
     )(qkv, nb, saved, init)
+
+
+def project_kernel(tokens_ref, weight_ref, gain_ref, qkv_ref, normed_ref, flipped_ref):
+    width = tokens_ref.shape[2]
+    lead = HEADS * FEAT
+
+    @pl.when(pl.program_id(0) == 0)
+    def _():
+        for c in range(HEADS * HROWS // 128):
+            piece = weight_ref[:, 128 * (c + 1) : 128 * (c + 2)].T
+            start = 128 * c
+            if start < 2 * lead:
+                each, first = FEAT, FEAT * (start // lead)
+                head = (start % lead) // FEAT
+            else:
+                each, first = HEAD_DIM, 2 * FEAT
+                head = (start - 2 * lead) // HEAD_DIM
+            for j in range(128 // each):
+                at = (head + j) * HROWS + first
+                flipped_ref[at : at + each, :] = piece[j * each : (j + 1) * each]
+
+    tokens = tokens_ref[0].astype(F32)
+    scale = lax.rsqrt(jnp.sum(tokens * tokens, -1, keepdims=True) * (1.0 / width) + epsilon)
+    normed = (tokens * scale * gain_ref[...]).astype(BF16)
+    normed_ref[...] = normed
+    qkv_ref[...] = dot(flipped_ref[...], normed, NT).astype(BF16)
+
+
+def project(tokens, early, gain):
+    rows, width = tokens.shape[1:]
+    tile = min(rows, 512)
+    return pl.pallas_call(
+        project_kernel,
+        grid=(rows // tile,),
+        in_specs=[
+            pl.BlockSpec((1, tile, width), lambda i: (0, i, 0)),
+            pl.BlockSpec(early.shape, lambda i: (0, 0), pipeline_mode=pl.Buffered(1)),
+            pl.BlockSpec((1, width), lambda i: (0, 0)),
+        ],
+        out_specs=[
+            pl.BlockSpec((HEADS * HROWS, tile), lambda i: (0, i)),
+            pl.BlockSpec((tile, width), lambda i: (i, 0)),
+            pl.BlockSpec((HEADS * HROWS, width), lambda i: (0, 0)),
+        ],
+        out_shape=[
+            jax.ShapeDtypeStruct((HEADS * HROWS, rows), BF16),
+            jax.ShapeDtypeStruct((rows, width), BF16),
+            jax.ShapeDtypeStruct((HEADS * HROWS, width), BF16),
+        ],
+        compiler_params=VMEM_LIMIT,
+        cost_estimate=cost(2 * HEADS * HROWS * rows * width),
+        name="project",
+    )(tokens, early, gain)
+
+
+def input_kernel(back_ref, flipped_ref, tokens_ref, resid_ref, gain_ref, out_ref, sum_ref):
+    width = tokens_ref.shape[2]
+    tokens = tokens_ref[0].astype(F32)
+    scale = lax.rsqrt(jnp.sum(tokens * tokens, -1, keepdims=True) * (1.0 / width) + epsilon)
+    unit = tokens * scale
+    normed_back = dot(back_ref[...], flipped_ref[...], TN)
+    terms = normed_back * unit
+
+    @pl.when(pl.program_id(0) == 0)
+    def _():
+        sum_ref[...] = jnp.zeros_like(sum_ref)
+
+    sum_ref[...] += jnp.sum(terms, 0, keepdims=True)
+    gain = gain_ref[...]
+    middle = jnp.sum(terms * gain, -1, keepdims=True) * (1.0 / width)
+    out_ref[0] = resid_ref[...] + scale * (normed_back * gain - unit * middle)
+
+
+def input_gradient(back, flipped, tokens, resid_back, gain):
+    rows, width = tokens.shape[1:]
+    tile = min(rows, 512)
+    return pl.pallas_call(
+        input_kernel,
+        grid=(rows // tile,),
+        in_specs=[
+            pl.BlockSpec((HEADS * HROWS, tile), lambda i: (0, i)),
+            pl.BlockSpec(flipped.shape, lambda i: (0, 0), pipeline_mode=pl.Buffered(1)),
+            pl.BlockSpec((1, tile, width), lambda i: (0, i, 0)),
+            pl.BlockSpec((tile, width), lambda i: (i, 0)),
+            pl.BlockSpec((1, width), lambda i: (0, 0)),
+        ],
+        out_specs=[
+            pl.BlockSpec((1, tile, width), lambda i: (0, i, 0)),
+            pl.BlockSpec((1, width), lambda i: (0, 0)),
+        ],
+        out_shape=[
+            jax.ShapeDtypeStruct((1, rows, width), F32),
+            jax.ShapeDtypeStruct((1, width), F32),
+        ],
+        compiler_params=VMEM_LIMIT,
+        cost_estimate=cost(2 * HEADS * HROWS * rows * width),
+        name="input_gradient",
+    )(back, flipped, tokens, resid_back, gain)
+
+
+def ffn_kernel(
+    padded,
+    count_ref,
+    tokens_ref,
+    target_ref,
+    mixed_ref,
+    gain_ref,
+    late_ref,
+    result_ref,
+    normed_ref,
+    hidden_ref,
+    branch_ref,
+    both_ref,
+    attended_ref,
+    resid_back_ref,
+    mixed_back_ref,
+    gain_sum_ref,
+    error_ref,
+    w_out,
+    w_gate,
+    w_up,
+    w_down,
+    slope,
+    active,
+    sems,
+):
+    step = pl.program_id(0)
+    tile, width = tokens_ref.shape[1:]
+    starts = (0, width, width + padded, width + 2 * padded)
+    copies = [
+        pltpu.make_async_copy(
+            late_ref.at[:, pl.ds(start, held.shape[1])], held, sems.at[k]
+        )
+        for k, (start, held) in enumerate(zip(starts, (w_out, w_gate, w_up, w_down)))
+    ]
+
+    @pl.when(step == 0)
+    def _():
+        for copy in copies:
+            copy.start()
+        gain_sum_ref[...] = jnp.zeros_like(gain_sum_ref)
+        error_ref[...] = jnp.zeros_like(error_ref)
+        copies[0].wait()
+
+    gain = gain_ref[...]
+    resid = tokens_ref[0].astype(F32) + dot(mixed_ref[...], w_out[...], TN)
+    scale = lax.rsqrt(jnp.sum(resid * resid, -1, keepdims=True) * (1.0 / width) + epsilon)
+    unit = resid * scale
+    normed = (unit * gain).astype(BF16)
+    normed_ref[...] = normed
+
+    @pl.when(step == 0)
+    def _():
+        copies[1].wait()
+        copies[2].wait()
+
+    for c in range(padded // 256):
+        cols = slice(c * 256, (c + 1) * 256)
+        gate = dot(normed, w_gate[:, cols], NN)
+        up = dot(normed, w_up[:, cols], NN)
+        sigmoid = jax.nn.sigmoid(gate)
+        activated = gate * sigmoid
+        hidden_ref[:, cols] = (activated * up).astype(BF16)
+        active[:, cols] = activated
+        slope[:, cols] = up * sigmoid * (1.0 + gate * (1.0 - sigmoid))
+
+    @pl.when(step == 0)
+    def _():
+        copies[3].wait()
+
+    full = resid + dot(hidden_ref[...], w_down[...], NT)
+    result_ref[0] = full.astype(BF16)
+    position = step * tile + lax.broadcasted_iota(jnp.int32, (tile, 1), 0)
+    difference = jnp.where(
+        position < count_ref[0], full - target_ref[0].astype(F32), 0.0
+    )
+    error_ref[...] += jnp.sum(difference * difference, 0, keepdims=True)
+    branch = difference.astype(BF16)
+    branch_ref[...] = branch
+    for c in range(padded // 256):
+        cols = slice(c * 256, (c + 1) * 256)
+        hidden_back = dot(branch, w_down[:, cols], NN).astype(BF16).astype(F32)
+        both_ref[:, cols] = (hidden_back * slope[:, cols]).astype(BF16)
+        both_ref[:, padded + c * 256 : padded + (c + 1) * 256] = (
+            hidden_back * active[:, cols]
+        ).astype(BF16)
+    ffn_back = dot(both_ref[:, :padded], w_gate[...], NT) + dot(
+        both_ref[:, padded:], w_up[...], NT
+    )
+    terms = ffn_back * unit
+    gain_sum_ref[...] += jnp.sum(terms, 0, keepdims=True)
+    middle = jnp.sum(terms * gain, -1, keepdims=True) * (1.0 / width)
+    resid_back = difference + scale * (ffn_back * gain - unit * middle)
+    resid_back_ref[...] = resid_back
+    attended = resid_back.astype(BF16)
+    attended_ref[...] = attended
+    mixed_back_ref[...] = dot(w_out[...], attended, NT).astype(BF16)
+
+
+def feed_forward(count, tokens, targets, mixed, gain, late, padded):
+    rows, width = tokens.shape[1:]
+    tile = min(rows, 256)
+    token_spec = pl.BlockSpec((1, tile, width), lambda i, c: (0, i, 0))
+
+    def flat(cols):
+        return pl.BlockSpec((tile, cols), lambda i, c: (i, 0))
+
+    tall = pl.BlockSpec((width, tile), lambda i, c: (0, i))
+    line = pl.BlockSpec((1, width), lambda i, c: (0, 0))
+    return pl.pallas_call(
+        functools.partial(ffn_kernel, padded),
+        grid_spec=pltpu.PrefetchScalarGridSpec(
+            num_scalar_prefetch=1,
+            grid=(rows // tile,),
+            in_specs=[
+                token_spec,
+                token_spec,
+                tall,
+                line,
+                pl.BlockSpec(memory_space=pl.ANY),
+            ],
+            out_specs=[
+                token_spec,
+                flat(width),
+                flat(padded),
+                flat(width),
+                flat(2 * padded),
+                flat(width),
+                flat(width),
+                tall,
+                line,
+                line,
+            ],
+            scratch_shapes=[
+                pltpu.VMEM((width, width), BF16),
+                pltpu.VMEM((width, padded), BF16),
+                pltpu.VMEM((width, padded), BF16),
+                pltpu.VMEM((width, padded), BF16),
+                pltpu.VMEM((tile, padded), F32),
+                pltpu.VMEM((tile, padded), F32),
+                pltpu.SemaphoreType.DMA((4,)),
+            ],
+        ),
+        out_shape=[
+            jax.ShapeDtypeStruct((1, rows, width), BF16),
+            jax.ShapeDtypeStruct((rows, width), BF16),
+            jax.ShapeDtypeStruct((rows, padded), BF16),
+            jax.ShapeDtypeStruct((rows, width), BF16),
+            jax.ShapeDtypeStruct((rows, 2 * padded), BF16),
+            jax.ShapeDtypeStruct((rows, width), BF16),
+            jax.ShapeDtypeStruct((rows, width), F32),
+            jax.ShapeDtypeStruct((width, rows), BF16),
+            jax.ShapeDtypeStruct((1, width), F32),
+            jax.ShapeDtypeStruct((1, width), F32),
+        ],
+        compiler_params=pltpu.CompilerParams(vmem_limit_bytes=60 * 1024 * 1024),
+        cost_estimate=cost(4 * rows * width * (width + 3 * padded)),
+        name="feed_forward",
+    )(count, tokens, targets, mixed, gain, late)
+
+
+def weight_grad_kernel(form, pick_ref, left_ref, right_ref, *refs):
+    if form == "flip":
+        total = dot(right_ref[...], left_ref[...], NN).T
+    else:
+        total = dot(left_ref[...], right_ref[...], NN if form == "rows" else TN)
+    if len(refs) > 1:
+        total = total + refs[0][...].astype(F32)
+    refs[-1][...] = total.astype(BF16)
+
+
+def weight_grad(left, right, pick, cols, tile, extra=None, form="plain"):
+    depth = right.shape[1] if form == "flip" else right.shape[0]
+    rows = left.shape[0] if form == "rows" else left.shape[1]
+    step = min(rows, 512)
+    each = cols // tile
+    if form == "rows":
+        left_spec = pl.BlockSpec((step, depth), lambda j, i, p: (i, 0))
+    else:
+        left_spec = pl.BlockSpec((depth, step), lambda j, i, p: (0, i))
+    if form == "flip":
+        right_spec = pl.BlockSpec((tile, depth), lambda j, i, p: (p[0] * each + j, 0))
+    else:
+        right_spec = pl.BlockSpec((depth, tile), lambda j, i, p: (0, p[0] * each + j))
+    out_spec = pl.BlockSpec((step, tile), lambda j, i, p: (i, j))
+    in_specs = [left_spec, right_spec]
+    operands = [left, right]
+    if extra is not None:
+        in_specs.append(out_spec)
+        operands.append(extra)
+    return pl.pallas_call(
+        functools.partial(weight_grad_kernel, form),
+        grid_spec=pltpu.PrefetchScalarGridSpec(
+            num_scalar_prefetch=1,
+            grid=(each, rows // step),
+            in_specs=in_specs,
+            out_specs=out_spec,
+        ),
+        out_shape=jax.ShapeDtypeStruct((rows, cols), BF16),
+        compiler_params=VMEM_LIMIT,
+        cost_estimate=cost(2 * rows * cols * depth),
+        name="weight_grad",
+    )(pick, *operands)
+
+
+def swap_core(array):
+    return lax.ppermute(array, "core", [(i, 1 - i) for i in range(2)])
+
+
+def halves_sum(left, right, core, cols, tile, form="plain"):
+    theirs = weight_grad(left, right, jnp.reshape(1 - core, (1,)), cols, tile, None, form)
+    arrived = swap_core(theirs)
+    return weight_grad(left, right, jnp.reshape(core, (1,)), cols, tile, arrived, form)
+
+
+def sum_over(pieces, axis, dim):
+    parts = lax.axis_size(axis)
+    index = lax.axis_index(axis)
+    total = lax.dynamic_index_in_dim(pieces, index, dim, keepdims=False).astype(F32)
+    for shift in range(1, parts):
+        sent = lax.dynamic_index_in_dim(
+            pieces, lax.rem(index + shift, parts), dim, keepdims=False
+        )
+        pairs = [(i, (i + shift) % parts) for i in range(parts)]
+        total = total + lax.ppermute(sent, axis, pairs).astype(F32)
+    return total.astype(BF16)
+
+
+def rows_sum(block, seq_first):
+    seq_parts, z_parts = lax.axis_size("seq"), lax.axis_size("z")
+    cols = block.shape[1]
+    pieces = block.reshape(seq_parts, z_parts, 2, -1, cols)
+    if seq_first:
+        pieces = sum_over(pieces, "seq", 0)
+        pieces = sum_over(pieces, "y", 1)
+    else:
+        pieces = sum_over(pieces, "y", 2)
+        pieces = sum_over(pieces, "seq", 0)
+    own = sum_over(pieces, "z", 0)
+    return own.reshape(2, -1, cols)
+
+
+def whole_rows(own, core):
+    kept = lax.dynamic_index_in_dim(own, core, 0, keepdims=False)
+    other = swap_core(lax.dynamic_index_in_dim(own, 1 - core, 0, keepdims=False))
+    first = jnp.where(core == 0, kept, other)
+    second = jnp.where(core == 0, other, kept)
+    return first, second
 
 
 def shifted_sum(array, parts, sign):
@@ -311,128 +679,114 @@
     w_up,
     w_down,
 ):
-    both = ("seq", "fsdp")
+    everyone = ("seq", "z", "y", "core")
     seq_parts = lax.axis_size("seq")
+    devices = lax.axis_size(everyone)
     seq_index = lax.axis_index("seq")
-    batch_index = lax.axis_index("fsdp")
+    batch_index = lax.axis_index(("z", "y", "core"))
+    core = lax.axis_index("core")
     rows, width = inputs.shape[1:]
     hidden_units = w_gate.shape[1]
-    tokens = inputs[0].astype(F32)
-    target = targets[0].astype(F32)
+    padded = -(-hidden_units // 256) * 256
     owners = jnp.arange(valid_count.shape[0])
     count = jnp.sum(jnp.where(owners == batch_index, valid_count, 0))
     total_valid = jnp.sum(valid_count).astype(F32)
-    positions = seq_index * rows + jnp.arange(rows)
-    valid = (positions < count).astype(F32)[:, None]
+    valid_here = jnp.reshape(count - seq_index * rows, (1,))
     gains = jnp.pad(jnp.stack([gain_mix, gain_ffn], 1), ((0, 0), (0, 126)))
     early = jnp.concatenate([gains, w_query, w_key, w_value], 1)
-    early = lax.all_gather(early, both, axis=0, tiled=True)
-    gain_one = early[:, 0].astype(F32)
-    gain_two = early[:, 1].astype(F32)
+    early = lax.all_gather(early, everyone, axis=0, tiled=True)
+    gain_one = early[:, 0].astype(F32)[None]
+    gain_two = early[:, 1].astype(F32)[None]
+    fill = ((0, 0), (0, padded - hidden_units))
     late = lax.all_gather(
-        jnp.concatenate([w_out, w_gate, w_up, w_down], 1), both, axis=0, tiled=True
+        jnp.concatenate(
+            [w_out, jnp.pad(w_gate, fill), jnp.pad(w_up, fill), jnp.pad(w_down, fill)], 1
+        ),
+        everyone,
+        axis=0,
+        tiled=True,
     )
-    full_out = late[:, :width]
-    full_gate = late[:, width : width + hidden_units]
-    full_up = late[:, width + hidden_units : width + 2 * hidden_units]
-    full_down = late[:, width + 2 * hidden_units :]
     lead = HEADS * FEAT
-    w_qkv = jnp.concatenate(
-        [
-            early[:, 128 : 128 + lead].reshape(width, HEADS, FEAT),
-            early[:, 128 + lead : 128 + 2 * lead].reshape(width, HEADS, FEAT),
-            early[:, 128 + 2 * lead :].reshape(width, HEADS, HEAD_DIM),
-        ],
-        2,
-    ).reshape(width, HEADS * HROWS)
-    w_qkv_t = w_qkv.T
-    scale_mix = lax.rsqrt(jnp.mean(tokens * tokens, -1, keepdims=True) + epsilon)
-    unit_mix = tokens * scale_mix
-    normed = (unit_mix * gain_one).astype(BF16)
-    qkv = dot(w_qkv_t, normed, NT).astype(BF16)
+    qkv, normed, flipped = project(inputs, early, gain_one)
     state = shifted_sum(local_state(qkv), seq_parts, 1)
     mixed, den, saved = attention_forward(qkv, state)
-    resid = tokens + dot(mixed, full_out, TN)
-    scale_ffn = lax.rsqrt(jnp.mean(resid * resid, -1, keepdims=True) + epsilon)
-    unit_ffn = resid * scale_ffn
-    normed_ffn = (unit_ffn * gain_two).astype(BF16)
-    gate = dot(normed_ffn, full_gate, NN)
-    upward = dot(normed_ffn, full_up, NN)
-    sigmoid = jax.nn.sigmoid(gate)
-    activated = gate * sigmoid
-    hidden = (activated * upward).astype(BF16)
-    full_result = resid + dot(hidden, full_down, NT)
-    difference = valid * (full_result - target)
-    local_error = 0.5 * jnp.sum(difference * difference)
-    error = lax.psum(local_error, both)
-    loss = 2.0 * error / (width * total_valid)
-    branch_back = difference.astype(BF16)
-    grad_down = dot(branch_back, hidden, TN)
-    hidden_back = dot(branch_back, full_down, NN).astype(BF16).astype(F32)
-    gate_back = (hidden_back * upward * sigmoid * (1.0 + gate * (1.0 - sigmoid))).astype(BF16)
-    up_back = (hidden_back * activated).astype(BF16)
-    grad_gate = dot(normed_ffn, gate_back, TN)
-    grad_up = dot(normed_ffn, up_back, TN)
-    ffn_back = dot(gate_back, full_gate, NT) + dot(up_back, full_up, NT)
-    grad_gain_two = jnp.sum(ffn_back * unit_ffn, 0)
-    scaled_back = ffn_back * gain_two
-    resid_back = difference + scale_ffn * (
-        scaled_back - unit_ffn * jnp.mean(scaled_back * unit_ffn, -1, keepdims=True)
+    (
+        result,
+        normed_ffn,
+        hidden,
+        branch_back,
+        both_back,
+        attended_back,
+        resid_back,
+        mixed_back,
+        gain_two_sum,
+        squares,
+    ) = feed_forward(valid_here, inputs, targets, mixed, gain_two, late, padded)
+    local_error = 0.5 * jnp.sum(squares)
+    gate_up_half = halves_sum(normed_ffn, both_back, core, padded, padded // 2)
+    down_half = halves_sum(branch_back, hidden, core, padded // 2, padded // 2)
+    out_half = halves_sum(mixed, attended_back, core, width // 2, width // 2, "rows")
+    mixed_back, gate_up_half, down_half, out_half = lax.optimization_barrier(
+        (mixed_back, gate_up_half, down_half, out_half)
     )
-    attended_back = resid_back.astype(BF16)
-    grad_out = dot(mixed, attended_back, NN)
-    late_grads = jnp.concatenate(
-        [g.astype(BF16) for g in (grad_out, grad_gate, grad_up, grad_down)], 1
-    )
-    late_sums = scatter(late_grads)
-    mixed_back = dot(full_out, attended_back, NT).astype(BF16)
+    gate_up_own = rows_sum(gate_up_half, True)
+    down_out_own = rows_sum(jnp.concatenate([down_half, out_half], 1), False)
     nb, back = local_back_state(qkv, mixed_back, mixed, den)
     later = shifted_sum(back, seq_parts, -1)
     qkv_back = attention_backward(qkv, nb, saved, later)
-    grad_qkv = dot(qkv_back, normed, NN)
-    normed_back = dot(qkv_back, w_qkv_t, TN)
-    grad_gain_one = jnp.sum(normed_back * unit_mix, 0)
-    mix_back = normed_back * gain_one
-    input_back = resid_back + scale_mix * (
-        mix_back - unit_mix * jnp.mean(mix_back * unit_mix, -1, keepdims=True)
+    qkv_cols = HEADS * HROWS // 2
+    qkv_half = halves_sum(normed, qkv_back, core, qkv_cols, qkv_cols, "flip")
+    input_back, gain_one_sum = input_gradient(qkv_back, flipped, inputs, resid_back, gain_one)
+    high = lax.reduce_precision(local_error, 8, 7)
+    middle = lax.reduce_precision(local_error - high, 8, 7)
+    low = lax.reduce_precision(local_error - high - middle, 8, 7)
+    extra = -(-(2 + 3 * devices) // 128) * 128
+    column = lax.broadcasted_iota(jnp.int32, (width, extra), 1)
+    place = 2 + 3 * lax.axis_index(everyone)
+    side = jnp.where(column == 0, gain_one_sum.T, 0.0)
+    side = jnp.where(column == 1, gain_two_sum.T, side)
+    side = jnp.where(column == place, high, side)
+    side = jnp.where(column == place + 1, middle, side)
+    side = jnp.where(column == place + 2, low, side).astype(BF16)
+    side = (side.astype(F32) + swap_core(side).astype(F32)).astype(BF16)
+    qkv_own = rows_sum(jnp.concatenate([qkv_half, side], 1), True)
+    gate_sum, up_sum = whole_rows(gate_up_own, core)
+    pair = jnp.concatenate(whole_rows(down_out_own, core), 0).reshape(2, -1, (padded + width) // 2)
+    down_sum = jnp.concatenate([pair[0, :, : padded // 2], pair[1, :, : padded // 2]], 1)
+    out_sum = jnp.concatenate([pair[0, :, padded // 2 :], pair[1, :, padded // 2 :]], 1)
+    first, second = whole_rows(qkv_own, core)
+    side_sum = first[:, qkv_cols:].astype(F32)
+    loss = 2.0 * jnp.sum(side_sum[0, 2 : 2 + 3 * devices]) / (width * total_valid)
+    qkv_sum = jnp.concatenate([first[:, :qkv_cols], second[:, :qkv_cols]], 1).astype(F32)
+    own = qkv_sum.shape[0]
+    qkv_sum = qkv_sum.reshape(own, HEADS, HROWS)
+    return (
+        result,
+        loss,
+        input_back,
+        side_sum[:, 0],
+        qkv_sum[:, :, :FEAT].reshape(own, lead),
+        qkv_sum[:, :, FEAT : 2 * FEAT].reshape(own, lead),
+        qkv_sum[:, :, 2 * FEAT :].reshape(own, HEADS * HEAD_DIM),
+        out_sum.astype(F32),
+        side_sum[:, 1],
+        gate_sum[:, :hidden_units].astype(F32),
+        up_sum[:, :hidden_units].astype(F32),
+        down_sum[:, :hidden_units].astype(F32),
     )
-    grad_gains = jnp.pad(jnp.stack([grad_gain_one, grad_gain_two], 1), ((0, 0), (0, 126)))
-    early_grads = jnp.concatenate([grad_gains.astype(BF16), grad_qkv.astype(BF16).T], 1)
-    early_sums = scatter(early_grads)
-    qkv_sums = early_sums[:, 128:].reshape(-1, HEADS, HROWS)
-    own = early_sums.shape[0]
-    return (
-        full_result.astype(BF16)[None],
-        loss,
-        input_back[None],
-        early_sums[:, 0],
-        qkv_sums[:, :, :FEAT].reshape(own, lead),
-        qkv_sums[:, :, FEAT : 2 * FEAT].reshape(own, lead),
-        qkv_sums[:, :, 2 * FEAT :].reshape(own, HEADS * HEAD_DIM),
-        late_sums[:, :width],
-        early_sums[:, 1],
-        late_sums[:, width : width + hidden_units],
-        late_sums[:, width + hidden_units : width + 2 * hidden_units],
-        late_sums[:, width + 2 * hidden_units :],
+
+
+def solution(mesh):
+    seq_parts, fsdp_parts = mesh.shape["seq"], mesh.shape["fsdp"]
+    fine = jax.sharding.Mesh(
+        mesh.devices.reshape(seq_parts, fsdp_parts // 4, 2, 2), ("seq", "z", "y", "core")
     )
-
-
-def scatter(grads):
-    seq_parts = lax.axis_size("seq")
-    fsdp_parts = lax.axis_size("fsdp")
-    grouped = grads.reshape((seq_parts, fsdp_parts, -1) + grads.shape[1:])
-    part = lax.psum_scatter(grouped, "seq", scatter_dimension=0, tiled=True)
-    part = lax.psum_scatter(part, "fsdp", scatter_dimension=1, tiled=True)
-    return part.reshape((-1,) + grads.shape[1:]).astype(F32)
-
-
-def solution(mesh):
-    both = P(("seq", "fsdp"))
-    rows = P(("seq", "fsdp"), None)
-    tokens = P("fsdp", "seq", None)
+    both = P(("seq", "z", "y", "core"))
+    rows = P(("seq", "z", "y", "core"), None)
+    tokens = P(("z", "y", "core"), "seq", None)
     return jax.shard_map(
         body,
-        mesh=mesh,
+        mesh=fine,
         in_specs=(tokens, tokens, P(), both, rows, rows, rows, rows, both, rows, rows, rows),
         out_specs=(tokens, P(), tokens, both, rows, rows, rows, rows, both, rows, rows, rows),
         check_vma=False,

time: 1140 us -> 693 us (0.61)
  waiting for transfers between devices: 537 us -> 254 us
  matrix products: 254 us -> 0 us
  Pallas kernels: 113 us -> 330 us
  local copies, waits for them, and re-layouts: 86.4 us -> 15.6 us
  other arithmetic: 78.1 us -> 30.9 us
  blocking collectives: 39.4 us -> 0 us
  starting transfers between devices: 5.1 us -> 32.4 us
    reduce_scatter x4 -> x0, waiting for transfers between devices: 408 us -> none  [the longest x2 271 us: scatter(): part = lax.psum_scatter(grouped, 'seq', scatter_dimension=0, tiled=True)]
    dot_general x15 -> x0, matrix products: 254 us -> none  [dot(): return lax.dot_general(left, right, dims, preferred_element_type=F32)]
    pallas_call x0 -> x11, Pallas kernels: none -> 216 us  [the longest x1 100 us: feed_forward(): pl.pallas_call(functools.partial(ffn_kernel, padded), grid_spec=pltpu.Pre...]
    ppermute x0 -> x23, waiting for transfers between devices: none -> 87.9 us  [the longest x15 86.3 us: sum_over(): total = total + lax.ppermute(sent, axis, pairs).astype(F32)]
    psum x1 -> x0, blocking collectives: 39.4 us -> none  [body(): error = lax.psum(local_error, both)]
    concatenate x3 -> x4, other arithmetic: 38.8 us -> 3.85 us  [the longest x1 1.97 us: body(): jnp.concatenate([w_out, jnp.pad(w_gate, fill), jnp.pad(w_up, fill), jnp.p...]
    unnamed x62 -> x34, local copies, waits for them, and re-layouts: 42.7 us -> 8.02 us
    ppermute x0 -> x23, starting transfers between devices: none -> 27.6 us  [the longest x15 26.1 us: sum_over(): total = total + lax.ppermute(sent, axis, pairs).astype(F32)]
  transfers between devices with their start and end apart: 8 -> 27, of which waited for: 8 -> 14; matrix products, arithmetic and copies ran while one was open for 16% -> 5% of each run, Pallas kernels for 4% -> 26%
where the time goes in v2:
time: 693 us; the launch traced here: 684 us
  Pallas kernels  330 us (48%)
  waiting for transfers between devices  254 us (37%)
  starting transfers between devices  32.4 us (5%)
  other arithmetic  30.9 us (4%)
  between operations  21.5 us (3%)
  local copies, waits for them, and re-layouts  15.6 us (2%)
    pallas_call x1, Pallas kernels, feed_forward(): pl.pallas_call(functools.partial(ffn_kernel, padded), grid_spec=pltpu.Pre...  100 us
    pallas_call x8, Pallas kernels, weight_grad(): pl.pallas_call(functools.partial(weight_grad_kernel, form), grid_spec=plt...  87.6 us
    ppermute x15, waiting for transfers between devices, sum_over(): total = total + lax.ppermute(sent, axis, pairs).astype(F32)  86.3 us
    ppermute x2, waiting for transfers between devices, shifted_sum(): total = total + lax.ppermute(array, 'seq', pairs)  68.9 us
    all_gather x1, waiting for transfers between devices, body(): early = lax.all_gather(early, everyone, axis=0, tiled=True)  62.4 us
    pallas_call x1, Pallas kernels, attention_backward(): pl.pallas_call(functools.partial(backward_kernel, blocks), grid=(HEADS //...  53.3 us
    pallas_call x1, Pallas kernels, attention_forward(): pl.pallas_call(functools.partial(forward_kernel, blocks), grid=(HEADS //...  36.3 us
    all_gather x1, waiting for transfers between devices, body(): lax.all_gather(jnp.concatenate([w_out, jnp.pad(w_gate, fill), jnp.pad(w_u...  34.2 us
  transfers between devices with their start and end apart: 27, of which 14 were waited for; matrix products, arithmetic and copies ran while one was open for 5% of the time, Pallas kernels for 26%

profile of v2, /device:TPU:0, one launch (start us, length us, event | category | flops | bytes accessed | tf_op | source)
XLA Modules:
  0.0 684.0 jit_solution(11610822538848515474)
XLA Ops:
  8.0 1.5 fusion.27
  9.6 2.0 fusion.15
  11.6 62.4 %all-gather.3.cloned.1.call-done.weight_ref = bf16[1024,1664]{1,0:T(8,128)(2,1)} async-done(((bf16[32,1664]{1,0:T(8,128)(2,1)}), bf16[1024,1664]{1,0:T(8,128)(2,1)}) %all-gather.3.cloned.1.call-update) | async-done | bytes 3407888 | tf_op jit(solution)/shard_map/all_gather | solution.py:697
  74.0 1.9 convert_reduce_fusion
  75.9 12.8 %project.1 = (bf16[1536,2048]{1,0:T(8,128)(2,1)}, bf16[2048,1024]{1,0:T(8,128)(2,1)}, bf16[1536,1024]{1,0:T(8,128)(2,1)}) custom-call(bf16[1,2048,1024]{2,1,0:T(8,128)(2,1)} %tokens_ref.5, bf16[1024,1664]{1,0:T(8,128)(2,1)} %all-gather.3.cloned.1.call-done.weight_ref, f32[1,1024]{1,0:T(1,128)} %bitcast.122), custom_call_target="tpu_custom_call" | custom-call | flops 6442450944 | tf_op jit(solution)/shard_map/project/pallas_call | solution.py:338
  88.7 11.0 %key_state.1 = f32[16,80,176]{2,1,0:T(8,128)} custom-call(bf16[1536,2048]{1,0:T(8,128)(2,1)} %get-tuple-element.36.qkv_ref), custom_call_target="tpu_custom_call" | custom-call | flops 10000000000 | tf_op jit(solution)/shard_map/key_state/pallas_call | solution.py:230
  99.7 3.4 collective-permute-start
  104.4 44.5 %collective-permute-done.init_ref = f32[16,80,176]{2,1,0:T(8,128)S(1)} collective-permute-done((f32[16,80,176]{2,1,0:T(8,128)}, f32[16,80,176]{2,1,0:T(8,128)S(1)}, u32[]{:S(2)}, u32[]{:S(2)}) %collective-permute-start) | collective-permute-done | bytes 901152 | tf_op jit(solution)/shard_map/ppermute | solution.py:664
  149.9 36.3 %attend.1 = (bf16[1024,2048]{1,0:T(8,128)(2,1)}, f32[4,4,2048]{2,1,0:T(4,128)}, bf16[16,8,160,176]{3,2,1,0:T(8,128)(2,1)}) custom-call(bf16[1536,2048]{1,0:T(8,128)(2,1)} %get-tuple-element.36.qkv_ref, f32[16,80,176]{2,1,0:T(8,128)} %copy-done.14), custom_call_target="tpu_custom_call" | custom-call | flops 35999997952 | tf_op jit(solution)/shard_map/attend/pallas_call | solution.py:245
  186.2 34.2 %all-gather.5.cloned.1.call-done.late_ref = bf16[1024,9472]{1,0:T(8,128)(2,1)} async-done(((bf16[32,9472]{1,0:T(8,128)(2,1)}), bf16[1024,9472]{1,0:T(8,128)(2,1)}) %all-gather.5.cloned.1.call-update) | async-done | bytes 19398672 | tf_op jit(solution)/shard_map/all_gather | solution.py:701
  220.4 100.1 %feed_forward.1 = (bf16[1,2048,1024]{2,1,0:T(8,128)(2,1)}, bf16[2048,1024]{1,0:T(8,128)(2,1)}, bf16[2048,2816]{1,0:T(8,128)(2,1)}, bf16[2048,1024]{1,0:T(8,128)(...) custom-call(s32[1]{0:T(128)} %bitcast.count_ref, ...), custom_call_target="tpu_custom_call" | custom-call | flops 79456894976 | tf_op jit(solution)/shard_map/feed_forward/pallas_call | solution.py:516
  320.6 18.8 %weight_grad.8 = bf16[1024,2816]{1,0:T(8,128)(2,1)} custom-call(s32[1]{0:T(128)} %bitcast.4.pick_ref, bf16[2048,1024]{1,0:T(8,128)(2,1)} %get-tuple-element.41.left_ref, bf16[2048,5632]{1,0:T(8,128)(2,1)} %get-tuple-element.42.right_ref), custom_call_target="tpu_custom_call" | custom-call | flops 11811160064 | tf_op jit(solution)/shard_map/weight_grad/pallas_call | solution.py:597
  339.6 11.3 %weight_grad.10 = bf16[1024,1408]{1,0:T(8,128)(2,1)} custom-call(s32[1]{0:T(128)} %bitcast.4.pick_ref, bf16[2048,1024]{1,0:T(8,128)(2,1)} %get-tuple-element.43.left_ref, bf16[2048,2816]{1,0:T(8,128)(2,1)} %get-tuple-element.44.right_ref), custom_call_target="tpu_custom_call" | custom-call | flops 5905580032 | tf_op jit(solution)/shard_map/weight_grad/pallas_call | solution.py:597
  351.1 5.6 weight_grad.12
  362.6 5.7 weight_grad.13
  368.3 11.9 %weight_grad.11 = bf16[1024,1408]{1,0:T(8,128)(2,1)} custom-call(s32[1]{0:T(128)} %bitcast.3.pick_ref, bf16[2048,1024]{1,0:T(8,128)(2,1)} %get-tuple-element.43.left_ref, bf16[2048,2816]{1,0:T(8,128)(2,1)} %get-tuple-element.44.right_ref, bf16[1024,1408]{1,0:T(8,128)(2,1)} %collective-permute-done.2.refs_0_), custom_call_target="tpu_custom_call" | custom-call | flops 5905580032 | tf_op jit(solution)/shard_map/weight_grad/pallas_call | solution.py:597
  380.2 19.4 %weight_grad.9 = bf16[1024,2816]{1,0:T(8,128)(2,1)} custom-call(s32[1]{0:T(128)} %bitcast.3.pick_ref, bf16[2048,1024]{1,0:T(8,128)(2,1)} %get-tuple-element.41.left_ref, bf16[2048,5632]{1,0:T(8,128)(2,1)} %get-tuple-element.42.right_ref, bf16[1024,2816]{1,0:T(8,128)(2,1)} %collective-permute-done.1.refs_0_), custom_call_target="tpu_custom_call" | custom-call | flops 11811160064 | tf_op jit(solution)/shard_map/weight_grad/pallas_call | solution.py:597
  399.6 13.2 %query_state.1 = (bf16[16,80,2048]{2,1,0:T(8,128)(2,1)}, f32[16,80,176]{2,1,0:T(8,128)}) custom-call(bf16[1536,2048]{1,0:T(8,128)(2,1)} %get-tuple-element.36.qkv_ref, bf16[1024,2048]{1,0:T(8,128)(2,1)} %get-tuple-element.46.grad_ref, bf16[1024,2048]{1,0:T(8,128)(2,1)} %get-tuple-element.37.mixed_ref.left_ref, f32[4,4,2048]{2,1,0:T(4,128)} %get-tuple-element.47.den_ref), custom_call_target="tpu_custom_call" | custom-call | flops 12999999488 | tf_op jit(solution)/shard_map/query_state/pallas_call | solution.py:268
  414.6 1.5 collective-permute-start.13
  416.7 1.8 dynamic-slice_bitcast_fusion
  418.5 3.7 collective-permute-start.19
  422.2 24.4 %collective-permute-done.4.init_ref = f32[16,80,176]{2,1,0:T(8,128)} collective-permute-done((f32[16,80,176]{2,1,0:T(8,128)}, f32[16,80,176]{2,1,0:T(8,128)}, u32[]{:S(2)}, u32[]{:S(2)}) %collective-permute-start.4) | collective-permute-done | bytes 901152 | tf_op jit(solution)/shard_map/ppermute | solution.py:664
  446.6 53.3 %attend_back.1.right_ref.back_ref = bf16[1536,2048]{1,0:T(8,128)(2,1)} custom-call(bf16[1536,2048]{1,0:T(8,128)(2,1)} %get-tuple-element.36.qkv_ref, bf16[16,80,2048]{2,1,0:T(8,128)(2,1)} %get-tuple-element.48.nb_ref, bf16[16,8,160,176]{3,2,1,0:T(8,128)(2,1)} %get-tuple-element.49.saved_ref, f32[16,80,176]{2,1,0:T(8,128)} %collective-permute-done.4.init_ref), custom_call_target="tpu_custom_call" | custom-call | flops 52999999488 | tf_op jit(solution)/shard_map/attend_back/pallas_call | solution.py:291
  499.9 7.1 %weight_grad.14 = bf16[1024,768]{1,0:T(8,128)(2,1)} custom-call(s32[1]{0:T(128)} %bitcast.4.pick_ref, bf16[2048,1024]{1,0:T(8,128)(2,1)} %get-tuple-element.39.left_ref, bf16[1536,2048]{1,0:T(8,128)(2,1)} %attend_back.1.right_ref.back_ref), custom_call_target="tpu_custom_call" | custom-call | flops 3221225472 | tf_op jit(solution)/shard_map/weight_grad/pallas_call | solution.py:597
  507.1 15.9 %input_gradient.1 = (f32[1,2048,1024]{2,1,0:T(8,128)}, f32[1,1024]{1,0:T(1,128)}) custom-call(bf16[1536,2048]{1,0:T(8,128)(2,1)} %attend_back.1.right_ref.back_ref, bf16[1536,1024]{1,0:T(8,128)(2,1)} %get-tuple-element.53.flipped_ref, bf16[1,2048,1024]{2,1,0:T(8,128)(2,1)} %tokens_ref.5, f32[2048,1024]{1,0:T(8,128)} %get-tuple-element.54.resid_ref, ...), custom_call_target="tpu_custom_call" | custom-call | flops 6442450944 | tf_op jit(solution)/shard_map/input_gradient/pallas_call | solution.py:383
  523.0 3.7 select_convert_fusion
  527.2 2.1 fusion.1
  531.0 3.2 add_convert_fusion
  535.4 7.8 %weight_grad.15 = bf16[1024,768]{1,0:T(8,128)(2,1)} custom-call(s32[1]{0:T(128)} %bitcast.3.pick_ref, bf16[2048,1024]{1,0:T(8,128)(2,1)} %get-tuple-element.39.left_ref, bf16[1536,2048]{1,0:T(8,128)(2,1)} %attend_back.1.right_ref.back_ref, bf16[1024,768]{1,0:T(8,128)(2,1)} %copy-done.4), custom_call_target="tpu_custom_call" | custom-call | flops 3221225472 | tf_op jit(solution)/shard_map/weight_grad/pallas_call | solution.py:597
  543.2 1.6 pad_maximum_fusion.1
  544.9 2.1 collective-permute-start.7
  547.0 8.3 %collective-permute-done.14 = bf16[4,64,1920]{2,1,0:T(8,128)(2,1)} collective-permute-done((bf16[4,64,1920]{2,1,0:T(8,128)(2,1)}, bf16[4,64,1920]{2,1,0:T(8,128)(2,1)}, u32[]{:S(2)}, u32[]{:S(2)}) %collective-permute-start.14) | collective-permute-done | bytes 983072 | tf_op jit(solution)/shard_map/ppermute | solution.py:631
  556.9 1.9 collective-permute-start.16
  558.8 2.4 collective-permute-start.17
  561.2 3.4 fusion
  564.6 3.0 collective-permute-done.15
  567.6 7.9 %collective-permute-done.16 = bf16[64,1920]{1,0:T(8,128)(2,1)S(1)} collective-permute-done((bf16[64,1920]{1,0:T(8,128)(2,1)S(1)}, bf16[64,1920]{1,0:T(8,128)(2,1)S(1)}, u32[]{:S(2)}, u32[]{:S(2)}) %collective-permute-start.16) | collective-permute-done | bytes 245792 | tf_op jit(solution)/shard_map/ppermute | solution.py:631
  577.0 1.5 collective-permute-start.20
  580.2 40.8 %collective-permute-done.8 = bf16[4,64,896]{2,1,0:T(8,128)(2,1)S(1)} collective-permute-done((bf16[4,64,896]{2,1,0:T(8,128)(2,1)S(1)}, bf16[4,64,896]{2,1,0:T(8,128)(2,1)S(1)}, u32[]{:S(2)}, u32[]{:S(2)}) %collective-permute-start.8) | collective-permute-done | bytes 458784 | tf_op jit(solution)/shard_map/ppermute | solution.py:631
  621.2 3.9 collective-permute-start.10
  625.1 3.4 collective-permute-start.11
  628.5 3.3 collective-permute-done.11
  631.7 4.4 collective-permute-done.9
  641.2 1.7 fusion.2
  644.3 2.1 collective-permute-start.22
  646.5 2.7 collective-permute-start.23
  653.2 4.1 collective-permute-done.21
  657.4 14.6 %collective-permute-done.22 = bf16[64,2816]{1,0:T(8,128)(2,1)S(1)} collective-permute-done((bf16[64,2816]{1,0:T(8,128)(2,1)S(1)}, bf16[64,2816]{1,0:T(8,128)(2,1)S(1)}, u32[]{:S(2)}, u32[]{:S(2)}) %collective-permute-start.22) | collective-permute-done | bytes 360480 | tf_op jit(solution)/shard_map/ppermute | solution.py:631
  (114 shorter events, 29.2 us)
Async XLA Ops:
  7.2 66.8 %all-gather.3.cloned.1.call-start = ((), (), s32[]{:S(2)}) async-start(), calls=%async_computation | async-start | bytes 3514368 | tf_op jit(solution)/shard_map/all_gather | solution.py:697
  9.5 210.9 %all-gather.5.cloned.1.call-start = ((), (), s32[]{:S(2)}) async-start(), calls=%async_computation.1 | async-start | bytes 20004864 | tf_op jit(solution)/shard_map/all_gather | solution.py:701
  88.7 14.4 %copy-start.13 = (s32[16]{0:T(128)S(1)}, s32[16]{0:T(128)}, u32[]{:S(2)}) copy-start(s32[16]{0:T(128)} %param.14) | copy-start | bytes 196
  99.7 49.2 %collective-permute-start = (f32[16,80,176]{2,1,0:T(8,128)}, f32[16,80,176]{2,1,0:T(8,128)S(1)}, u32[]{:S(2)}, u32[]{:S(2)}) collective-permute-start(f32[16,80,176]{2,1,0:T(8,128)} %key_state.1), channel_id=1, source_target_pairs={{0,16},{1,17},{2,18},{3,19},{4,20},{5,21},{6,22},{7,23},{8,24},{9,... | collective-permute-start | bytes 2703368 | tf_op jit(solution)/shard_map/ppermute | solution.py:664
  148.9 1.1 copy-start.14
  339.3 40.8 %collective-permute-start.1 = (bf16[1024,2816]{1,0:T(8,128)(2,1)}, bf16[1024,2816]{1,0:T(8,128)(2,1)}, u32[]{:S(2)}, u32[]{:S(2)}) collective-permute-start(bf16[1024,2816]{1,0:T(8,128)(2,1)} %weight_grad.8), channel_id=1, source_target_pairs={{0,1},{1,0},{2,3},{3,2},{4,5},{5,4},{6,7},{7,6},{8,9},{9,8},{10,11... | collective-permute-start | bytes 17301512 | tf_op jit(solution)/shard_map/ppermute | solution.py:613
  350.9 17.4 %collective-permute-start.2 = (bf16[1024,1408]{1,0:T(8,128)(2,1)}, bf16[1024,1408]{1,0:T(8,128)(2,1)}, u32[]{:S(2)}, u32[]{:S(2)}) collective-permute-start(bf16[1024,1408]{1,0:T(8,128)(2,1)} %weight_grad.10), channel_id=1, source_target_pairs={{0,1},{1,0},{2,3},{3,2},{4,5},{5,4},{6,7},{7,6},{8,9},{9,8},{10,11... | collective-permute-start | bytes 8650760 | tf_op jit(solution)/shard_map/ppermute | solution.py:613
  351.1 6.4 copy-start.9
  356.7 4.9 collective-permute-start.3
  357.0 166.0 %copy-start.10 = (pred[128]{0:T(512)(128)(4,1)}, pred[128]{0:T(512)(128)(4,1)S(1)}, u32[]{:S(2)}) copy-start(pred[128]{0:T(512)(128)(4,1)S(1)} %iota_compare_fusion.9) | copy-start | bytes 388
  361.6 1.0 copy-start.5
  399.6 14.5 %copy-start.2 = (bf16[1024,512]{1,0:T(8,128)(2,1)S(1)}, bf16[1024,512]{1,0:T(8,128)(2,1)}, u32[]{:S(2)}) copy-start(bf16[1024,512]{1,0:T(8,128)(2,1)} %weight_grad.13) | copy-start | bytes 3145732
  399.6 14.5 %copy-start.3 = (bf16[1024,1408]{1,0:T(8,128)(2,1)S(1)}, bf16[1024,1408]{1,0:T(8,128)(2,1)}, u32[]{:S(2)}) copy-start(bf16[1024,1408]{1,0:T(8,128)(2,1)} %weight_grad.11) | copy-start | bytes 8650756
  412.8 33.8 %collective-permute-start.4 = (f32[16,80,176]{2,1,0:T(8,128)}, f32[16,80,176]{2,1,0:T(8,128)}, u32[]{:S(2)}, u32[]{:S(2)}) collective-permute-start(f32[16,80,176]{2,1,0:T(8,128)} %get-tuple-element.50), channel_id=1, source_target_pairs={{16,0},{17,1},{18,2},{19,3},{20,4},{21,5},{22,6},{23,7},{24,8},{25... | collective-permute-start | bytes 2703368 | tf_op jit(solution)/shard_map/ppermute | solution.py:664
  414.1 2.6 copy-start
  414.6 112.6 %collective-permute-start.13 = (bf16[2,4,64,1920]{3,2,1,0:T(8,128)(2,1)S(1)}, bf16[2,4,64,1920]{3,2,1,0:T(8,128)(2,1)}, u32[]{:S(2)}, u32[]{:S(2)}) collective-permute-start(bf16[2,4,64,1920]{3,2,1,0:T(8,128)(2,1)S(1)} %dynamic-slice_bitcast_fusion.1), channel_id=1, source_target_pairs={{0,2},{2,0},{1,3},{3,1},{4,6},{6,4},{5,7},{7,5},{8,10},{10,8},{9,1... | collective-permute-start | bytes 5898248 | tf_op jit(solution)/shard_map/ppermute | solution.py:631
  418.5 142.7 %collective-permute-start.19 = (bf16[4,2,64,2816]{3,2,1,0:T(8,128)(2,1)}, bf16[4,2,64,2816]{3,2,1,0:T(8,128)(2,1)}, u32[]{:S(2)}, u32[]{:S(2)}) collective-permute-start(bf16[4,2,64,2816]{3,2,1,0:T(8,128)(2,1)} %dynamic-slice_bitcast_fusion), channel_id=1, source_target_pairs={{0,16},{16,0},{1,17},{17,1},{2,18},{18,2},{3,19},{19,3},{4,20},{20... | collective-permute-start | bytes 8650760 | tf_op jit(solution)/shard_map/ppermute | solution.py:631
  507.1 27.2 %collective-permute-start.5 = (bf16[1024,768]{1,0:T(8,128)(2,1)}, bf16[1024,768]{1,0:T(8,128)(2,1)S(1)}, u32[]{:S(2)}, u32[]{:S(2)}) collective-permute-start(bf16[1024,768]{1,0:T(8,128)(2,1)} %weight_grad.14), channel_id=1, source_target_pairs={{0,1},{1,0},{2,3},{3,2},{4,5},{5,4},{6,7},{7,6},{8,9},{9,8},{10,11... | collective-permute-start | bytes 4718600 | tf_op jit(solution)/shard_map/ppermute | solution.py:613
  507.1 15.9 %copy-start.7 = (f32[1,1024]{1,0:T(1,128)S(1)}, f32[1,1024]{1,0:T(1,128)}, u32[]{:S(2)}) copy-start(f32[1,1024]{1,0:T(1,128)} %get-tuple-element.52) | copy-start | bytes 12292
  507.1 15.9 %copy-start.11 = (pred[128]{0:T(512)(128)(4,1)S(1)}, pred[128]{0:T(512)(128)(4,1)}, u32[]{:S(2)}) copy-start(pred[128]{0:T(512)(128)(4,1)} %get-tuple-element.113) | copy-start | bytes 388
  507.1 15.9 %copy-start.12 = (pred[128]{0:T(512)(128)(4,1)S(1)}, pred[128]{0:T(512)(128)(4,1)}, u32[]{:S(2)}) copy-start(pred[128]{0:T(512)(128)(4,1)} %get-tuple-element.114) | copy-start | bytes 388
  526.7 4.3 copy-start.8
  526.7 4.3 collective-permute-start.6
  530.3 24.9 %collective-permute-start.14 = (bf16[4,64,1920]{2,1,0:T(8,128)(2,1)}, bf16[4,64,1920]{2,1,0:T(8,128)(2,1)}, u32[]{:S(2)}, u32[]{:S(2)}) collective-permute-start(bf16[4,64,1920]{2,1,0:T(8,128)(2,1)} %dynamic-slice_bitcast_fusion.3), channel_id=1, source_target_pairs={{0,16},{16,0},{1,17},{17,1},{2,18},{18,2},{3,19},{19,3},{4,20},{20... | collective-permute-start | bytes 2949128 | tf_op jit(solution)/shard_map/ppermute | solution.py:631
  534.3 1.2 copy-start.4
  544.9 33.6 %collective-permute-start.7 = (bf16[4,2,64,896]{3,2,1,0:T(8,128)(2,1)S(1)}, bf16[4,2,64,896]{3,2,1,0:T(8,128)(2,1)S(1)}, u32[]{:S(2)}, u32[]{:S(2)}) collective-permute-start(bf16[4,2,64,896]{3,2,1,0:T(8,128)(2,1)S(1)} %dynamic-slice_bitcast_fusion.4), channel_id=1, source_target_pairs={{0,16},{16,0},{1,17},{17,1},{2,18},{18,2},{3,19},{19,3},{4,20},{20... | collective-permute-start | bytes 2752520 | tf_op jit(solution)/shard_map/ppermute | solution.py:631
  556.8 10.8 %collective-permute-start.15 = (bf16[64,1920]{1,0:T(8,128)(2,1)S(1)}, bf16[64,1920]{1,0:T(8,128)(2,1)S(1)}, u32[]{:S(2)}, u32[]{:S(2)}) collective-permute-start(bf16[64,1920]{1,0:T(8,128)(2,1)S(1)} %get-tuple-element.91), channel_id=1, source_target_pairs={{0,4},{4,8},{8,12},{12,0},{1,5},{5,9},{9,13},{13,1},{2,6},{6,10},{... | collective-permute-start | bytes 737288 | tf_op jit(solution)/shard_map/ppermute | solution.py:631
  556.9 18.5 %collective-permute-start.16 = (bf16[64,1920]{1,0:T(8,128)(2,1)S(1)}, bf16[64,1920]{1,0:T(8,128)(2,1)S(1)}, u32[]{:S(2)}, u32[]{:S(2)}) collective-permute-start(bf16[64,1920]{1,0:T(8,128)(2,1)S(1)} %get-tuple-element.93), channel_id=1, source_target_pairs={{0,8},{4,12},{8,0},{12,4},{1,9},{5,13},{9,1},{13,5},{2,10},{6,14},... | collective-permute-start | bytes 737288 | tf_op jit(solution)/shard_map/ppermute | solution.py:631
  558.8 16.7 %collective-permute-start.17 = (bf16[64,1920]{1,0:T(8,128)(2,1)S(1)}, bf16[64,1920]{1,0:T(8,128)(2,1)S(1)}, u32[]{:S(2)}, u32[]{:S(2)}) collective-permute-start(bf16[64,1920]{1,0:T(8,128)(2,1)S(1)} %get-tuple-element.92), channel_id=1, source_target_pairs={{0,12},{4,0},{8,4},{12,8},{1,13},{5,1},{9,5},{13,9},{2,14},{6,2},{... | collective-permute-start | bytes 737288 | tf_op jit(solution)/shard_map/ppermute | solution.py:631
  575.6 2.8 collective-permute-start.18
  577.0 64.2 %collective-permute-start.20 = (bf16[4,64,2816]{2,1,0:T(8,128)(2,1)}, bf16[4,64,2816]{2,1,0:T(8,128)(2,1)}, u32[]{:S(2)}, u32[]{:S(2)}) collective-permute-start(bf16[4,64,2816]{2,1,0:T(8,128)(2,1)} %dynamic-slice_bitcast_fusion.2), channel_id=1, source_target_pairs={{0,2},{2,0},{1,3},{3,1},{4,6},{6,4},{5,7},{7,5},{8,10},{10,8},{9,1... | collective-permute-start | bytes 4325384 | tf_op jit(solution)/shard_map/ppermute | solution.py:631
  578.8 42.2 %collective-permute-start.8 = (bf16[4,64,896]{2,1,0:T(8,128)(2,1)S(1)}, bf16[4,64,896]{2,1,0:T(8,128)(2,1)S(1)}, u32[]{:S(2)}, u32[]{:S(2)}) collective-permute-start(bf16[4,64,896]{2,1,0:T(8,128)(2,1)S(1)} %dynamic-slice_bitcast_fusion.5), channel_id=1, source_target_pairs={{0,2},{2,0},{1,3},{3,1},{4,6},{6,4},{5,7},{7,5},{8,10},{10,8},{9,1... | collective-permute-start | bytes 1376264 | tf_op jit(solution)/shard_map/ppermute | solution.py:631
  621.2 7.3 %collective-permute-start.10 = (bf16[64,896]{1,0:T(8,128)(2,1)S(1)}, bf16[64,896]{1,0:T(8,128)(2,1)S(1)}, u32[]{:S(2)}, u32[]{:S(2)}) collective-permute-start(bf16[64,896]{1,0:T(8,128)(2,1)S(1)} %get-tuple-element.96), channel_id=1, source_target_pairs={{0,8},{4,12},{8,0},{12,4},{1,9},{5,13},{9,1},{13,5},{2,10},{6,14},... | collective-permute-start | bytes 344072 | tf_op jit(solution)/shard_map/ppermute | solution.py:631
  625.1 6.7 collective-permute-start.11
  628.4 7.6 %collective-permute-start.9 = (bf16[64,896]{1,0:T(8,128)(2,1)S(1)}, bf16[64,896]{1,0:T(8,128)(2,1)S(1)}, u32[]{:S(2)}, u32[]{:S(2)}) collective-permute-start(bf16[64,896]{1,0:T(8,128)(2,1)S(1)} %get-tuple-element.94), channel_id=1, source_target_pairs={{0,4},{4,8},{8,12},{12,0},{1,5},{5,9},{9,13},{13,1},{2,6},{6,10},{... | collective-permute-start | bytes 344072 | tf_op jit(solution)/shard_map/ppermute | solution.py:631
  637.0 1.7 collective-permute-start.12
  638.7 0.7 copy-start.6
  642.9 1.2 copy-start.1
  644.1 13.2 %collective-permute-start.21 = (bf16[64,2816]{1,0:T(8,128)(2,1)S(1)}, bf16[64,2816]{1,0:T(8,128)(2,1)S(1)}, u32[]{:S(2)}, u32[]{:S(2)}) collective-permute-start(bf16[64,2816]{1,0:T(8,128)(2,1)S(1)} %get-tuple-element.88), channel_id=1, source_target_pairs={{0,4},{4,8},{8,12},{12,0},{1,5},{5,9},{9,13},{13,1},{2,6},{6,10},{... | collective-permute-start | bytes 1081352 | tf_op jit(solution)/shard_map/ppermute | solution.py:631
  644.3 27.6 %collective-permute-start.22 = (bf16[64,2816]{1,0:T(8,128)(2,1)S(1)}, bf16[64,2816]{1,0:T(8,128)(2,1)S(1)}, u32[]{:S(2)}, u32[]{:S(2)}) collective-permute-start(bf16[64,2816]{1,0:T(8,128)(2,1)S(1)} %get-tuple-element.90), channel_id=1, source_target_pairs={{0,8},{4,12},{8,0},{12,4},{1,9},{5,13},{9,1},{13,5},{2,10},{6,14},... | collective-permute-start | bytes 1081352 | tf_op jit(solution)/shard_map/ppermute | solution.py:631
  646.5 25.5 %collective-permute-start.23 = (bf16[64,2816]{1,0:T(8,128)(2,1)S(1)}, bf16[64,2816]{1,0:T(8,128)(2,1)S(1)}, u32[]{:S(2)}, u32[]{:S(2)}) collective-permute-start(bf16[64,2816]{1,0:T(8,128)(2,1)S(1)} %get-tuple-element.89), channel_id=1, source_target_pairs={{0,12},{4,0},{8,4},{12,8},{1,13},{5,1},{9,5},{13,9},{2,14},{6,2},{... | collective-permute-start | bytes 1081352 | tf_op jit(solution)/shard_map/ppermute | solution.py:631
  673.2 1.5 collective-permute-start.24
Sparse Core Ops, SparseCore 0:
  11.5 62.4 all-gather.2
  76.8 143.5 all-gather.4

commit v3 on v2

--- a/solution.py
+++ b/solution.py
@@ -18,6 +18,7 @@
 FROWS = GROUPS * FEAT
 VROWS = HEAD_DIM + 16
 PAIR = 2 * VROWS
+SENT = HEAD_DIM + 8
 HG = 4
 
 epsilon = 1e-05
@@ -77,6 +78,24 @@
 
 def twice(rows):
     return jnp.concatenate([rows, rows], 0)
+
+
+def pack_states(sums, out_ref):
+    fill = jnp.zeros((SENT, 2 * 128 - 2 * (FROWS - 128) - 128), F32)
+    for i in range(len(sums) // 2):
+        a, b = sums[2 * i][:SENT], sums[2 * i + 1][:SENT]
+        out_ref[i, 0] = a[:, :128]
+        out_ref[i, 1] = b[:, :128]
+        out_ref[i, 2] = jnp.concatenate([a[:, 128:], b[:, 128:], fill], 1)
+
+
+def unpack_states(packed_ref, state):
+    side = FROWS - 128
+    state[...] = jnp.zeros_like(state)
+    for i in range(state.shape[0] // 2):
+        for j in range(2):
+            state[2 * i + j, :SENT, :128] = packed_ref[i, j]
+            state[2 * i + j, :SENT, 128:] = packed_ref[i, 2][:, j * side : (j + 1) * side]
 
 
 def state_kernel(blocks, qkv_ref, out_ref):
@@ -96,17 +115,17 @@
 
     zero = jnp.zeros((VROWS, FROWS), F32)
     sums = lax.fori_loop(0, blocks, step, (zero,) * HG)
-    for h in range(HG):
-        out_ref[h] = sums[h]
-
-
-def forward_kernel(blocks, qkv_ref, init_ref, mixed_ref, den_ref, saved_ref, state):
+    pack_states(sums, out_ref)
+
+
+def forward_kernel(blocks, qkv_ref, init_ref, *refs):
     ones2 = first_row(16, CUT, 2).astype(BF16)
     const = first_row(FEAT, CUT)
     one_low = const.astype(BF16)
+    mixed_ref, rest_ref, den_ref, saved_ref, state = refs[-5:]
     scale = 2.0 * lane_scale()
     mask = causal_mask()
-    state[...] = init_ref[...]
+    unpack_states(init_ref, state)
 
     def step(b, carry):
         cols = pl.ds(pl.multiple_of(b * CUT, CUT), CUT)
@@ -125,9 +144,11 @@
             earlier = dot(low, phi_rows(q.astype(F32), const), NN)
             numer = dot(v_aug, weight, NN) + (earlier[:VROWS] + earlier[VROWS:])
             den = numer[HEAD_DIM : HEAD_DIM + 1]
-            mixed_ref[h * HEAD_DIM : (h + 1) * HEAD_DIM, cols] = (
-                numer[:HEAD_DIM] / den
-            ).astype(BF16)
+            wide = numer[:HEAD_DIM] * (1.0 / den)
+            mixed_low = wide.astype(BF16)
+            rows = slice(h * HEAD_DIM, (h + 1) * HEAD_DIM)
+            mixed_ref[rows, cols] = mixed_low
+            rest_ref[rows, cols] = (wide - mixed_low.astype(F32)).astype(BF16)
             den_ref[0, h : h + 1, cols] = 0.5 * den
             state[h] += dot(v_aug, phi_rows(k.astype(F32), const), NT)
         return carry
@@ -135,7 +156,9 @@
     lax.fori_loop(0, blocks, step, 0)
 
 
-def back_state_kernel(blocks, qkv_ref, grad_ref, mixed_ref, den_ref, nb_ref, out_ref):
+def back_state_kernel(
+    blocks, qkv_ref, grad_ref, mixed_ref, rest_ref, den_ref, nb_ref, out_ref
+):
     const = first_row(FEAT, CUT)
     row = lax.broadcasted_iota(jnp.int32, (16, CUT), 0)
 
@@ -149,7 +172,9 @@
             g = grad_ref[rows, cols].astype(F32)
             inverse = 1.0 / den_ref[0, h : h + 1, cols]
             db = -inverse * jnp.sum(
-                g * mixed_ref[rows, cols].astype(F32), axis=0, keepdims=True
+                g * (mixed_ref[rows, cols].astype(F32) + rest_ref[rows, cols].astype(F32)),
+                axis=0,
+                keepdims=True,
             )
             nb = (g * inverse).astype(BF16)
             high = db.astype(BF16).astype(F32)
@@ -161,17 +186,17 @@
 
     zero = jnp.zeros((VROWS, FROWS), F32)
     sums = lax.fori_loop(0, blocks, step, (zero,) * HG)
-    for h in range(HG):
-        out_ref[h] = sums[h]
-
-
-def backward_kernel(blocks, qkv_ref, nb_ref, saved_ref, init_ref, out_ref, state):
+    pack_states(sums, out_ref)
+
+
+def backward_kernel(blocks, qkv_ref, nb_ref, saved_ref, init_ref, *refs):
     ones2 = first_row(16, CUT, 2).astype(BF16)
     const = first_row(FEAT, CUT)
     one_low = const.astype(BF16)
+    out_ref, state = refs[-2:]
     scale = lane_scale()
     mask = causal_mask()
-    state[...] = init_ref[...]
+    unpack_states(init_ref, state)
 
     def step(i, carry):
         b = blocks - 1 - i
@@ -225,45 +250,66 @@
 VMEM_LIMIT = pltpu.CompilerParams(vmem_limit_bytes=56 * 1024 * 1024)
 
 
-def local_state(qkv):
+def packed_shape(heads):
+    return jax.ShapeDtypeStruct((heads // 2, 3, SENT, 128), F32)
+
+
+def packed_spec():
+    return pl.BlockSpec((HG // 2, 3, SENT, 128), lambda g: (g, 0, 0, 0))
+
+
+def local_state(qkv, start, count):
     cols = qkv.shape[1]
+    first = start // HG
     return pl.pallas_call(
         functools.partial(state_kernel, cols // CUT),
-        grid=(HEADS // HG,),
-        in_specs=[head_spec(HROWS, cols)],
-        out_specs=lead_spec(VROWS, FROWS),
-        out_shape=jax.ShapeDtypeStruct((HEADS, VROWS, FROWS), F32),
+        grid=(count // HG,),
+        in_specs=[pl.BlockSpec((HG * HROWS, cols), lambda g: (first + g, 0))],
+        out_specs=packed_spec(),
+        out_shape=packed_shape(count),
         compiler_params=VMEM_LIMIT,
-        cost_estimate=cost(10e9 * cols / 2048),
+        cost_estimate=cost(11e9 * cols / 2048 * count / HEADS),
         name="key_state",
     )(qkv)
 
 
-def attention_forward(qkv, init):
+def attention_forward(qkv, init, start, count, filled=()):
     cols = qkv.shape[1]
     blocks = cols // CUT
+    first = start // HG
+
+    def head_rows(rows):
+        return pl.BlockSpec((HG * rows, cols), lambda g: (first + g, 0))
+
+    def lead(*tail):
+        return pl.BlockSpec((HG,) + tail, lambda g: (first + g,) + (0,) * len(tail))
+
     return pl.pallas_call(
         functools.partial(forward_kernel, blocks),
-        grid=(HEADS // HG,),
-        in_specs=[head_spec(HROWS, cols), lead_spec(VROWS, FROWS)],
+        grid=(count // HG,),
+        in_specs=[head_rows(HROWS), packed_spec()]
+        + [pl.BlockSpec(memory_space=pl.ANY)] * len(filled),
         out_specs=[
-            head_spec(HEAD_DIM, cols),
-            pl.BlockSpec((1, HG, cols), lambda g: (g, 0, 0)),
-            lead_spec(blocks, PAIR, FROWS),
+            head_rows(HEAD_DIM),
+            head_rows(HEAD_DIM),
+            pl.BlockSpec((1, HG, cols), lambda g: (first + g, 0, 0)),
+            lead(blocks, PAIR, FROWS),
         ],
         out_shape=[
+            jax.ShapeDtypeStruct((HEADS * HEAD_DIM, cols), BF16),
             jax.ShapeDtypeStruct((HEADS * HEAD_DIM, cols), BF16),
             jax.ShapeDtypeStruct((HEADS // HG, HG, cols), F32),
             jax.ShapeDtypeStruct((HEADS, blocks, PAIR, FROWS), BF16),
         ],
         scratch_shapes=[pltpu.VMEM((HG, VROWS, FROWS), F32)],
         compiler_params=VMEM_LIMIT,
-        cost_estimate=cost(36e9 * cols / 2048),
+        cost_estimate=cost(36e9 * cols / 2048 * count / HEADS),
+        input_output_aliases={2 + i: i for i in range(len(filled))},
         name="attend",
-    )(qkv, init)
-
-
-def local_back_state(qkv, grad, mixed, den):
+    )(qkv, init, *filled)
+
+
+def local_back_state(qkv, grad, mixed, rest, den):
     cols = qkv.shape[1]
     return pl.pallas_call(
         functools.partial(back_state_kernel, cols // CUT),
@@ -272,38 +318,167 @@
             head_spec(HROWS, cols),
             head_spec(HEAD_DIM, cols),
             head_spec(HEAD_DIM, cols),
+            head_spec(HEAD_DIM, cols),
             pl.BlockSpec((1, HG, cols), lambda g: (g, 0, 0)),
         ],
-        out_specs=[lead_spec(VROWS, cols), lead_spec(VROWS, FROWS)],
+        out_specs=[lead_spec(VROWS, cols), packed_spec()],
         out_shape=[
             jax.ShapeDtypeStruct((HEADS, VROWS, cols), BF16),
-            jax.ShapeDtypeStruct((HEADS, VROWS, FROWS), F32),
+            packed_shape(HEADS),
         ],
         compiler_params=VMEM_LIMIT,
         cost_estimate=cost(13e9 * cols / 2048),
         name="query_state",
-    )(qkv, grad, mixed, den)
-
-
-def attention_backward(qkv, nb, saved, init):
+    )(qkv, grad, mixed, rest, den)
+
+
+def attention_backward(qkv, nb, saved, init, start, count, filled=None):
     cols = qkv.shape[1]
     blocks = cols // CUT
+    first = start // HG
+
+    def head_rows(rows):
+        return pl.BlockSpec((HG * rows, cols), lambda g: (first + g, 0))
+
+    def lead(*tail):
+        return pl.BlockSpec((HG,) + tail, lambda g: (first + g,) + (0,) * len(tail))
+
+    operands = [qkv, nb, saved, init]
+    in_specs = [
+        head_rows(HROWS),
+        lead(VROWS, cols),
+        lead(blocks, PAIR, FROWS),
+        pl.BlockSpec((HG // 2, 3, SENT, 128), lambda g: (first + g, 0, 0, 0)),
+    ]
+    aliases = {}
+    if filled is not None:
+        operands.append(filled)
+        in_specs.append(pl.BlockSpec(memory_space=pl.ANY))
+        aliases = {4: 0}
     return pl.pallas_call(
         functools.partial(backward_kernel, blocks),
-        grid=(HEADS // HG,),
-        in_specs=[
-            head_spec(HROWS, cols),
-            lead_spec(VROWS, cols),
-            lead_spec(blocks, PAIR, FROWS),
-            lead_spec(VROWS, FROWS),
-        ],
-        out_specs=head_spec(HROWS, cols),
+        grid=(count // HG,),
+        in_specs=in_specs,
+        out_specs=head_rows(HROWS),
         out_shape=jax.ShapeDtypeStruct((HEADS * HROWS, cols), BF16),
         scratch_shapes=[pltpu.VMEM((HG, VROWS, FROWS), F32)],
         compiler_params=VMEM_LIMIT,
-        cost_estimate=cost(53e9 * cols / 2048),
+        cost_estimate=cost(53e9 * cols / 2048 * count / HEADS),
+        input_output_aliases=aliases,
         name="attend_back",
-    )(qkv, nb, saved, init)
+    )(*operands)
+
+
+MESH = pl.DeviceIdType.MESH
+
+
+def gather_kernel(shape, split, shard_ref, out_ref, local_sem, *sems):
+    seq_parts, z_parts = shape
+    s, z = lax.axis_index("seq"), lax.axis_index("z")
+    y, c = lax.axis_index("y"), lax.axis_index("core")
+    cols = shard_ref.shape[1]
+    left, right = pl.ds(0, split), pl.ds(split, cols - split)
+    every = slice(None)
+
+    def peer(ds=0, dz=0, dy=0, dc=0):
+        return (
+            lax.rem(s + ds, seq_parts),
+            lax.rem(z + dz, z_parts),
+            lax.rem(y + dy, 2),
+            lax.rem(c + dc, 2),
+        )
+
+    def send(kind, slot, src, dst, device):
+        return pltpu.make_async_remote_copy(
+            src_ref=src,
+            dst_ref=dst,
+            send_sem=sems[2 * kind].at[slot],
+            recv_sem=sems[2 * kind + 1].at[slot],
+            device_id=device,
+            device_id_type=MESH,
+        )
+
+    barrier = pltpu.get_barrier_semaphore()
+    peers = [peer(ds=j) for j in range(1, seq_parts)]
+    peers += [peer(dz=k) for k in range(1, z_parts)]
+    peers += [peer(dy=1), peer(dc=1)]
+    for device in peers:
+        pl.semaphore_signal(barrier, inc=1, device_id=device, device_id_type=MESH)
+    own = pltpu.make_async_copy(shard_ref, out_ref.at[s, z, y, c], local_sem)
+    own.start()
+    pl.semaphore_wait(barrier, len(peers))
+
+    order = [0] + sorted(range(1, z_parts), key=lambda k: min(k, z_parts - k))
+    slab = {k: lax.rem(z + z_parts - k, z_parts) for k in order}
+    along = {
+        k: send(0, k, shard_ref, out_ref.at[s, z, y, c], peer(dz=k)) for k in order[1:]
+    }
+    for k in order[1:]:
+        along[k].start()
+    own.wait()
+    first_y, first_x = {}, {}
+    for k in order:
+        if k:
+            along[k].wait_recv()
+        at = out_ref.at[s, slab[k], y, c, :, left]
+        first_y[k] = send(1, k, at, at, peer(dy=1))
+        first_y[k].start()
+        at = out_ref.at[s, slab[k], y, c, :, right]
+        first_x[k] = [
+            send(2, k * seq_parts + j, at, at, peer(ds=j)) for j in range(1, seq_parts)
+        ]
+        for copy in first_x[k]:
+            copy.start()
+    then_x, then_y, across = {}, {}, {}
+    for k in order:
+        first_y[k].wait_recv()
+        at = out_ref.at[s, slab[k], :, c, :, left]
+        then_x[k] = [
+            send(3, k * seq_parts + j, at, at, peer(ds=j)) for j in range(1, seq_parts)
+        ]
+        for copy in then_x[k]:
+            copy.start()
+        for copy in first_x[k]:
+            copy.wait_recv()
+        at = out_ref.at[:, slab[k], y, c, :, right]
+        then_y[k] = send(4, k, at, at, peer(dy=1))
+        then_y[k].start()
+    for k in order:
+        for copy in then_x[k]:
+            copy.wait_recv()
+        then_y[k].wait_recv()
+        at = out_ref.at[:, slab[k], :, c]
+        across[k] = send(5, k, at, at, peer(dc=1))
+        across[k].start()
+    for k in order:
+        across[k].wait_recv()
+    for k in order:
+        if k:
+            along[k].wait_send()
+        first_y[k].wait_send()
+        then_y[k].wait_send()
+        across[k].wait_send()
+        for copy in first_x[k] + then_x[k]:
+            copy.wait_send()
+
+
+def gather_rows(shard):
+    own, cols = shard.shape
+    seq_parts, z_parts = lax.axis_size("seq"), lax.axis_size("z")
+    split = cols // 256 * 128
+    counts = (z_parts, z_parts, z_parts * seq_parts, z_parts * seq_parts, z_parts, z_parts)
+    out = pl.pallas_call(
+        functools.partial(gather_kernel, (seq_parts, z_parts), split),
+        in_specs=[pl.BlockSpec(memory_space=pl.ANY)],
+        out_specs=pl.BlockSpec(memory_space=pl.ANY),
+        out_shape=jax.ShapeDtypeStruct((seq_parts, z_parts, 2, 2, own, cols), BF16),
+        scratch_shapes=[pltpu.SemaphoreType.DMA]
+        + [pltpu.SemaphoreType.DMA((n,)) for n in counts for _ in range(2)],
+        compiler_params=pltpu.CompilerParams(collective_id=0, has_side_effects=True),
+        cost_estimate=cost(25e9),
+        name="gather_rows",
+    )(shard)
+    return out.reshape(-1, cols)
 
 
 def project_kernel(tokens_ref, weight_ref, gain_ref, qkv_ref, normed_ref, flipped_ref):
@@ -328,7 +503,7 @@
     tokens = tokens_ref[0].astype(F32)
     scale = lax.rsqrt(jnp.sum(tokens * tokens, -1, keepdims=True) * (1.0 / width) + epsilon)
     normed = (tokens * scale * gain_ref[...]).astype(BF16)
-    normed_ref[...] = normed
+    normed_ref[...] = normed.T
     qkv_ref[...] = dot(flipped_ref[...], normed, NT).astype(BF16)
 
 
@@ -340,17 +515,19 @@
         grid=(rows // tile,),
         in_specs=[
             pl.BlockSpec((1, tile, width), lambda i: (0, i, 0)),
-            pl.BlockSpec(early.shape, lambda i: (0, 0), pipeline_mode=pl.Buffered(1)),
+            pl.BlockSpec(
+                (width, 128 + HEADS * HROWS), lambda i: (0, 0), pipeline_mode=pl.Buffered(1)
+            ),
             pl.BlockSpec((1, width), lambda i: (0, 0)),
         ],
         out_specs=[
             pl.BlockSpec((HEADS * HROWS, tile), lambda i: (0, i)),
-            pl.BlockSpec((tile, width), lambda i: (i, 0)),
+            pl.BlockSpec((width, tile), lambda i: (0, i)),
             pl.BlockSpec((HEADS * HROWS, width), lambda i: (0, 0)),
         ],
         out_shape=[
             jax.ShapeDtypeStruct((HEADS * HROWS, rows), BF16),
-            jax.ShapeDtypeStruct((rows, width), BF16),
+            jax.ShapeDtypeStruct((width, rows), BF16),
             jax.ShapeDtypeStruct((HEADS * HROWS, width), BF16),
         ],
         compiler_params=VMEM_LIMIT,
@@ -359,49 +536,46 @@
     )(tokens, early, gain)
 
 
-def input_kernel(back_ref, flipped_ref, tokens_ref, resid_ref, gain_ref, out_ref, sum_ref):
+def input_kernel(back_ref, flipped_ref, tokens_ref, resid_ref, gain_ref, *refs):
+    out_ref = refs[-1]
     width = tokens_ref.shape[2]
     tokens = tokens_ref[0].astype(F32)
     scale = lax.rsqrt(jnp.sum(tokens * tokens, -1, keepdims=True) * (1.0 / width) + epsilon)
     unit = tokens * scale
     normed_back = dot(back_ref[...], flipped_ref[...], TN)
-    terms = normed_back * unit
-
-    @pl.when(pl.program_id(0) == 0)
-    def _():
-        sum_ref[...] = jnp.zeros_like(sum_ref)
-
-    sum_ref[...] += jnp.sum(terms, 0, keepdims=True)
-    gain = gain_ref[...]
-    middle = jnp.sum(terms * gain, -1, keepdims=True) * (1.0 / width)
-    out_ref[0] = resid_ref[...] + scale * (normed_back * gain - unit * middle)
-
-
-def input_gradient(back, flipped, tokens, resid_back, gain):
+    scaled = normed_back * gain_ref[...]
+    middle = jnp.sum(scaled * unit, -1, keepdims=True) * (1.0 / width)
+    out_ref[0] = resid_ref[...] + scale * (scaled - unit * middle)
+
+
+def input_gradient(back, flipped, tokens, resid_back, gain, first, count, filled=None):
     rows, width = tokens.shape[1:]
-    tile = min(rows, 512)
+    tile = min(rows // 2, 512)
+    first, count = first // tile, count // tile
+    operands = [back, flipped, tokens, resid_back, gain]
+    in_specs = [
+        pl.BlockSpec((HEADS * HROWS, tile), lambda i: (0, first + i)),
+        pl.BlockSpec(flipped.shape, lambda i: (0, 0), pipeline_mode=pl.Buffered(1)),
+        pl.BlockSpec((1, tile, width), lambda i: (0, first + i, 0)),
+        pl.BlockSpec((tile, width), lambda i: (first + i, 0)),
+        pl.BlockSpec((1, width), lambda i: (0, 0)),
+    ]
+    aliases = {}
+    if filled is not None:
+        operands.append(filled)
+        in_specs.append(pl.BlockSpec(memory_space=pl.ANY))
+        aliases = {5: 0}
     return pl.pallas_call(
         input_kernel,
-        grid=(rows // tile,),
-        in_specs=[
-            pl.BlockSpec((HEADS * HROWS, tile), lambda i: (0, i)),
-            pl.BlockSpec(flipped.shape, lambda i: (0, 0), pipeline_mode=pl.Buffered(1)),
-            pl.BlockSpec((1, tile, width), lambda i: (0, i, 0)),
-            pl.BlockSpec((tile, width), lambda i: (i, 0)),
-            pl.BlockSpec((1, width), lambda i: (0, 0)),
-        ],
-        out_specs=[
-            pl.BlockSpec((1, tile, width), lambda i: (0, i, 0)),
-            pl.BlockSpec((1, width), lambda i: (0, 0)),
-        ],
-        out_shape=[
-            jax.ShapeDtypeStruct((1, rows, width), F32),
-            jax.ShapeDtypeStruct((1, width), F32),
-        ],
+        grid=(count,),
+        in_specs=in_specs,
+        out_specs=pl.BlockSpec((1, tile, width), lambda i: (0, first + i, 0)),
+        out_shape=jax.ShapeDtypeStruct((1, rows, width), F32),
         compiler_params=VMEM_LIMIT,
-        cost_estimate=cost(2 * HEADS * HROWS * rows * width),
+        cost_estimate=cost(4 * HEADS * HROWS * count * tile * width),
+        input_output_aliases=aliases,
         name="input_gradient",
-    )(back, flipped, tokens, resid_back, gain)
+    )(*operands)
 
 
 def ffn_kernel(
@@ -411,6 +585,7 @@
     target_ref,
     mixed_ref,
     gain_ref,
+    early_ref,
     late_ref,
     result_ref,
     normed_ref,
@@ -420,7 +595,6 @@
     attended_ref,
     resid_back_ref,
     mixed_back_ref,
-    gain_sum_ref,
     error_ref,
     w_out,
     w_gate,
@@ -432,19 +606,19 @@
 ):
     step = pl.program_id(0)
     tile, width = tokens_ref.shape[1:]
-    starts = (0, width, width + padded, width + 2 * padded)
     copies = [
         pltpu.make_async_copy(
-            late_ref.at[:, pl.ds(start, held.shape[1])], held, sems.at[k]
+            early_ref.at[:, pl.ds(128 + HEADS * HROWS, width)], w_out, sems.at[0]
         )
-        for k, (start, held) in enumerate(zip(starts, (w_out, w_gate, w_up, w_down)))
+    ] + [
+        pltpu.make_async_copy(late_ref.at[:, pl.ds(k * padded, padded)], held, sems.at[k + 1])
+        for k, held in enumerate((w_gate, w_up, w_down))
     ]
 
     @pl.when(step == 0)
     def _():
         for copy in copies:
             copy.start()
-        gain_sum_ref[...] = jnp.zeros_like(gain_sum_ref)
         error_ref[...] = jnp.zeros_like(error_ref)
         copies[0].wait()
 
@@ -453,7 +627,7 @@
     scale = lax.rsqrt(jnp.sum(resid * resid, -1, keepdims=True) * (1.0 / width) + epsilon)
     unit = resid * scale
     normed = (unit * gain).astype(BF16)
-    normed_ref[...] = normed
+    normed_ref[...] = normed.T
 
     @pl.when(step == 0)
     def _():
@@ -482,7 +656,7 @@
     )
     error_ref[...] += jnp.sum(difference * difference, 0, keepdims=True)
     branch = difference.astype(BF16)
-    branch_ref[...] = branch
+    branch_ref[...] = branch.T
     for c in range(padded // 256):
         cols = slice(c * 256, (c + 1) * 256)
         hidden_back = dot(branch, w_down[:, cols], NN).astype(BF16).astype(F32)
@@ -493,17 +667,16 @@
     ffn_back = dot(both_ref[:, :padded], w_gate[...], NT) + dot(
         both_ref[:, padded:], w_up[...], NT
     )
-    terms = ffn_back * unit
-    gain_sum_ref[...] += jnp.sum(terms, 0, keepdims=True)
-    middle = jnp.sum(terms * gain, -1, keepdims=True) * (1.0 / width)
-    resid_back = difference + scale * (ffn_back * gain - unit * middle)
+    scaled = ffn_back * gain
+    middle = jnp.sum(scaled * unit, -1, keepdims=True) * (1.0 / width)
+    resid_back = difference + scale * (scaled - unit * middle)
     resid_back_ref[...] = resid_back
     attended = resid_back.astype(BF16)
     attended_ref[...] = attended
     mixed_back_ref[...] = dot(w_out[...], attended, NT).astype(BF16)
 
 
-def feed_forward(count, tokens, targets, mixed, gain, late, padded):
+def feed_forward(count, tokens, targets, mixed, gain, early, late, padded):
     rows, width = tokens.shape[1:]
     tile = min(rows, 256)
     token_spec = pl.BlockSpec((1, tile, width), lambda i, c: (0, i, 0))
@@ -524,17 +697,17 @@
                 tall,
                 line,
                 pl.BlockSpec(memory_space=pl.ANY),
+                pl.BlockSpec(memory_space=pl.ANY),
             ],
             out_specs=[
                 token_spec,
-                flat(width),
+                tall,
                 flat(padded),
-                flat(width),
+                tall,
                 flat(2 * padded),
                 flat(width),
                 flat(width),
                 tall,
-                line,
                 line,
             ],
             scratch_shapes=[
@@ -549,42 +722,34 @@
         ),
         out_shape=[
             jax.ShapeDtypeStruct((1, rows, width), BF16),
-            jax.ShapeDtypeStruct((rows, width), BF16),
+            jax.ShapeDtypeStruct((width, rows), BF16),
             jax.ShapeDtypeStruct((rows, padded), BF16),
-            jax.ShapeDtypeStruct((rows, width), BF16),
+            jax.ShapeDtypeStruct((width, rows), BF16),
             jax.ShapeDtypeStruct((rows, 2 * padded), BF16),
             jax.ShapeDtypeStruct((rows, width), BF16),
             jax.ShapeDtypeStruct((rows, width), F32),
             jax.ShapeDtypeStruct((width, rows), BF16),
             jax.ShapeDtypeStruct((1, width), F32),
-            jax.ShapeDtypeStruct((1, width), F32),
         ],
         compiler_params=pltpu.CompilerParams(vmem_limit_bytes=60 * 1024 * 1024),
         cost_estimate=cost(4 * rows * width * (width + 3 * padded)),
         name="feed_forward",
-    )(count, tokens, targets, mixed, gain, late)
+    )(count, tokens, targets, mixed, gain, early, late)
 
 
 def weight_grad_kernel(form, pick_ref, left_ref, right_ref, *refs):
-    if form == "flip":
-        total = dot(right_ref[...], left_ref[...], NN).T
-    else:
-        total = dot(left_ref[...], right_ref[...], NN if form == "rows" else TN)
+    total = dot(left_ref[...], right_ref[...], form)
     if len(refs) > 1:
         total = total + refs[0][...].astype(F32)
     refs[-1][...] = total.astype(BF16)
 
 
-def weight_grad(left, right, pick, cols, tile, extra=None, form="plain"):
-    depth = right.shape[1] if form == "flip" else right.shape[0]
-    rows = left.shape[0] if form == "rows" else left.shape[1]
+def weight_grad(left, right, pick, cols, tile, extra=None, form=NN):
+    rows, depth = left.shape
     step = min(rows, 512)
     each = cols // tile
-    if form == "rows":
-        left_spec = pl.BlockSpec((step, depth), lambda j, i, p: (i, 0))
-    else:
-        left_spec = pl.BlockSpec((depth, step), lambda j, i, p: (0, i))
-    if form == "flip":
+    left_spec = pl.BlockSpec((step, depth), lambda j, i, p: (i, 0))
+    if form is NT:
         right_spec = pl.BlockSpec((tile, depth), lambda j, i, p: (p[0] * each + j, 0))
     else:
         right_spec = pl.BlockSpec((depth, tile), lambda j, i, p: (0, p[0] * each + j))
@@ -613,12 +778,6 @@
     return lax.ppermute(array, "core", [(i, 1 - i) for i in range(2)])
 
 
-def halves_sum(left, right, core, cols, tile, form="plain"):
-    theirs = weight_grad(left, right, jnp.reshape(1 - core, (1,)), cols, tile, None, form)
-    arrived = swap_core(theirs)
-    return weight_grad(left, right, jnp.reshape(core, (1,)), cols, tile, arrived, form)
-
-
 def sum_over(pieces, axis, dim):
     parts = lax.axis_size(axis)
     index = lax.axis_index(axis)
@@ -632,18 +791,9 @@
     return total.astype(BF16)
 
 
-def rows_sum(block, seq_first):
+def as_pieces(block):
     seq_parts, z_parts = lax.axis_size("seq"), lax.axis_size("z")
-    cols = block.shape[1]
-    pieces = block.reshape(seq_parts, z_parts, 2, -1, cols)
-    if seq_first:
-        pieces = sum_over(pieces, "seq", 0)
-        pieces = sum_over(pieces, "y", 1)
-    else:
-        pieces = sum_over(pieces, "y", 2)
-        pieces = sum_over(pieces, "seq", 0)
-    own = sum_over(pieces, "z", 0)
-    return own.reshape(2, -1, cols)
+    return block.reshape(seq_parts, z_parts, 2, -1, block.shape[1])
 
 
 def whole_rows(own, core):
@@ -693,23 +843,24 @@
     total_valid = jnp.sum(valid_count).astype(F32)
     valid_here = jnp.reshape(count - seq_index * rows, (1,))
     gains = jnp.pad(jnp.stack([gain_mix, gain_ffn], 1), ((0, 0), (0, 126)))
-    early = jnp.concatenate([gains, w_query, w_key, w_value], 1)
-    early = lax.all_gather(early, everyone, axis=0, tiled=True)
+    early = gather_rows(jnp.concatenate([gains, w_query, w_key, w_value, w_out], 1))
+    fill = ((0, 0), (0, padded - hidden_units))
+    late = jnp.concatenate(
+        [jnp.pad(w_gate, fill), jnp.pad(w_up, fill), jnp.pad(w_down, fill)], 1
+    )
+    late = lax.all_gather(late, everyone, axis=0, tiled=True)
     gain_one = early[:, 0].astype(F32)[None]
     gain_two = early[:, 1].astype(F32)[None]
-    fill = ((0, 0), (0, padded - hidden_units))
-    late = lax.all_gather(
-        jnp.concatenate(
-            [w_out, jnp.pad(w_gate, fill), jnp.pad(w_up, fill), jnp.pad(w_down, fill)], 1
-        ),
-        everyone,
-        axis=0,
-        tiled=True,
-    )
     lead = HEADS * FEAT
     qkv, normed, flipped = project(inputs, early, gain_one)
-    state = shifted_sum(local_state(qkv), seq_parts, 1)
-    mixed, den, saved = attention_forward(qkv, state)
+    tie = lax.optimization_barrier
+    upper = HEADS // 2
+    lower_state = local_state(qkv, 0, upper)
+    lower_init = shifted_sum(lower_state, seq_parts, 1)
+    qkv, lower_state = tie((qkv, lower_state))
+    upper_init = shifted_sum(local_state(qkv, upper, upper), seq_parts, 1)
+    filled = attention_forward(qkv, lower_init, 0, upper)
+    mixed, rest, den, saved = attention_forward(qkv, upper_init, upper, upper, filled)
     (
         result,
         normed_ffn,
@@ -719,59 +870,111 @@
         attended_back,
         resid_back,
         mixed_back,
-        gain_two_sum,
         squares,
-    ) = feed_forward(valid_here, inputs, targets, mixed, gain_two, late, padded)
+    ) = feed_forward(valid_here, inputs, targets, mixed, gain_two, early, late, padded)
     local_error = 0.5 * jnp.sum(squares)
-    gate_up_half = halves_sum(normed_ffn, both_back, core, padded, padded // 2)
-    down_half = halves_sum(branch_back, hidden, core, padded // 2, padded // 2)
-    out_half = halves_sum(mixed, attended_back, core, width // 2, width // 2, "rows")
-    mixed_back, gate_up_half, down_half, out_half = lax.optimization_barrier(
-        (mixed_back, gate_up_half, down_half, out_half)
-    )
-    gate_up_own = rows_sum(gate_up_half, True)
-    down_out_own = rows_sum(jnp.concatenate([down_half, out_half], 1), False)
-    nb, back = local_back_state(qkv, mixed_back, mixed, den)
-    later = shifted_sum(back, seq_parts, -1)
-    qkv_back = attention_backward(qkv, nb, saved, later)
-    qkv_cols = HEADS * HROWS // 2
-    qkv_half = halves_sum(normed, qkv_back, core, qkv_cols, qkv_cols, "flip")
-    input_back, gain_one_sum = input_gradient(qkv_back, flipped, inputs, resid_back, gain_one)
+    mine, others = jnp.reshape(core, (1,)), jnp.reshape(1 - core, (1,))
+    half, out_half, qkv_cols = padded // 2, width // 2, HEADS * HROWS // 2
+    part = HEADS // 4
+
     high = lax.reduce_precision(local_error, 8, 7)
     middle = lax.reduce_precision(local_error - high, 8, 7)
     low = lax.reduce_precision(local_error - high - middle, 8, 7)
-    extra = -(-(2 + 3 * devices) // 128) * 128
-    column = lax.broadcasted_iota(jnp.int32, (width, extra), 1)
-    place = 2 + 3 * lax.axis_index(everyone)
-    side = jnp.where(column == 0, gain_one_sum.T, 0.0)
-    side = jnp.where(column == 1, gain_two_sum.T, side)
-    side = jnp.where(column == place, high, side)
+    column = lax.broadcasted_iota(jnp.int32, (width, -(-3 * devices // 128) * 128), 1)
+    place = 3 * lax.axis_index(everyone)
+    side = jnp.where(column == place, high, 0.0)
     side = jnp.where(column == place + 1, middle, side)
     side = jnp.where(column == place + 2, low, side).astype(BF16)
     side = (side.astype(F32) + swap_core(side).astype(F32)).astype(BF16)
-    qkv_own = rows_sum(jnp.concatenate([qkv_half, side], 1), True)
-    gate_sum, up_sum = whole_rows(gate_up_own, core)
-    pair = jnp.concatenate(whole_rows(down_out_own, core), 0).reshape(2, -1, (padded + width) // 2)
-    down_sum = jnp.concatenate([pair[0, :, : padded // 2], pair[1, :, : padded // 2]], 1)
-    out_sum = jnp.concatenate([pair[0, :, padded // 2 :], pair[1, :, padded // 2 :]], 1)
-    first, second = whole_rows(qkv_own, core)
-    side_sum = first[:, qkv_cols:].astype(F32)
-    loss = 2.0 * jnp.sum(side_sum[0, 2 : 2 + 3 * devices]) / (width * total_valid)
-    qkv_sum = jnp.concatenate([first[:, :qkv_cols], second[:, :qkv_cols]], 1).astype(F32)
-    own = qkv_sum.shape[0]
-    qkv_sum = qkv_sum.reshape(own, HEADS, HROWS)
+
+    nb, back = local_back_state(qkv, mixed_back, mixed, rest, den)
+    later = shifted_sum(back, seq_parts, -1)
+    normed_ffn, nb = tie((normed_ffn, nb))
+    gate_up_sent = weight_grad(normed_ffn, both_back, others, padded, half)
+    gate_up_come = swap_core(gate_up_sent)
+    branch_back, gate_up_sent = tie((branch_back, gate_up_sent))
+    down_sent = weight_grad(branch_back, hidden, others, half, half)
+    normed_ffn, down_sent = tie((normed_ffn, down_sent))
+    gate_up = weight_grad(normed_ffn, both_back, mine, padded, half, gate_up_come)
+    down_come = swap_core(down_sent)
+    a_one = sum_over(as_pieces(gate_up[:, :half]), "seq", 0)
+    a_two = sum_over(as_pieces(gate_up[:, half:]), "y", 2)
+    mixed, gate_up = tie((mixed, gate_up))
+    out_sent = weight_grad(mixed, attended_back, others, out_half, out_half)
+    out_come = swap_core(out_sent)
+    branch_back, out_sent = tie((branch_back, out_sent))
+    down = weight_grad(branch_back, hidden, mine, half, half, down_come)
+    mixed, down = tie((mixed, down))
+    outer = weight_grad(mixed, attended_back, mine, out_half, out_half, out_come)
+    cut = 128 * ((half + out_half + side.shape[1]) // 256)
+    b_one = down[:, :cut]
+    b_two = jnp.concatenate([down[:, cut:], outer, side], 1)
+    nb, b_one, b_two = tie((nb, b_one, b_two))
+    qkv_back = attention_backward(qkv, nb, saved, later, 0, part)
+    nb, a_one, a_two, b_one, b_two = tie((nb, a_one, a_two, b_one, b_two))
+    a_one = sum_over(a_one, "y", 1)
+    a_two = sum_over(a_two, "seq", 0)
+    b_one = sum_over(as_pieces(b_one), "seq", 0)
+    b_two = sum_over(as_pieces(b_two), "y", 2)
+    qkv_back = attention_backward(qkv, nb, saved, later, part, part, qkv_back)
+    qkv_back = attention_backward(qkv, nb, saved, later, 2 * part, part, qkv_back)
+    nb, a_one, a_two, b_one, b_two = tie((nb, a_one, a_two, b_one, b_two))
+    a_own = sum_over(jnp.concatenate([a_one, a_two], 2), "z", 0)
+    b_one = sum_over(b_one, "y", 1)
+    b_two = sum_over(b_two, "seq", 0)
+    qkv_back = attention_backward(qkv, nb, saved, later, 3 * part, part, qkv_back)
+    qkv_back, b_one, b_two = tie((qkv_back, b_one, b_two))
+    b_own = sum_over(jnp.concatenate([b_one, b_two], 2), "z", 0)
+    qkv_sent = weight_grad(normed, qkv_back, others, qkv_cols, qkv_cols, None, NT)
+    qkv_come = swap_core(qkv_sent)
+    c_all = weight_grad(normed, qkv_back, mine, qkv_cols, qkv_cols, qkv_come, NT)
+    c_cut = 128 * (qkv_cols // 256)
+    c_one = sum_over(as_pieces(c_all[:, :c_cut]), "seq", 0)
+    c_two = sum_over(as_pieces(c_all[:, c_cut:]), "y", 2)
+    qkv_back, c_all = tie((qkv_back, c_all))
+    split = rows // 2
+    early_part = input_gradient(qkv_back, flipped, inputs, resid_back, gain_one, 0, split)
+    early_part, c_one, c_two = tie((early_part, c_one, c_two))
+    c_one = sum_over(c_one, "y", 1)
+    c_two = sum_over(c_two, "seq", 0)
+    input_back = input_gradient(
+        qkv_back, flipped, inputs, resid_back, gain_one, split, split, early_part
+    )
+    input_back, c_one, c_two = tie((input_back, c_one, c_two))
+    c_own = sum_over(jnp.concatenate([c_one, c_two], 2), "z", 0)
+    own = w_query.shape[0]
+    gate_sum, up_sum = whole_rows(a_own.reshape(2, own, -1), core)
+    pair = whole_rows(b_own.reshape(2, own, -1), core)
+    down_sum = jnp.concatenate([pair[0][:, :half], pair[1][:, :half]], 1)
+    out_sum = jnp.concatenate(
+        [pair[0][:, half : half + out_half], pair[1][:, half : half + out_half]], 1
+    )
+    errors = pair[0][0, half + out_half : half + out_half + 3 * devices].astype(F32)
+    loss = 2.0 * jnp.sum(errors) / (width * total_valid)
+    first, second = whole_rows(c_own.reshape(2, own, -1), core)
+    qkv_sum = jnp.concatenate([first, second], 1).astype(F32).reshape(own, HEADS, HROWS)
+    grad_query = qkv_sum[:, :, :FEAT].reshape(own, lead)
+    grad_key = qkv_sum[:, :, FEAT : 2 * FEAT].reshape(own, lead)
+    grad_value = qkv_sum[:, :, 2 * FEAT :].reshape(own, HEADS * HEAD_DIM)
+    grad_gate = gate_sum[:, :hidden_units].astype(F32)
+    grad_up = up_sum[:, :hidden_units].astype(F32)
+
+    def gain_grad(gain, *pairs):
+        total = sum(jnp.sum(w.astype(F32) * grad, 1) for w, grad in pairs)
+        return total / gain.astype(F32)
+
     return (
         result,
         loss,
         input_back,
-        side_sum[:, 0],
-        qkv_sum[:, :, :FEAT].reshape(own, lead),
-        qkv_sum[:, :, FEAT : 2 * FEAT].reshape(own, lead),
-        qkv_sum[:, :, 2 * FEAT :].reshape(own, HEADS * HEAD_DIM),
+        gain_grad(gain_mix, (w_query, grad_query), (w_key, grad_key), (w_value, grad_value)),
+        grad_query,
+        grad_key,
+        grad_value,
         out_sum.astype(F32),
-        side_sum[:, 1],
-        gate_sum[:, :hidden_units].astype(F32),
-        up_sum[:, :hidden_units].astype(F32),
+        gain_grad(gain_ffn, (w_gate, grad_gate), (w_up, grad_up)),
+        grad_gate,
+        grad_up,
         down_sum[:, :hidden_units].astype(F32),
     )
 

time: 693 us -> 571 us (0.82)
  waiting for transfers between devices: 254 us -> 38 us
  Pallas kernels: 330 us -> 411 us
  starting transfers between devices: 32.4 us -> 49.6 us
  other arithmetic: 30.9 us -> 23.1 us
  local copies, waits for them, and re-layouts: 15.6 us -> 23.2 us
    all_gather x2 -> x1, waiting for transfers between devices: 96.6 us -> 0.01 us  [body(): late = lax.all_gather(late, everyone, axis=0, tiled=True)]
    pallas_call x4 -> x11, Pallas kernels: 116 us -> 195 us  [the longest x4 64.8 us: attention_backward(): pl.pallas_call(functools.partial(backward_kernel, blocks), grid=(count //...]
    ppermute x15 -> x21, waiting for transfers between devices: 86.3 us -> 26.3 us  [sum_over(): total = total + lax.ppermute(sent, axis, pairs).astype(F32)]
    ppermute x2 -> x3, waiting for transfers between devices: 68.9 us -> 10.9 us  [shifted_sum(): total = total + lax.ppermute(array, 'seq', pairs)]
    ppermute x15 -> x21, starting transfers between devices: 26.1 us -> 41 us  [sum_over(): total = total + lax.ppermute(sent, axis, pairs).astype(F32)]
  transfers between devices with their start and end apart: 27 -> 33, of which waited for: 14 -> 10; matrix products, arithmetic and copies ran while one was open for 5% -> 6% of each run, Pallas kernels for 26% -> 47%
where the time goes in v3:
time: 571 us; the launch traced here: 566 us
  Pallas kernels  411 us (72%)
  starting transfers between devices  49.6 us (9%)
  waiting for transfers between devices  38 us (7%)
  local copies, waits for them, and re-layouts  23.2 us (4%)
  other arithmetic  23.1 us (4%)
  between operations  21.6 us (4%)
    pallas_call x1, Pallas kernels, feed_forward(): pl.pallas_call(functools.partial(ffn_kernel, padded), grid_spec=pltpu.Pre...  102 us
    pallas_call x8, Pallas kernels, weight_grad(): pl.pallas_call(functools.partial(weight_grad_kernel, form), grid_spec=plt...  87.2 us
    pallas_call x4, Pallas kernels, attention_backward(): pl.pallas_call(functools.partial(backward_kernel, blocks), grid=(count //...  64.8 us
    pallas_call x1, Pallas kernels, gather_rows(): pl.pallas_call(functools.partial(gather_kernel, (seq_parts, z_parts), spl...  57 us
    ppermute x21, starting transfers between devices, sum_over(): total = total + lax.ppermute(sent, axis, pairs).astype(F32)  41 us
    pallas_call x2, Pallas kernels, attention_forward(): pl.pallas_call(functools.partial(forward_kernel, blocks), grid=(count //...  40.9 us
    ppermute x21, waiting for transfers between devices, sum_over(): total = total + lax.ppermute(sent, axis, pairs).astype(F32)  26.3 us
    pallas_call x2, Pallas kernels, input_gradient(): pl.pallas_call(input_kernel, grid=(count,), in_specs=in_specs, out_specs=...  19 us
  transfers between devices with their start and end apart: 33, of which 10 were waited for; matrix products, arithmetic and copies ran while one was open for 6% of the time, Pallas kernels for 47%

profile of v3, /device:TPU:0, one launch (start us, length us, event | category | flops | bytes accessed | tf_op | source)
XLA Modules:
  0.0 566.3 jit_solution(2064998014007696147)
XLA Ops:
  7.2 1.9 fusion.18
  13.8 57.0 %gather_rows.1 = bf16[2,4,2,2,32,2688]{5,4,3,2,1,0:T(8,128)(2,1)} custom-call(bf16[32,2688]{1,0:T(8,128)(2,1)} %copy-done.14), custom_call_target="tpu_custom_call" | custom-call | flops 24999999488 | tf_op jit(solution)/shard_map/gather_rows/pallas_call | solution.py:470
  70.8 1.9 convert_reduce_fusion
  72.7 12.9 %project.1 = (bf16[1536,2048]{1,0:T(8,128)(2,1)}, bf16[1024,2048]{1,0:T(8,128)(2,1)}, bf16[1536,1024]{1,0:T(8,128)(2,1)}) custom-call(bf16[1,2048,1024]{2,1,0:T(8,128)(2,1)} %tokens_ref.7, bf16[1024,2688]{1,0:T(8,128)(2,1)} %bitcast.149, f32[1,1024]{1,0:T(1,128)} %bitcast.151), custom_call_target="tpu_custom_call" | custom-call | flops 6442450944 | tf_op jit(solution)/shard_map/project/pallas_call | solution.py:513
  85.6 6.6 %key_state.2 = f32[4,3,72,128]{3,2,1,0:T(8,128)} custom-call(bf16[1536,2048]{1,0:T(8,128)(2,1)} %get-tuple-element.68.qkv_ref), custom_call_target="tpu_custom_call" | custom-call | flops 5500000256 | tf_op jit(solution)/shard_map/key_state/pallas_call | solution.py:264
  92.1 4.8 collective-permute-start.1
  96.9 6.6 %key_state.3 = f32[4,3,72,128]{3,2,1,0:T(8,128)} custom-call(bf16[1536,2048]{1,0:T(8,128)(2,1)} %get-tuple-element.68.qkv_ref), custom_call_target="tpu_custom_call" | custom-call | flops 5500000256 | tf_op jit(solution)/shard_map/key_state/pallas_call | solution.py:264
  106.4 10.8 %collective-permute-done.1.init_ref = f32[4,3,72,128]{3,2,1,0:T(8,128)S(1)} collective-permute-done((f32[4,3,72,128]{3,2,1,0:T(8,128)}, f32[4,3,72,128]{3,2,1,0:T(8,128)S(1)}, u32[]{:S(2)}, u32[]{:S(2)}) %collective-permute-start.1) | collective-permute-done | bytes 442400 | tf_op jit(solution)/shard_map/ppermute | solution.py:814
  118.0 20.3 %attend.2 = (bf16[1024,2048]{1,0:T(8,128)(2,1)}, bf16[1024,2048]{1,0:T(8,128)(2,1)}, f32[4,4,2048]{2,1,0:T(4,128)}, bf16[16,8,160,176]{3,2,1,0:T(8,128)(2,1)}) custom-call(bf16[1536,2048]{1,0:T(8,128)(2,1)} %get-tuple-element.68.qkv_ref, f32[4,3,72,128]{3,2,1,0:T(8,128)} %copy-done.16), custom_call_target="tpu_custom_call" | custom-call | flops 17999998976 | tf_op jit(solution)/shard_map/attend/pallas_call | solution.py:287
  139.1 20.6 %attend.3 = (bf16[1024,2048]{1,0:T(8,128)(2,1)}, bf16[1024,2048]{1,0:T(8,128)(2,1)}, f32[4,4,2048]{2,1,0:T(4,128)}, bf16[16,8,160,176]{3,2,1,0:T(8,128)(2,1)}) custom-call(bf16[1536,2048]{1,0:T(8,128)(2,1)} %get-tuple-element.68.qkv_ref, f32[4,3,72,128]{3,2,1,0:T(8,128)} %copy-done.15, ...), custom_call_target="tpu_custom_call", output_to_operand_aliasing={{0}: (2, {}), {1}: (3, {}), {2}: (4, {}), {3}: (5, {})} | custom-call | flops 17999998976 | tf_op jit(solution)/shard_map/attend/pallas_call | solution.py:287
  159.7 101.7 %feed_forward.1 = (bf16[1,2048,1024]{2,1,0:T(8,128)(2,1)}, bf16[1024,2048]{1,0:T(8,128)(2,1)}, bf16[2048,2816]{1,0:T(8,128)(2,1)}, bf16[1024,2048]{1,0:T(8,128)(...) custom-call(s32[1]{0:T(128)} %bitcast.count_ref, ...), custom_call_target="tpu_custom_call" | custom-call | flops 79456894976 | tf_op jit(solution)/shard_map/feed_forward/pallas_call | solution.py:689
  261.3 14.1 %query_state.1 = (bf16[16,80,2048]{2,1,0:T(8,128)(2,1)}, f32[8,3,72,128]{3,2,1,0:T(8,128)}) custom-call(bf16[1536,2048]{1,0:T(8,128)(2,1)} %get-tuple-element.68.qkv_ref, bf16[1024,2048]{1,0:T(8,128)(2,1)} %get-tuple-element.76.grad_ref, bf16[1024,2048]{1,0:T(8,128)(2,1)} %get-tuple-element.92.mixed_ref.left_ref, ...), custom_call_target="tpu_custom_call" | custom-call | flops 12999999488 | tf_op jit(solution)/shard_map/query_state/pallas_call | solution.py:314
  275.5 19.0 %weight_grad.8 = bf16[1024,2816]{1,0:T(8,128)(2,1)} custom-call(s32[1]{0:T(128)} %bitcast.5.pick_ref, bf16[1024,2048]{1,0:T(8,128)(2,1)} %get-tuple-element.86.left_ref, bf16[2048,5632]{1,0:T(8,128)(2,1)} %get-tuple-element.83.right_ref), custom_call_target="tpu_custom_call" | custom-call | flops 11811160064 | tf_op jit(solution)/shard_map/weight_grad/pallas_call | solution.py:762
  294.4 11.2 %weight_grad.9 = bf16[1024,1408]{1,0:T(8,128)(2,1)} custom-call(s32[1]{0:T(128)} %bitcast.5.pick_ref, bf16[1024,2048]{1,0:T(8,128)(2,1)} %get-tuple-element.89.left_ref, bf16[2048,2816]{1,0:T(8,128)(2,1)} %get-tuple-element.85.right_ref), custom_call_target="tpu_custom_call" | custom-call | flops 5905580032 | tf_op jit(solution)/shard_map/weight_grad/pallas_call | solution.py:762
  316.6 19.5 %weight_grad.10 = bf16[1024,2816]{1,0:T(8,128)(2,1)} custom-call(s32[1]{0:T(128)} %bitcast.4.pick_ref, bf16[1024,2048]{1,0:T(8,128)(2,1)} %get-tuple-element.86.left_ref, bf16[2048,5632]{1,0:T(8,128)(2,1)} %get-tuple-element.83.right_ref, bf16[1024,2816]{1,0:T(8,128)(2,1)} %collective-permute-done.2.refs_0_), custom_call_target="tpu_custom_call" | custom-call | flops 11811160064 | tf_op jit(solution)/shard_map/weight_grad/pallas_call | solution.py:762
  336.2 5.6 weight_grad.11
  342.0 11.7 %weight_grad.12 = bf16[1024,1408]{1,0:T(8,128)(2,1)} custom-call(s32[1]{0:T(128)} %bitcast.4.pick_ref, bf16[1024,2048]{1,0:T(8,128)(2,1)} %get-tuple-element.89.left_ref, bf16[2048,2816]{1,0:T(8,128)(2,1)} %get-tuple-element.85.right_ref, bf16[1024,1408]{1,0:T(8,128)(2,1)} %collective-permute-done.3.refs_0_), custom_call_target="tpu_custom_call" | custom-call | flops 5905580032 | tf_op jit(solution)/shard_map/weight_grad/pallas_call | solution.py:762
  353.7 3.1 fusion.31
  359.7 3.4 collective-permute-start.6
  364.1 5.7 %weight_grad.13 = bf16[1024,512]{1,0:T(8,128)(2,1)} custom-call(s32[1]{0:T(128)} %bitcast.4.pick_ref, bf16[1024,2048]{1,0:T(8,128)(2,1)} %get-tuple-element.92.mixed_ref.left_ref, bf16[2048,1024]{1,0:T(8,128)(2,1)} %get-tuple-element.88.right_ref, bf16[1024,512]{1,0:T(8,128)(2,1)} %copy-done.2), custom_call_target="tpu_custom_call" | custom-call | flops 2147483648 | tf_op jit(solution)/shard_map/weight_grad/pallas_call | solution.py:762
  369.8 1.5 pad_maximum_fusion
  371.4 16.1 %attend_back.4.refs_0_ = bf16[1536,2048]{1,0:T(8,128)(2,1)} custom-call(bf16[1536,2048]{1,0:T(8,128)(2,1)} %get-tuple-element.68.qkv_ref, bf16[16,80,2048]{2,1,0:T(8,128)(2,1)} %get-tuple-element.102.nb_ref, bf16[16,8,160,176]{3,2,1,0:T(8,128)(2,1)} %get-tuple-element.103.saved_ref, f32[8,3,72,128]{3,2,1,0:T(8,128)} %collective-permute-done.12.init_ref), custom_call_target="tpu_custom_call" | custom-call | flops 13249999872 | tf_op jit(solution)/shard_map/attend_back/pallas_call | solution.py:358
  387.5 3.3 collective-permute-done.7
  390.8 1.7 fusion
  392.5 3.0 collective-permute-done.6
  395.6 1.7 fusion.1
  398.4 1.7 collective-permute-start.11
  401.3 1.7 collective-permute-start.10
  406.1 16.1 %attend_back.5.refs_0_ = bf16[1536,2048]{1,0:T(8,128)(2,1)} custom-call(bf16[1536,2048]{1,0:T(8,128)(2,1)} %get-tuple-element.68.qkv_ref, bf16[16,80,2048]{2,1,0:T(8,128)(2,1)} %get-tuple-element.102.nb_ref, bf16[16,8,160,176]{3,2,1,0:T(8,128)(2,1)} %get-tuple-element.103.saved_ref, ...), custom_call_target="tpu_custom_call", output_to_operand_aliasing={{}: (4, {})} | custom-call | flops 13249999872 | tf_op jit(solution)/shard_map/attend_back/pallas_call | solution.py:358
  422.2 16.3 %attend_back.6.refs_0_ = bf16[1536,2048]{1,0:T(8,128)(2,1)} custom-call(bf16[1536,2048]{1,0:T(8,128)(2,1)} %get-tuple-element.68.qkv_ref, bf16[16,80,2048]{2,1,0:T(8,128)(2,1)} %get-tuple-element.102.nb_ref, bf16[16,8,160,176]{3,2,1,0:T(8,128)(2,1)} %get-tuple-element.103.saved_ref, ...), custom_call_target="tpu_custom_call", output_to_operand_aliasing={{}: (4, {})} | custom-call | flops 13249999872 | tf_op jit(solution)/shard_map/attend_back/pallas_call | solution.py:358
  438.5 3.0 collective-permute-done.9
  443.0 1.7 fusion.2
  448.2 2.3 collective-permute-start.28
  450.5 1.5 collective-permute-start.29
  452.0 2.8 collective-permute-start.30
  454.9 16.2 %attend_back.7.right_ref.back_ref = bf16[1536,2048]{1,0:T(8,128)(2,1)} custom-call(bf16[1536,2048]{1,0:T(8,128)(2,1)} %get-tuple-element.68.qkv_ref, bf16[16,80,2048]{2,1,0:T(8,128)(2,1)} %get-tuple-element.102.nb_ref, bf16[16,8,160,176]{3,2,1,0:T(8,128)(2,1)} %get-tuple-element.103.saved_ref, ...), custom_call_target="tpu_custom_call", output_to_operand_aliasing={{}: (4, {})} | custom-call | flops 13249999872 | tf_op jit(solution)/shard_map/attend_back/pallas_call | solution.py:358
  471.1 2.7 collective-permute-done.29
  474.7 8.2 %collective-permute-start.15 = (bf16[64,2048]{1,0:T(8,128)(2,1)S(1)}, bf16[64,2048]{1,0:T(8,128)(2,1)S(1)}, u32[]{:S(2)}, u32[]{:S(2)}) collective-permute-start(bf16[64,2048]{1,0:T(8,128)(2,1)S(1)} %get-tuple-element.165), channel_id=1, source_target_pairs={{0,4},{4,8},{8,12},{12,0},{1,5},{5,9},{9,13},{13,1},{2,6},{6,10},{... | collective-permute-start | bytes 786440 | tf_op jit(solution)/shard_map/ppermute | solution.py:790
  483.0 2.5 collective-permute-start.16
  485.4 7.1 %weight_grad.14 = bf16[1024,768]{1,0:T(8,128)(2,1)} custom-call(s32[1]{0:T(128)} %bitcast.5.pick_ref, bf16[1024,2048]{1,0:T(8,128)(2,1)} %get-tuple-element.110.left_ref, bf16[1536,2048]{1,0:T(8,128)(2,1)} %attend_back.7.right_ref.back_ref), custom_call_target="tpu_custom_call" | custom-call | flops 3221225472 | tf_op jit(solution)/shard_map/weight_grad/pallas_call | solution.py:762
  493.7 9.5 %collective-permute-done.16 = bf16[64,2048]{1,0:T(8,128)(2,1)S(1)} collective-permute-done((bf16[64,2048]{1,0:T(8,128)(2,1)S(1)}, bf16[64,2048]{1,0:T(8,128)(2,1)S(1)}, u32[]{:S(2)}, u32[]{:S(2)}) %collective-permute-start.16) | collective-permute-done | bytes 262176 | tf_op jit(solution)/shard_map/ppermute | solution.py:790
  506.8 7.4 %weight_grad.15 = bf16[1024,768]{1,0:T(8,128)(2,1)} custom-call(s32[1]{0:T(128)} %bitcast.4.pick_ref, bf16[1024,2048]{1,0:T(8,128)(2,1)} %get-tuple-element.110.left_ref, bf16[1536,2048]{1,0:T(8,128)(2,1)} %attend_back.7.right_ref.back_ref, bf16[1024,768]{1,0:T(8,128)(2,1)} %copy-done.1), custom_call_target="tpu_custom_call" | custom-call | flops 3221225472 | tf_op jit(solution)/shard_map/weight_grad/pallas_call | solution.py:762
  514.1 1.5 fusion.32
  518.3 9.5 %input_gradient.2.refs_0_ = f32[1,2048,1024]{2,1,0:T(8,128)} custom-call(bf16[1536,2048]{1,0:T(8,128)(2,1)} %attend_back.7.right_ref.back_ref, bf16[1536,1024]{1,0:T(8,128)(2,1)} %get-tuple-element.112.flipped_ref, bf16[1,2048,1024]{2,1,0:T(8,128)(2,1)} %tokens_ref.7, f32[2048,1024]{1,0:T(8,128)} %get-tuple-element.113.resid_ref, f32[1,1024]{1,0:T(1,128)} %bitcast.152), custom_call_target="tpu_custom_call" | custom-call | flops 6442450944 | tf_op jit(solution)/shard_map/input_gradient/pallas_call | solution.py:568
  530.1 9.5 %input_gradient.3 = f32[1,2048,1024]{2,1,0:T(8,128)} custom-call(bf16[1536,2048]{1,0:T(8,128)(2,1)} %attend_back.7.right_ref.back_ref, bf16[1536,1024]{1,0:T(8,128)(2,1)} %get-tuple-element.112.flipped_ref, bf16[1,2048,1024]{2,1,0:T(8,128)(2,1)} %tokens_ref.7, f32[2048,1024]{1,0:T(8,128)} %get-tuple-element.113.resid_ref, ...), custom_call_target="tpu_custom_call", output_to_operand_aliasing={{}: (5, {})} | custom-call | flops 6442450944 | tf_op jit(solution)/shard_map/input_gradient/pallas_call | solution.py:568
  539.9 6.2 %collective-permute-start.24 = (bf16[64,768]{1,0:T(8,128)(2,1)S(1)}, bf16[64,768]{1,0:T(8,128)(2,1)S(1)}, u32[]{:S(2)}, u32[]{:S(2)}) collective-permute-start(bf16[64,768]{1,0:T(8,128)(2,1)S(1)} %get-tuple-element.172), channel_id=1, source_target_pairs={{0,4},{4,8},{8,12},{12,0},{1,5},{5,9},{9,13},{13,1},{2,6},{6,10},{... | collective-permute-start | bytes 294920 | tf_op jit(solution)/shard_map/ppermute | solution.py:790
  546.4 2.0 collective-permute-start.26
  549.3 4.2 collective-permute-done.25
  (166 shorter events, 45.0 us)
Async XLA Ops:
  7.2 152.5 %all-gather.2.cloned.1.call-start = ((), (), s32[]{:S(2)}) async-start(), calls=%async_computation | async-start | bytes 17842176 | tf_op jit(solution)/shard_map/all_gather | solution.py:851
  92.1 12.9 %copy-start.12 = (s32[16]{0:T(128)S(1)}, s32[16]{0:T(128)}, u32[]{:S(2)}) copy-start(s32[16]{0:T(128)} %param.14) | copy-start | bytes 196
  92.1 25.1 %collective-permute-start.1 = (f32[4,3,72,128]{3,2,1,0:T(8,128)}, f32[4,3,72,128]{3,2,1,0:T(8,128)S(1)}, u32[]{:S(2)}, u32[]{:S(2)}) collective-permute-start(f32[4,3,72,128]{3,2,1,0:T(8,128)} %key_state.2), channel_id=1, source_target_pairs={{0,16},{1,17},{2,18},{3,19},{4,20},{5,21},{6,22},{7,23},{8,24},{9,... | collective-permute-start | bytes 1327112 | tf_op jit(solution)/shard_map/ppermute | solution.py:814
  103.6 34.7 %collective-permute-start = (f32[4,3,72,128]{3,2,1,0:T(8,128)}, f32[4,3,72,128]{3,2,1,0:T(8,128)S(1)}, u32[]{:S(2)}, u32[]{:S(2)}) collective-permute-start(f32[4,3,72,128]{3,2,1,0:T(8,128)} %key_state.3), channel_id=1, source_target_pairs={{0,16},{1,17},{2,18},{3,19},{4,20},{5,21},{6,22},{7,23},{8,24},{9,... | collective-permute-start | bytes 1327112 | tf_op jit(solution)/shard_map/ppermute | solution.py:814
  294.4 22.2 %collective-permute-start.2 = (bf16[1024,2816]{1,0:T(8,128)(2,1)}, bf16[1024,2816]{1,0:T(8,128)(2,1)}, u32[]{:S(2)}, u32[]{:S(2)}) collective-permute-start(bf16[1024,2816]{1,0:T(8,128)(2,1)} %weight_grad.8), channel_id=1, source_target_pairs={{0,1},{1,0},{2,3},{3,2},{4,5},{5,4},{6,7},{7,6},{8,9},{9,8},{10,11... | collective-permute-start | bytes 17301512 | tf_op jit(solution)/shard_map/ppermute | solution.py:778
  294.4 11.8 %copy-start.10 = (f32[1,1024]{1,0:T(1,128)S(1)}, f32[1,1024]{1,0:T(1,128)}, u32[]{:S(2)}) copy-start(f32[1,1024]{1,0:T(1,128)} %get-tuple-element.93) | copy-start | bytes 12292
  294.4 18.0 %copy-start.8 = (bf16[32,256]{1,0:T(8,128)(2,1)S(1)}, bf16[32,256]{1,0:T(8,128)(2,1)}, u32[]{:S(2)}) copy-start(bf16[32,256]{1,0:T(8,128)(2,1)} %param.16) | copy-start | bytes 49156
  294.4 18.1 %copy-start.9 = (bf16[32,256]{1,0:T(8,128)(2,1)S(1)}, bf16[32,256]{1,0:T(8,128)(2,1)}, u32[]{:S(2)}) copy-start(bf16[32,256]{1,0:T(8,128)(2,1)} %param.17) | copy-start | bytes 49156
  305.7 36.3 %collective-permute-start.3 = (bf16[1024,1408]{1,0:T(8,128)(2,1)}, bf16[1024,1408]{1,0:T(8,128)(2,1)}, u32[]{:S(2)}, u32[]{:S(2)}) collective-permute-start(bf16[1024,1408]{1,0:T(8,128)(2,1)} %weight_grad.9), channel_id=1, source_target_pairs={{0,1},{1,0},{2,3},{3,2},{4,5},{5,4},{6,7},{7,6},{8,9},{9,8},{10,11... | collective-permute-start | bytes 8650760 | tf_op jit(solution)/shard_map/ppermute | solution.py:778
  312.3 3.0 collective-permute-start.5
  313.9 57.4 %collective-permute-start.12 = (f32[8,3,72,128]{3,2,1,0:T(8,128)}, f32[8,3,72,128]{3,2,1,0:T(8,128)}, u32[]{:S(2)}, u32[]{:S(2)}) collective-permute-start(f32[8,3,72,128]{3,2,1,0:T(8,128)} %get-tuple-element.104), channel_id=1, source_target_pairs={{16,0},{17,1},{18,2},{19,3},{20,4},{21,5},{22,6},{23,7},{24,8},{25... | collective-permute-start | bytes 2654216 | tf_op jit(solution)/shard_map/ppermute | solution.py:814
  341.7 21.4 %collective-permute-start.4 = (bf16[1024,512]{1,0:T(8,128)(2,1)}, bf16[1024,512]{1,0:T(8,128)(2,1)S(1)}, u32[]{:S(2)}, u32[]{:S(2)}) collective-permute-start(bf16[1024,512]{1,0:T(8,128)(2,1)} %weight_grad.11), channel_id=1, source_target_pairs={{0,1},{1,0},{2,3},{3,2},{4,5},{5,4},{6,7},{7,6},{8,9},{9,8},{10,11... | collective-permute-start | bytes 3145736 | tf_op jit(solution)/shard_map/ppermute | solution.py:778
  357.0 33.9 %collective-permute-start.7 = (bf16[2,4,64,1408]{3,2,1,0:T(8,128)(2,1)S(1)}, bf16[2,4,64,1408]{3,2,1,0:T(8,128)(2,1)}, u32[]{:S(2)}, u32[]{:S(2)}) collective-permute-start(bf16[2,4,64,1408]{3,2,1,0:T(8,128)(2,1)S(1)} %dynamic-slice_bitcast_fusion), channel_id=1, source_target_pairs={{0,2},{2,0},{1,3},{3,1},{4,6},{6,4},{5,7},{7,5},{8,10},{10,8},{9,1... | collective-permute-start | bytes 4325384 | tf_op jit(solution)/shard_map/ppermute | solution.py:790
  359.7 10.2 %slice-start = ((bf16[1024,1408]{1,0:T(8,128)(2,1)}), bf16[1024,384]{1,0:T(8,128)(2,1)S(1)}, s32[]{:S(2)}) async-start(bf16[1024,1408]{1,0:T(8,128)(2,1)} %weight_grad.12), calls=%async_computation.1 | async-start | bytes 1572864 | tf_op jit(solution)/shard_map/slice | solution.py:911
  359.7 35.9 %collective-permute-start.6 = (bf16[4,2,64,1408]{3,2,0,1:T(8,128)(2,1)}, bf16[4,2,64,1408]{3,2,0,1:T(8,128)(2,1)}, u32[]{:S(2)}, u32[]{:S(2)}) collective-permute-start(bf16[4,2,64,1408]{3,2,0,1:T(8,128)(2,1)} %bitcast.128), channel_id=1, source_target_pairs={{0,16},{16,0},{1,17},{17,1},{2,18},{18,2},{3,19},{19,3},{4,20},{20... | collective-permute-start | bytes 4325384 | tf_op jit(solution)/shard_map/ppermute | solution.py:790
  387.5 8.1 %copy-start = (bf16[1,4,2,64,1408]{4,3,2,1,0:T(8,128)(2,1)S(1)}, bf16[1,4,2,64,1408]{4,3,2,1,0:T(8,128)(2,1)}, u32[]{:S(2)}) copy-start(bf16[1,4,2,64,1408]{4,3,2,1,0:T(8,128)(2,1)} %get-tuple-element.156) | copy-start | bytes 4325380
  397.3 2.8 slice-start.1
  398.4 44.6 %collective-permute-start.11 = (bf16[2,4,64,1024]{3,2,1,0:T(8,128)(2,1)}, bf16[2,4,64,1024]{3,2,1,0:T(8,128)(2,1)}, u32[]{:S(2)}, u32[]{:S(2)}) collective-permute-start(bf16[2,4,64,1024]{3,2,1,0:T(8,128)(2,1)} %dynamic-slice_bitcast_fusion.1), channel_id=1, source_target_pairs={{0,2},{2,0},{1,3},{3,1},{4,6},{6,4},{5,7},{7,5},{8,10},{10,8},{9,1... | collective-permute-start | bytes 3145736 | tf_op jit(solution)/shard_map/ppermute | solution.py:790
  401.3 43.4 %collective-permute-start.10 = (bf16[4,2,64,1024]{3,2,0,1:T(8,128)(2,1)}, bf16[4,2,64,1024]{3,2,0,1:T(8,128)(2,1)S(1)}, u32[]{:S(2)}, u32[]{:S(2)}) collective-permute-start(bf16[4,2,64,1024]{3,2,0,1:T(8,128)(2,1)} %bitcast.129), channel_id=1, source_target_pairs={{0,16},{16,0},{1,17},{17,1},{2,18},{18,2},{3,19},{19,3},{4,20},{20... | collective-permute-start | bytes 3145736 | tf_op jit(solution)/shard_map/ppermute | solution.py:790
  404.0 37.5 %collective-permute-start.9 = (bf16[4,64,1408]{2,1,0:T(8,128)(2,1)}, bf16[4,64,1408]{2,1,0:T(8,128)(2,1)}, u32[]{:S(2)}, u32[]{:S(2)}) collective-permute-start(bf16[4,64,1408]{2,1,0:T(8,128)(2,1)} %dynamic-slice_bitcast_fusion.2), channel_id=1, source_target_pairs={{0,16},{16,0},{1,17},{17,1},{2,18},{18,2},{3,19},{19,3},{4,20},{20... | collective-permute-start | bytes 2162696 | tf_op jit(solution)/shard_map/ppermute | solution.py:790
  405.2 37.6 %collective-permute-start.8 = (bf16[4,64,1408]{2,1,0:T(8,128)(2,1)}, bf16[4,64,1408]{2,1,0:T(8,128)(2,1)S(1)}, u32[]{:S(2)}, u32[]{:S(2)}) collective-permute-start(bf16[4,64,1408]{2,1,0:T(8,128)(2,1)} %dynamic-slice_bitcast_fusion.3), channel_id=1, source_target_pairs={{0,2},{2,0},{1,3},{3,1},{4,6},{6,4},{5,7},{7,5},{8,10},{10,8},{9,1... | collective-permute-start | bytes 2162696 | tf_op jit(solution)/shard_map/ppermute | solution.py:790
  445.2 28.9 %collective-permute-start.14 = (bf16[4,64,1024]{2,1,0:T(8,128)(2,1)S(1)}, bf16[4,64,1024]{2,1,0:T(8,128)(2,1)S(1)}, u32[]{:S(2)}, u32[]{:S(2)}) collective-permute-start(bf16[4,64,1024]{2,1,0:T(8,128)(2,1)S(1)} %dynamic-slice_bitcast_fusion.4), channel_id=1, source_target_pairs={{0,16},{16,0},{1,17},{17,1},{2,18},{18,2},{3,19},{19,3},{4,20},{20... | collective-permute-start | bytes 1572872 | tf_op jit(solution)/shard_map/ppermute | solution.py:790
  446.7 27.6 %collective-permute-start.13 = (bf16[4,64,1024]{2,1,0:T(8,128)(2,1)S(1)}, bf16[4,64,1024]{2,1,0:T(8,128)(2,1)S(1)}, u32[]{:S(2)}, u32[]{:S(2)}) collective-permute-start(bf16[4,64,1024]{2,1,0:T(8,128)(2,1)S(1)} %dynamic-slice_bitcast_fusion.5), channel_id=1, source_target_pairs={{0,2},{2,0},{1,3},{3,1},{4,6},{6,4},{5,7},{7,5},{8,10},{10,8},{9,1... | collective-permute-start | bytes 1572872 | tf_op jit(solution)/shard_map/ppermute | solution.py:790
  448.2 22.9 %collective-permute-start.28 = (bf16[64,2816]{1,0:T(8,128)(2,1)S(1)}, bf16[64,2816]{1,0:T(8,128)(2,1)S(1)}, u32[]{:S(2)}, u32[]{:S(2)}) collective-permute-start(bf16[64,2816]{1,0:T(8,128)(2,1)S(1)} %get-tuple-element.162), channel_id=1, source_target_pairs={{0,4},{4,8},{8,12},{12,0},{1,5},{5,9},{9,13},{13,1},{2,6},{6,10},{... | collective-permute-start | bytes 1081352 | tf_op jit(solution)/shard_map/ppermute | solution.py:790
  450.5 23.3 %collective-permute-start.29 = (bf16[64,2816]{1,0:T(8,128)(2,1)S(1)}, bf16[64,2816]{1,0:T(8,128)(2,1)S(1)}, u32[]{:S(2)}, u32[]{:S(2)}) collective-permute-start(bf16[64,2816]{1,0:T(8,128)(2,1)S(1)} %get-tuple-element.164), channel_id=1, source_target_pairs={{0,8},{4,12},{8,0},{12,4},{1,9},{5,13},{9,1},{13,5},{2,10},{6,14},... | collective-permute-start | bytes 1081352 | tf_op jit(solution)/shard_map/ppermute | solution.py:790
  452.0 21.8 %collective-permute-start.30 = (bf16[64,2816]{1,0:T(8,128)(2,1)S(1)}, bf16[64,2816]{1,0:T(8,128)(2,1)S(1)}, u32[]{:S(2)}, u32[]{:S(2)}) collective-permute-start(bf16[64,2816]{1,0:T(8,128)(2,1)S(1)} %get-tuple-element.163), channel_id=1, source_target_pairs={{0,12},{4,0},{8,4},{12,8},{1,13},{5,1},{9,5},{13,9},{2,14},{6,2},{... | collective-permute-start | bytes 1081352 | tf_op jit(solution)/shard_map/ppermute | solution.py:790
  474.0 18.6 %collective-permute-start.31 = (bf16[32,2816]{1,0:T(8,128)(2,1)S(1)}, bf16[32,2816]{1,0:T(8,128)(2,1)S(1)}, u32[]{:S(2)}, u32[]{:S(2)}) collective-permute-start(bf16[32,2816]{1,0:T(8,128)(2,1)S(1)} %get-tuple-element.178), channel_id=1, source_target_pairs={{0,1},{1,0},{2,3},{3,2},{4,5},{5,4},{6,7},{7,6},{8,9},{9,8},{10,11... | collective-permute-start | bytes 540680 | tf_op jit(solution)/shard_map/ppermute | solution.py:778
  474.7 19.0 %collective-permute-start.15 = (bf16[64,2048]{1,0:T(8,128)(2,1)S(1)}, bf16[64,2048]{1,0:T(8,128)(2,1)S(1)}, u32[]{:S(2)}, u32[]{:S(2)}) collective-permute-start(bf16[64,2048]{1,0:T(8,128)(2,1)S(1)} %get-tuple-element.165), channel_id=1, source_target_pairs={{0,4},{4,8},{8,12},{12,0},{1,5},{5,9},{9,13},{13,1},{2,6},{6,10},{... | collective-permute-start | bytes 786440 | tf_op jit(solution)/shard_map/ppermute | solution.py:790
  483.0 20.2 %collective-permute-start.16 = (bf16[64,2048]{1,0:T(8,128)(2,1)S(1)}, bf16[64,2048]{1,0:T(8,128)(2,1)S(1)}, u32[]{:S(2)}, u32[]{:S(2)}) collective-permute-start(bf16[64,2048]{1,0:T(8,128)(2,1)S(1)} %get-tuple-element.167), channel_id=1, source_target_pairs={{0,8},{4,12},{8,0},{12,4},{1,9},{5,13},{9,1},{13,5},{2,10},{6,14},... | collective-permute-start | bytes 786440 | tf_op jit(solution)/shard_map/ppermute | solution.py:790
  485.4 17.7 %collective-permute-start.17 = (bf16[64,2048]{1,0:T(8,128)(2,1)S(1)}, bf16[64,2048]{1,0:T(8,128)(2,1)S(1)}, u32[]{:S(2)}, u32[]{:S(2)}) collective-permute-start(bf16[64,2048]{1,0:T(8,128)(2,1)S(1)} %get-tuple-element.166), channel_id=1, source_target_pairs={{0,12},{4,0},{8,4},{12,8},{1,13},{5,1},{9,5},{13,9},{2,14},{6,2},{... | collective-permute-start | bytes 786440 | tf_op jit(solution)/shard_map/ppermute | solution.py:790
  485.4 7.2 %copy-start.3 = (bf16[32,2752]{1,0:T(8,128)(2,1)S(1)}, bf16[32,2752]{1,0:T(8,128)(2,1)}, u32[]{:S(2)}) copy-start(bf16[32,2752]{1,0:T(8,128)(2,1)} %param.22) | copy-start | bytes 528388
  485.4 7.2 %copy-start.4 = (bf16[32,2752]{1,0:T(8,128)(2,1)S(1)}, bf16[32,2752]{1,0:T(8,128)(2,1)}, u32[]{:S(2)}) copy-start(bf16[32,2752]{1,0:T(8,128)(2,1)} %param.21) | copy-start | bytes 528388
  492.6 10.8 %copy-start.13 = (bf16[32]{0:T(256)(128)(2,1)S(1)}, bf16[32]{0:T(256)(128)(2,1)}, u32[]{:S(2)}) copy-start(bf16[32]{0:T(256)(128)(2,1)} %param.20) | copy-start | bytes 196
  492.6 13.0 %collective-permute-start.19 = (bf16[1024,768]{1,0:T(8,128)(2,1)}, bf16[1024,768]{1,0:T(8,128)(2,1)S(1)}, u32[]{:S(2)}, u32[]{:S(2)}) collective-permute-start(bf16[1024,768]{1,0:T(8,128)(2,1)} %weight_grad.14), channel_id=1, source_target_pairs={{0,1},{1,0},{2,3},{3,2},{4,5},{5,4},{6,7},{7,6},{8,9},{9,8},{10,11... | collective-permute-start | bytes 4718600 | tf_op jit(solution)/shard_map/ppermute | solution.py:778
  503.3 1.4 collective-permute-start.18
  505.6 1.1 copy-start.1
  515.7 12.1 %collective-permute-start.21 = (bf16[2,4,64,384]{3,2,1,0:T(8,128)(2,1)S(1)}, bf16[2,4,64,384]{3,2,1,0:T(8,128)(2,1)S(1)}, u32[]{:S(2)}, u32[]{:S(2)}) collective-permute-start(bf16[2,4,64,384]{3,2,1,0:T(8,128)(2,1)S(1)} %dynamic-slice_bitcast_fusion.6), channel_id=1, source_target_pairs={{0,2},{2,0},{1,3},{3,1},{4,6},{6,4},{5,7},{7,5},{8,10},{10,8},{9,1... | collective-permute-start | bytes 1179656 | tf_op jit(solution)/shard_map/ppermute | solution.py:790
  517.3 11.0 %collective-permute-start.20 = (bf16[4,2,64,384]{3,2,0,1:T(8,128)(2,1)S(1)}, bf16[4,2,64,384]{3,2,0,1:T(8,128)(2,1)S(1)}, u32[]{:S(2)}, u32[]{:S(2)}) collective-permute-start(bf16[4,2,64,384]{3,2,0,1:T(8,128)(2,1)S(1)} %bitcast.145), channel_id=1, source_target_pairs={{0,16},{16,0},{1,17},{17,1},{2,18},{18,2},{3,19},{19,3},{4,20},{20... | collective-permute-start | bytes 1179656 | tf_op jit(solution)/shard_map/ppermute | solution.py:790
  528.4 11.2 %collective-permute-start.23 = (bf16[4,64,384]{2,1,0:T(8,128)(2,1)S(1)}, bf16[4,64,384]{2,1,0:T(8,128)(2,1)S(1)}, u32[]{:S(2)}, u32[]{:S(2)}) collective-permute-start(bf16[4,64,384]{2,1,0:T(8,128)(2,1)S(1)} %dynamic-slice_bitcast_fusion.13), channel_id=1, source_target_pairs={{0,16},{16,0},{1,17},{17,1},{2,18},{18,2},{3,19},{19,3},{4,20},{20... | collective-permute-start | bytes 589832 | tf_op jit(solution)/shard_map/ppermute | solution.py:790
  529.4 10.3 %collective-permute-start.22 = (bf16[4,64,384]{2,1,0:T(8,128)(2,1)S(1)}, bf16[4,64,384]{2,1,0:T(8,128)(2,1)S(1)}, u32[]{:S(2)}, u32[]{:S(2)}) collective-permute-start(bf16[4,64,384]{2,1,0:T(8,128)(2,1)S(1)} %dynamic-slice_bitcast_fusion.14), channel_id=1, source_target_pairs={{0,2},{2,0},{1,3},{3,1},{4,6},{6,4},{5,7},{7,5},{8,10},{10,8},{9,1... | collective-permute-start | bytes 589832 | tf_op jit(solution)/shard_map/ppermute | solution.py:790
  539.9 9.4 %collective-permute-start.24 = (bf16[64,768]{1,0:T(8,128)(2,1)S(1)}, bf16[64,768]{1,0:T(8,128)(2,1)S(1)}, u32[]{:S(2)}, u32[]{:S(2)}) collective-permute-start(bf16[64,768]{1,0:T(8,128)(2,1)S(1)} %get-tuple-element.172), channel_id=1, source_target_pairs={{0,4},{4,8},{8,12},{12,0},{1,5},{5,9},{9,13},{13,1},{2,6},{6,10},{... | collective-permute-start | bytes 294920 | tf_op jit(solution)/shard_map/ppermute | solution.py:790
  546.0 7.5 %collective-permute-start.25 = (bf16[64,768]{1,0:T(8,128)(2,1)S(1)}, bf16[64,768]{1,0:T(8,128)(2,1)S(1)}, u32[]{:S(2)}, u32[]{:S(2)}) collective-permute-start(bf16[64,768]{1,0:T(8,128)(2,1)S(1)} %get-tuple-element.174), channel_id=1, source_target_pairs={{0,8},{4,12},{8,0},{12,4},{1,9},{5,13},{9,1},{13,5},{2,10},{6,14},... | collective-permute-start | bytes 294920 | tf_op jit(solution)/shard_map/ppermute | solution.py:790
  546.4 7.0 %collective-permute-start.26 = (bf16[64,768]{1,0:T(8,128)(2,1)S(1)}, bf16[64,768]{1,0:T(8,128)(2,1)S(1)}, u32[]{:S(2)}, u32[]{:S(2)}) collective-permute-start(bf16[64,768]{1,0:T(8,128)(2,1)S(1)} %get-tuple-element.173), channel_id=1, source_target_pairs={{0,12},{4,0},{8,4},{12,8},{1,13},{5,1},{9,5},{13,9},{2,14},{6,2},{... | collective-permute-start | bytes 294920 | tf_op jit(solution)/shard_map/ppermute | solution.py:790
  549.1 6.9 %copy-start.6 = (bf16[32,1024]{1,0:T(8,128)(2,1)S(1)}, bf16[32,1024]{1,0:T(8,128)(2,1)}, u32[]{:S(2)}) copy-start(bf16[32,1024]{1,0:T(8,128)(2,1)} %param.18) | copy-start | bytes 196612
  553.6 4.0 copy-start.7
  553.6 1.4 collective-permute-start.27
  555.1 2.5 copy-start.11
  556.0 2.1 copy-start.5
  (4 other events, 3.2 us)
Sparse Core Ops, SparseCore 0:
  11.5 132.8 all-gather.1

commit v4 on v3

--- a/solution.py
+++ b/solution.py
@@ -20,6 +20,7 @@
 PAIR = 2 * VROWS
 SENT = HEAD_DIM + 8
 HG = 4
+FIRST_BACK, SECOND_BACK = 4, 2
 
 epsilon = 1e-05
 F32 = jnp.float32
@@ -122,7 +123,7 @@
     ones2 = first_row(16, CUT, 2).astype(BF16)
     const = first_row(FEAT, CUT)
     one_low = const.astype(BF16)
-    mixed_ref, rest_ref, den_ref, saved_ref, state = refs[-5:]
+    mixed_ref, den_ref, saved_ref, state = refs[-4:]
     scale = 2.0 * lane_scale()
     mask = causal_mask()
     unpack_states(init_ref, state)
@@ -144,11 +145,8 @@
             earlier = dot(low, phi_rows(q.astype(F32), const), NN)
             numer = dot(v_aug, weight, NN) + (earlier[:VROWS] + earlier[VROWS:])
             den = numer[HEAD_DIM : HEAD_DIM + 1]
-            wide = numer[:HEAD_DIM] * (1.0 / den)
-            mixed_low = wide.astype(BF16)
             rows = slice(h * HEAD_DIM, (h + 1) * HEAD_DIM)
-            mixed_ref[rows, cols] = mixed_low
-            rest_ref[rows, cols] = (wide - mixed_low.astype(F32)).astype(BF16)
+            mixed_ref[rows, cols] = (numer[:HEAD_DIM] * (1.0 / den)).astype(BF16)
             den_ref[0, h : h + 1, cols] = 0.5 * den
             state[h] += dot(v_aug, phi_rows(k.astype(F32), const), NT)
         return carry
@@ -156,9 +154,7 @@
     lax.fori_loop(0, blocks, step, 0)
 
 
-def back_state_kernel(
-    blocks, qkv_ref, grad_ref, mixed_ref, rest_ref, den_ref, nb_ref, out_ref
-):
+def back_state_kernel(blocks, qkv_ref, grad_ref, mixed_ref, den_ref, nb_ref, out_ref):
     const = first_row(FEAT, CUT)
     row = lax.broadcasted_iota(jnp.int32, (16, CUT), 0)
 
@@ -172,9 +168,7 @@
             g = grad_ref[rows, cols].astype(F32)
             inverse = 1.0 / den_ref[0, h : h + 1, cols]
             db = -inverse * jnp.sum(
-                g * (mixed_ref[rows, cols].astype(F32) + rest_ref[rows, cols].astype(F32)),
-                axis=0,
-                keepdims=True,
+                g * mixed_ref[rows, cols].astype(F32), axis=0, keepdims=True
             )
             nb = (g * inverse).astype(BF16)
             high = db.astype(BF16).astype(F32)
@@ -189,17 +183,49 @@
     pack_states(sums, out_ref)
 
 
-def backward_kernel(blocks, qkv_ref, nb_ref, saved_ref, init_ref, *refs):
+def backward_kernel(
+    sizes,
+    blocks,
+    qkv_ref,
+    nb_ref,
+    saved_ref,
+    init_ref,
+    one_ref,
+    two_ref,
+    block_ref,
+    out_ref,
+    pair_out,
+    part_out,
+    state,
+    *refs,
+):
     ones2 = first_row(16, CUT, 2).astype(BF16)
     const = first_row(FEAT, CUT)
     one_low = const.astype(BF16)
-    out_ref, state = refs[-2:]
     scale = lane_scale()
     mask = causal_mask()
-    unpack_states(init_ref, state)
+    halves = pl.num_programs(1)
+    at = pl.program_id(0) * halves + pl.program_id(1)
+    last = pl.num_programs(0) * halves - 1
+    each = blocks // halves
+    by_seq, by_z, by_y, by_core = neighbours(sizes)
+    count = 6 + 8
+    first = RowSums(sizes, (one_ref, two_ref), refs[:count], pair_out, summed=True)
+    refs = refs[count:]
+    second = RowSums(sizes, block_ref, refs[:6] + (part_out,) + refs[6:])
+
+    @pl.when(at == 0)
+    def _():
+        greet(by_seq + by_z + [by_y, by_core])
+        first.second()
+        second.start()
+
+    @pl.when(pl.program_id(1) == 0)
+    def _():
+        unpack_states(init_ref, state)
 
     def step(i, carry):
-        b = blocks - 1 - i
+        b = blocks - 1 - (pl.program_id(1) * each + i)
         cols = pl.ds(pl.multiple_of(b * CUT, CUT), CUT)
         for h in range(HG):
             base = h * HROWS
@@ -232,11 +258,26 @@
             state[h] += dot(nb, phi_rows(qf, const), NT)
         return carry
 
-    lax.fori_loop(0, blocks, step, 0)
+    lax.fori_loop(0, each, step, 0)
+
+    @pl.when(at == last - FIRST_BACK)
+    def _():
+        first.third()
+
+    @pl.when(at == last - SECOND_BACK)
+    def _():
+        second.second()
+
+    @pl.when(at == last)
+    def _():
+        second.third()
+        first.fourth()
+        second.finish()
+        first.finish()
 
 
 def cost(flops):
-    return pl.CostEstimate(flops=int(flops), bytes_accessed=0, transcendentals=0)
+    return pl.CostEstimate(flops=int(flops * 0.02), bytes_accessed=0, transcendentals=0)
 
 
 def head_spec(rows, cols):
@@ -291,12 +332,10 @@
         + [pl.BlockSpec(memory_space=pl.ANY)] * len(filled),
         out_specs=[
             head_rows(HEAD_DIM),
-            head_rows(HEAD_DIM),
             pl.BlockSpec((1, HG, cols), lambda g: (first + g, 0, 0)),
             lead(blocks, PAIR, FROWS),
         ],
         out_shape=[
-            jax.ShapeDtypeStruct((HEADS * HEAD_DIM, cols), BF16),
             jax.ShapeDtypeStruct((HEADS * HEAD_DIM, cols), BF16),
             jax.ShapeDtypeStruct((HEADS // HG, HG, cols), F32),
             jax.ShapeDtypeStruct((HEADS, blocks, PAIR, FROWS), BF16),
@@ -309,14 +348,13 @@
     )(qkv, init, *filled)
 
 
-def local_back_state(qkv, grad, mixed, rest, den):
+def local_back_state(qkv, grad, mixed, den):
     cols = qkv.shape[1]
     return pl.pallas_call(
         functools.partial(back_state_kernel, cols // CUT),
         grid=(HEADS // HG,),
         in_specs=[
             head_spec(HROWS, cols),
-            head_spec(HEAD_DIM, cols),
             head_spec(HEAD_DIM, cols),
             head_spec(HEAD_DIM, cols),
             pl.BlockSpec((1, HG, cols), lambda g: (g, 0, 0)),
@@ -329,44 +367,59 @@
         compiler_params=VMEM_LIMIT,
         cost_estimate=cost(13e9 * cols / 2048),
         name="query_state",
-    )(qkv, grad, mixed, rest, den)
-
-
-def attention_backward(qkv, nb, saved, init, start, count, filled=None):
+    )(qkv, grad, mixed, den)
+
+
+def attention_backward(qkv, nb, saved, init, one, two, block, own):
     cols = qkv.shape[1]
     blocks = cols // CUT
-    first = start // HG
+    sizes = lax.axis_size("seq"), lax.axis_size("z")
+    width = block.shape[-1]
+    cut = 128 * (width // 256)
+    wide = one.shape[-1] + two.shape[-1]
+    first_buffers, first_sems = row_sum_scratch(
+        sizes, own, one.shape[-1], two.shape[-1], summed=True
+    )
+    second_buffers, second_sems = row_sum_scratch(
+        sizes, own, cut, width - cut, ends=False, keep=False
+    )
 
     def head_rows(rows):
-        return pl.BlockSpec((HG * rows, cols), lambda g: (first + g, 0))
+        return pl.BlockSpec((HG * rows, cols), lambda g, p: (g, 0))
 
     def lead(*tail):
-        return pl.BlockSpec((HG,) + tail, lambda g: (first + g,) + (0,) * len(tail))
-
-    operands = [qkv, nb, saved, init]
-    in_specs = [
-        head_rows(HROWS),
-        lead(VROWS, cols),
-        lead(blocks, PAIR, FROWS),
-        pl.BlockSpec((HG // 2, 3, SENT, 128), lambda g: (first + g, 0, 0, 0)),
-    ]
-    aliases = {}
-    if filled is not None:
-        operands.append(filled)
-        in_specs.append(pl.BlockSpec(memory_space=pl.ANY))
-        aliases = {4: 0}
+        return pl.BlockSpec((HG,) + tail, lambda g, p: (g,) + (0,) * len(tail))
+
+    here = pl.BlockSpec(memory_space=pltpu.VMEM)
     return pl.pallas_call(
-        functools.partial(backward_kernel, blocks),
-        grid=(count // HG,),
-        in_specs=in_specs,
-        out_specs=head_rows(HROWS),
-        out_shape=jax.ShapeDtypeStruct((HEADS * HROWS, cols), BF16),
-        scratch_shapes=[pltpu.VMEM((HG, VROWS, FROWS), F32)],
-        compiler_params=VMEM_LIMIT,
-        cost_estimate=cost(53e9 * cols / 2048 * count / HEADS),
-        input_output_aliases=aliases,
+        functools.partial(backward_kernel, sizes, blocks),
+        grid=(HEADS // HG, 2),
+        in_specs=[
+            head_rows(HROWS),
+            lead(VROWS, cols),
+            lead(blocks, PAIR, FROWS),
+            pl.BlockSpec((HG // 2, 3, SENT, 128), lambda g, p: (g, 0, 0, 0)),
+            here,
+            here,
+            here,
+        ],
+        out_specs=[head_rows(HROWS), here, here],
+        out_shape=[
+            jax.ShapeDtypeStruct((HEADS * HROWS, cols), BF16),
+            jax.ShapeDtypeStruct((2, own, wide), BF16),
+            jax.ShapeDtypeStruct((sizes[1], 2, own, width), BF16),
+        ],
+        scratch_shapes=[pltpu.VMEM((HG, VROWS, FROWS), F32)]
+        + first_buffers
+        + first_sems
+        + second_buffers
+        + second_sems,
+        compiler_params=pltpu.CompilerParams(
+            collective_id=2, has_side_effects=True, vmem_limit_bytes=58 * 1024 * 1024
+        ),
+        cost_estimate=cost(53e9 * cols / 2048),
         name="attend_back",
-    )(*operands)
+    )(qkv, nb, saved, init, one, two, block.reshape(sizes + (2, 2, own, width)))
 
 
 MESH = pl.DeviceIdType.MESH
@@ -481,12 +534,13 @@
     return out.reshape(-1, cols)
 
 
-def project_kernel(tokens_ref, weight_ref, gain_ref, qkv_ref, normed_ref, flipped_ref):
+def project_kernel(tokens_ref, weight_ref, qkv_ref, normed_ref, flipped_ref, gain_ref):
     width = tokens_ref.shape[2]
     lead = HEADS * FEAT
 
     @pl.when(pl.program_id(0) == 0)
     def _():
+        gain_ref[...] = weight_ref[:, :128].astype(F32).T[:8]
         for c in range(HEADS * HROWS // 128):
             piece = weight_ref[:, 128 * (c + 1) : 128 * (c + 2)].T
             start = 128 * c
@@ -502,12 +556,12 @@
 
     tokens = tokens_ref[0].astype(F32)
     scale = lax.rsqrt(jnp.sum(tokens * tokens, -1, keepdims=True) * (1.0 / width) + epsilon)
-    normed = (tokens * scale * gain_ref[...]).astype(BF16)
+    normed = (tokens * scale * gain_ref[0:1]).astype(BF16)
     normed_ref[...] = normed.T
     qkv_ref[...] = dot(flipped_ref[...], normed, NT).astype(BF16)
 
 
-def project(tokens, early, gain):
+def project(tokens, early):
     rows, width = tokens.shape[1:]
     tile = min(rows, 512)
     return pl.pallas_call(
@@ -518,64 +572,329 @@
             pl.BlockSpec(
                 (width, 128 + HEADS * HROWS), lambda i: (0, 0), pipeline_mode=pl.Buffered(1)
             ),
-            pl.BlockSpec((1, width), lambda i: (0, 0)),
         ],
         out_specs=[
             pl.BlockSpec((HEADS * HROWS, tile), lambda i: (0, i)),
             pl.BlockSpec((width, tile), lambda i: (0, i)),
             pl.BlockSpec((HEADS * HROWS, width), lambda i: (0, 0)),
+            pl.BlockSpec((8, width), lambda i: (0, 0)),
         ],
         out_shape=[
             jax.ShapeDtypeStruct((HEADS * HROWS, rows), BF16),
             jax.ShapeDtypeStruct((width, rows), BF16),
             jax.ShapeDtypeStruct((HEADS * HROWS, width), BF16),
+            jax.ShapeDtypeStruct((8, width), F32),
         ],
         compiler_params=VMEM_LIMIT,
         cost_estimate=cost(2 * HEADS * HROWS * rows * width),
         name="project",
-    )(tokens, early, gain)
-
-
-def input_kernel(back_ref, flipped_ref, tokens_ref, resid_ref, gain_ref, *refs):
-    out_ref = refs[-1]
+    )(tokens, early)
+
+
+def remote(src, dst, sems, slot, device):
+    return pltpu.make_async_remote_copy(
+        src_ref=src,
+        dst_ref=dst,
+        send_sem=sems[0].at[slot],
+        recv_sem=sems[1].at[slot],
+        device_id=device,
+        device_id_type=MESH,
+    )
+
+
+def positions():
+    return tuple(lax.axis_index(name) for name in ("seq", "z", "y", "core"))
+
+
+def neighbours(sizes):
+    seq_parts, z_parts = sizes
+    s, z, y, c = positions()
+    by_seq = [(lax.rem(s + j, seq_parts), z, y, c) for j in range(1, seq_parts)]
+    by_z = [(s, lax.rem(z + k, z_parts), y, c) for k in range(1, z_parts)]
+    return by_seq, by_z, (s, z, 1 - y, c), (s, z, y, 1 - c)
+
+
+def greet(devices):
+    barrier = pltpu.get_barrier_semaphore()
+    for device in devices:
+        pl.semaphore_signal(barrier, inc=1, device_id=device, device_id_type=MESH)
+    pl.semaphore_wait(barrier, len(devices))
+
+
+class RowSums:
+    def __init__(self, sizes, source, refs, out_ref=None, summed=False):
+        seq_parts, z_parts = self.sizes = sizes
+        s, z, y, c = self.place = positions()
+        by_seq, by_z, by_y, by_core = neighbours(sizes)
+        self.source, self.summed, self.out_ref = source, summed, out_ref
+        refs = list(refs)
+        if summed:
+            self.x_sum, self.y_sum = source
+        else:
+            self.x_in, self.x_sum, self.y_in, self.y_sum = refs[:4]
+            del refs[:4]
+        self.then_y_in, self.then_x_in, self.row_sum = refs[:3]
+        del refs[:3]
+        self.cut = self.x_sum.shape[-1]
+        rest = self.y_sum.shape[-1]
+        if out_ref is not None:
+            self.z_in, self.own_sum, self.swapped = refs[:3]
+            del refs[:3]
+        pairs = [refs[2 * i : 2 * i + 2] for i in range(len(refs) // 2)]
+        others = range(1, seq_parts)
+        self.first = []
+        if not summed:
+            left, right = pl.ds(0, self.cut), pl.ds(self.cut, rest)
+            self.first_x = [
+                remote(
+                    source.at[lax.rem(s + j, seq_parts), :, :, :, :, left],
+                    self.x_in.at[j - 1],
+                    pairs[2],
+                    j - 1,
+                    by_seq[j - 1],
+                )
+                for j in others
+            ]
+            self.first_y = remote(
+                source.at[:, :, 1 - y, :, :, right], self.y_in, pairs[3], 0, by_y
+            )
+            self.first = self.first_x + [self.first_y]
+        self.then_y = remote(self.x_sum.at[:, 1 - y], self.then_y_in, pairs[0], 0, by_y)
+        self.then_x = [
+            remote(
+                self.y_sum.at[lax.rem(s + j, seq_parts)],
+                self.then_x_in.at[j - 1],
+                pairs[1],
+                j - 1,
+                by_seq[j - 1],
+            )
+            for j in others
+        ]
+        if out_ref is not None:
+            self.along = along_z(sizes, self.row_sum, self.z_in, pairs[-2])
+            self.across = remote(self.own_sum.at[1 - c], self.swapped, pairs[-1], 0, by_core)
+
+    def start(self):
+        for copy in self.first:
+            copy.start()
+
+    def second(self):
+        s, z, y, c = self.place
+        if not self.summed:
+            for copy in self.first_x:
+                copy.wait_recv()
+            total = self.source[s, :, :, :, :, : self.cut].astype(F32)
+            for j in range(self.sizes[0] - 1):
+                total = total + self.x_in[j].astype(F32)
+            self.x_sum[...] = total.astype(BF16)
+        self.then_y.start()
+        if not self.summed:
+            self.first_y.wait_recv()
+            total = self.source[:, :, y, :, :, self.cut :].astype(F32)
+            self.y_sum[...] = (total + self.y_in[...].astype(F32)).astype(BF16)
+        for copy in self.then_x:
+            copy.start()
+
+    def third(self):
+        s, z, y, c = self.place
+        self.then_y.wait_recv()
+        total = self.x_sum[:, y].astype(F32) + self.then_y_in[...].astype(F32)
+        self.row_sum[:, :, :, : self.cut] = total.astype(BF16)
+        for copy in self.then_x:
+            copy.wait_recv()
+        total = self.y_sum[s].astype(F32)
+        for j in range(self.sizes[0] - 1):
+            total = total + self.then_x_in[j].astype(F32)
+        self.row_sum[:, :, :, self.cut :] = total.astype(BF16)
+        if self.out_ref is not None:
+            for copy in self.along:
+                copy.start()
+
+    def fourth(self):
+        sum_z(self.along, self.row_sum, self.z_in, self.own_sum)
+        self.across.start()
+        c = self.place[3]
+        self.out_ref[c] = self.own_sum[c]
+
+    def finish(self):
+        for copy in self.first + [self.then_y] + self.then_x:
+            copy.wait_send()
+        if self.out_ref is not None:
+            self.across.wait_recv()
+            self.out_ref[1 - self.place[3]] = self.swapped[...]
+            self.across.wait_send()
+            for copy in self.along:
+                copy.wait_send()
+
+
+def along_z(sizes, source, z_in, sems):
+    z_parts = sizes[1]
+    z = positions()[1]
+    by_z = neighbours(sizes)[1]
+    return [
+        remote(source.at[lax.rem(z + k, z_parts)], z_in.at[k - 1], sems, k - 1, by_z[k - 1])
+        for k in range(1, z_parts)
+    ]
+
+
+def sum_z(copies, source, z_in, own_sum):
+    for copy in copies:
+        copy.wait_recv()
+    total = source[positions()[1]].astype(F32)
+    for k in range(len(copies)):
+        total = total + z_in[k].astype(F32)
+    own_sum[...] = total.astype(BF16)
+
+
+def row_sum_scratch(sizes, own, cut, rest, summed=False, ends=True, keep=True):
+    seq_parts, z_parts = sizes
+    cols = cut + rest
+
+    def low(*shape):
+        return pltpu.VMEM(shape, BF16)
+
+    first = [
+        low(seq_parts - 1, z_parts, 2, 2, own, cut),
+        low(z_parts, 2, 2, own, cut),
+        low(seq_parts, z_parts, 2, own, rest),
+        low(seq_parts, z_parts, 2, own, rest),
+    ]
+    buffers = [] if summed else first
+    buffers += [low(z_parts, 2, own, cut), low(seq_parts - 1, z_parts, 2, own, rest)]
+    if keep:
+        buffers += [low(z_parts, 2, own, cols)]
+    counts = [1, seq_parts - 1]
+    if not summed:
+        counts += [seq_parts - 1, 1]
+    if ends:
+        buffers += [low(z_parts - 1, 2, own, cols), low(2, own, cols), low(own, cols)]
+        counts += [z_parts - 1, 1]
+    return buffers, [pltpu.SemaphoreType.DMA((n,)) for n in counts for _ in range(2)]
+
+
+def input_kernel(
+    sizes,
+    back_ref,
+    flipped_ref,
+    tokens_ref,
+    resid_ref,
+    gain_ref,
+    block_ref,
+    part_ref,
+    out_ref,
+    block_out,
+    part_out,
+    part_z_in,
+    part_sum,
+    part_swapped,
+    z_send,
+    z_recv,
+    core_send,
+    core_recv,
+    *refs,
+):
+    step = pl.program_id(0)
+    last = pl.num_programs(0) - 1
+    c = positions()[3]
+    by_seq, by_z, by_y, by_core = neighbours(sizes)
+    sums = RowSums(sizes, block_ref, refs, block_out)
+    part_along = along_z(sizes, part_ref, part_z_in, (z_send, z_recv))
+    part_across = remote(
+        part_sum.at[1 - c], part_swapped, (core_send, core_recv), 0, by_core
+    )
+
+    @pl.when(step == 0)
+    def _():
+        greet(by_seq + by_z + [by_y, by_core])
+        for copy in part_along:
+            copy.start()
+        sums.start()
+
     width = tokens_ref.shape[2]
     tokens = tokens_ref[0].astype(F32)
     scale = lax.rsqrt(jnp.sum(tokens * tokens, -1, keepdims=True) * (1.0 / width) + epsilon)
     unit = tokens * scale
     normed_back = dot(back_ref[...], flipped_ref[...], TN)
-    scaled = normed_back * gain_ref[...]
+    scaled = normed_back * gain_ref[0:1]
     middle = jnp.sum(scaled * unit, -1, keepdims=True) * (1.0 / width)
     out_ref[0] = resid_ref[...] + scale * (scaled - unit * middle)
 
-
-def input_gradient(back, flipped, tokens, resid_back, gain, first, count, filled=None):
+    @pl.when(step == last - 2)
+    def _():
+        sums.second()
+
+    @pl.when(step == last - 1)
+    def _():
+        sums.third()
+
+    @pl.when(step == last)
+    def _():
+        sum_z(part_along, part_ref, part_z_in, part_sum)
+        part_across.start()
+        part_out[c] = part_sum[c]
+        sums.fourth()
+        part_across.wait_recv()
+        part_out[1 - c] = part_swapped[...]
+        sums.finish()
+        for copy in part_along:
+            copy.wait_send()
+        part_across.wait_send()
+
+
+def input_gradient(back, flipped, tokens, resid_back, gain, block, part, own):
     rows, width = tokens.shape[1:]
-    tile = min(rows // 2, 512)
-    first, count = first // tile, count // tile
-    operands = [back, flipped, tokens, resid_back, gain]
-    in_specs = [
-        pl.BlockSpec((HEADS * HROWS, tile), lambda i: (0, first + i)),
-        pl.BlockSpec(flipped.shape, lambda i: (0, 0), pipeline_mode=pl.Buffered(1)),
-        pl.BlockSpec((1, tile, width), lambda i: (0, first + i, 0)),
-        pl.BlockSpec((tile, width), lambda i: (first + i, 0)),
-        pl.BlockSpec((1, width), lambda i: (0, 0)),
-    ]
-    aliases = {}
-    if filled is not None:
-        operands.append(filled)
-        in_specs.append(pl.BlockSpec(memory_space=pl.ANY))
-        aliases = {5: 0}
+    tile = min(rows // 4, 512)
+    sizes = lax.axis_size("seq"), lax.axis_size("z")
+    cols, part_cols = block.shape[-1], part.shape[-1]
+    cut = 128 * (cols // 256)
+    buffers, sems = row_sum_scratch(sizes, own, cut, cols - cut)
     return pl.pallas_call(
-        input_kernel,
-        grid=(count,),
-        in_specs=in_specs,
-        out_specs=pl.BlockSpec((1, tile, width), lambda i: (0, first + i, 0)),
-        out_shape=jax.ShapeDtypeStruct((1, rows, width), F32),
-        compiler_params=VMEM_LIMIT,
-        cost_estimate=cost(4 * HEADS * HROWS * count * tile * width),
-        input_output_aliases=aliases,
+        functools.partial(input_kernel, sizes),
+        grid=(rows // tile,),
+        in_specs=[
+            pl.BlockSpec((HEADS * HROWS, tile), lambda i: (0, i)),
+            pl.BlockSpec(flipped.shape, lambda i: (0, 0), pipeline_mode=pl.Buffered(1)),
+            pl.BlockSpec((1, tile, width), lambda i: (0, i, 0)),
+            pl.BlockSpec((tile, width), lambda i: (i, 0)),
+            pl.BlockSpec((8, width), lambda i: (0, 0)),
+            pl.BlockSpec(memory_space=pltpu.VMEM),
+            pl.BlockSpec(memory_space=pltpu.VMEM),
+        ],
+        out_specs=[
+            pl.BlockSpec((1, tile, width), lambda i: (0, i, 0)),
+            pl.BlockSpec(memory_space=pltpu.VMEM),
+            pl.BlockSpec(memory_space=pltpu.VMEM),
+        ],
+        out_shape=[
+            jax.ShapeDtypeStruct((1, rows, width), F32),
+            jax.ShapeDtypeStruct((2, own, cols), BF16),
+            jax.ShapeDtypeStruct((2, own, part_cols), BF16),
+        ],
+        scratch_shapes=[
+            pltpu.VMEM((sizes[1] - 1, 2, own, part_cols), BF16),
+            pltpu.VMEM((2, own, part_cols), BF16),
+            pltpu.VMEM((own, part_cols), BF16),
+            pltpu.SemaphoreType.DMA((sizes[1] - 1,)),
+            pltpu.SemaphoreType.DMA((sizes[1] - 1,)),
+            pltpu.SemaphoreType.DMA((1,)),
+            pltpu.SemaphoreType.DMA((1,)),
+        ]
+        + buffers
+        + sems,
+        compiler_params=pltpu.CompilerParams(
+            collective_id=1, has_side_effects=True, vmem_limit_bytes=56 * 1024 * 1024
+        ),
+        cost_estimate=cost(4 * HEADS * HROWS * rows * width),
         name="input_gradient",
-    )(*operands)
+    )(
+        back,
+        flipped,
+        tokens,
+        resid_back,
+        gain,
+        block.reshape(sizes + (2, 2, own, cols)),
+        part,
+    )
 
 
 def ffn_kernel(
@@ -585,7 +904,6 @@
     target_ref,
     mixed_ref,
     gain_ref,
-    early_ref,
     late_ref,
     result_ref,
     normed_ref,
@@ -606,13 +924,12 @@
 ):
     step = pl.program_id(0)
     tile, width = tokens_ref.shape[1:]
+    starts = (0, width, width + padded, width + 2 * padded)
     copies = [
         pltpu.make_async_copy(
-            early_ref.at[:, pl.ds(128 + HEADS * HROWS, width)], w_out, sems.at[0]
+            late_ref.at[:, pl.ds(start, held.shape[1])], held, sems.at[k]
         )
-    ] + [
-        pltpu.make_async_copy(late_ref.at[:, pl.ds(k * padded, padded)], held, sems.at[k + 1])
-        for k, held in enumerate((w_gate, w_up, w_down))
+        for k, (start, held) in enumerate(zip(starts, (w_out, w_gate, w_up, w_down)))
     ]
 
     @pl.when(step == 0)
@@ -622,7 +939,7 @@
         error_ref[...] = jnp.zeros_like(error_ref)
         copies[0].wait()
 
-    gain = gain_ref[...]
+    gain = gain_ref[1:2]
     resid = tokens_ref[0].astype(F32) + dot(mixed_ref[...], w_out[...], TN)
     scale = lax.rsqrt(jnp.sum(resid * resid, -1, keepdims=True) * (1.0 / width) + epsilon)
     unit = resid * scale
@@ -676,7 +993,7 @@
     mixed_back_ref[...] = dot(w_out[...], attended, NT).astype(BF16)
 
 
-def feed_forward(count, tokens, targets, mixed, gain, early, late, padded):
+def feed_forward(count, tokens, targets, mixed, gain, late, padded):
     rows, width = tokens.shape[1:]
     tile = min(rows, 256)
     token_spec = pl.BlockSpec((1, tile, width), lambda i, c: (0, i, 0))
@@ -695,8 +1012,7 @@
                 token_spec,
                 token_spec,
                 tall,
-                line,
-                pl.BlockSpec(memory_space=pl.ANY),
+                pl.BlockSpec((8, width), lambda i, c: (0, 0)),
                 pl.BlockSpec(memory_space=pl.ANY),
             ],
             out_specs=[
@@ -734,7 +1050,7 @@
         compiler_params=pltpu.CompilerParams(vmem_limit_bytes=60 * 1024 * 1024),
         cost_estimate=cost(4 * rows * width * (width + 3 * padded)),
         name="feed_forward",
-    )(count, tokens, targets, mixed, gain, early, late)
+    )(count, tokens, targets, mixed, gain, late)
 
 
 def weight_grad_kernel(form, pick_ref, left_ref, right_ref, *refs):
@@ -778,17 +1094,26 @@
     return lax.ppermute(array, "core", [(i, 1 - i) for i in range(2)])
 
 
-def sum_over(pieces, axis, dim):
+def to_send(pieces, axis, dim):
     parts = lax.axis_size(axis)
     index = lax.axis_index(axis)
-    total = lax.dynamic_index_in_dim(pieces, index, dim, keepdims=False).astype(F32)
-    for shift in range(1, parts):
-        sent = lax.dynamic_index_in_dim(
-            pieces, lax.rem(index + shift, parts), dim, keepdims=False
-        )
-        pairs = [(i, (i + shift) % parts) for i in range(parts)]
-        total = total + lax.ppermute(sent, axis, pairs).astype(F32)
-    return total.astype(BF16)
+    return [
+        lax.dynamic_index_in_dim(pieces, lax.rem(index + shift, parts), dim, keepdims=False)
+        for shift in range(parts)
+    ]
+
+
+def send(pieces, axis):
+    parts = lax.axis_size(axis)
+    return pieces[:1] + [
+        lax.ppermute(piece, axis, [(i, (i + shift) % parts) for i in range(parts)])
+        for shift, piece in enumerate(pieces)
+        if shift
+    ]
+
+
+def total(pieces):
+    return sum(piece.astype(F32) for piece in pieces).astype(BF16)
 
 
 def as_pieces(block):
@@ -843,16 +1168,14 @@
     total_valid = jnp.sum(valid_count).astype(F32)
     valid_here = jnp.reshape(count - seq_index * rows, (1,))
     gains = jnp.pad(jnp.stack([gain_mix, gain_ffn], 1), ((0, 0), (0, 126)))
-    early = gather_rows(jnp.concatenate([gains, w_query, w_key, w_value, w_out], 1))
+    early = gather_rows(jnp.concatenate([gains, w_query, w_key, w_value], 1))
     fill = ((0, 0), (0, padded - hidden_units))
     late = jnp.concatenate(
-        [jnp.pad(w_gate, fill), jnp.pad(w_up, fill), jnp.pad(w_down, fill)], 1
+        [w_out, jnp.pad(w_gate, fill), jnp.pad(w_up, fill), jnp.pad(w_down, fill)], 1
     )
     late = lax.all_gather(late, everyone, axis=0, tiled=True)
-    gain_one = early[:, 0].astype(F32)[None]
-    gain_two = early[:, 1].astype(F32)[None]
     lead = HEADS * FEAT
-    qkv, normed, flipped = project(inputs, early, gain_one)
+    qkv, normed, flipped, gain_rows = project(inputs, early)
     tie = lax.optimization_barrier
     upper = HEADS // 2
     lower_state = local_state(qkv, 0, upper)
@@ -860,7 +1183,7 @@
     qkv, lower_state = tie((qkv, lower_state))
     upper_init = shifted_sum(local_state(qkv, upper, upper), seq_parts, 1)
     filled = attention_forward(qkv, lower_init, 0, upper)
-    mixed, rest, den, saved = attention_forward(qkv, upper_init, upper, upper, filled)
+    mixed, den, saved = attention_forward(qkv, upper_init, upper, upper, filled)
     (
         result,
         normed_ffn,
@@ -871,11 +1194,10 @@
         resid_back,
         mixed_back,
         squares,
-    ) = feed_forward(valid_here, inputs, targets, mixed, gain_two, early, late, padded)
+    ) = feed_forward(valid_here, inputs, targets, mixed, gain_rows, late, padded)
     local_error = 0.5 * jnp.sum(squares)
     mine, others = jnp.reshape(core, (1,)), jnp.reshape(1 - core, (1,))
     half, out_half, qkv_cols = padded // 2, width // 2, HEADS * HROWS // 2
-    part = HEADS // 4
 
     high = lax.reduce_precision(local_error, 8, 7)
     middle = lax.reduce_precision(local_error - high, 8, 7)
@@ -885,9 +1207,8 @@
     side = jnp.where(column == place, high, 0.0)
     side = jnp.where(column == place + 1, middle, side)
     side = jnp.where(column == place + 2, low, side).astype(BF16)
-    side = (side.astype(F32) + swap_core(side).astype(F32)).astype(BF16)
-
-    nb, back = local_back_state(qkv, mixed_back, mixed, rest, den)
+
+    nb, back = local_back_state(qkv, mixed_back, mixed, den)
     later = shifted_sum(back, seq_parts, -1)
     normed_ffn, nb = tie((normed_ffn, nb))
     gate_up_sent = weight_grad(normed_ffn, both_back, others, padded, half)
@@ -897,61 +1218,39 @@
     normed_ffn, down_sent = tie((normed_ffn, down_sent))
     gate_up = weight_grad(normed_ffn, both_back, mine, padded, half, gate_up_come)
     down_come = swap_core(down_sent)
-    a_one = sum_over(as_pieces(gate_up[:, :half]), "seq", 0)
-    a_two = sum_over(as_pieces(gate_up[:, half:]), "y", 2)
-    mixed, gate_up = tie((mixed, gate_up))
+    a_one = to_send(as_pieces(gate_up[:, :half]), "seq", 0)
+    a_two = to_send(as_pieces(gate_up[:, half:]), "y", 2)
+    mixed, a_one, a_two, later = tie((mixed, a_one, a_two, later))
+    a_one, a_two = send(a_one, "seq"), send(a_two, "y")
     out_sent = weight_grad(mixed, attended_back, others, out_half, out_half)
     out_come = swap_core(out_sent)
     branch_back, out_sent = tie((branch_back, out_sent))
     down = weight_grad(branch_back, hidden, mine, half, half, down_come)
     mixed, down = tie((mixed, down))
     outer = weight_grad(mixed, attended_back, mine, out_half, out_half, out_come)
-    cut = 128 * ((half + out_half + side.shape[1]) // 256)
-    b_one = down[:, :cut]
-    b_two = jnp.concatenate([down[:, cut:], outer, side], 1)
-    nb, b_one, b_two = tie((nb, b_one, b_two))
-    qkv_back = attention_backward(qkv, nb, saved, later, 0, part)
-    nb, a_one, a_two, b_one, b_two = tie((nb, a_one, a_two, b_one, b_two))
-    a_one = sum_over(a_one, "y", 1)
-    a_two = sum_over(a_two, "seq", 0)
-    b_one = sum_over(as_pieces(b_one), "seq", 0)
-    b_two = sum_over(as_pieces(b_two), "y", 2)
-    qkv_back = attention_backward(qkv, nb, saved, later, part, part, qkv_back)
-    qkv_back = attention_backward(qkv, nb, saved, later, 2 * part, part, qkv_back)
-    nb, a_one, a_two, b_one, b_two = tie((nb, a_one, a_two, b_one, b_two))
-    a_own = sum_over(jnp.concatenate([a_one, a_two], 2), "z", 0)
-    b_one = sum_over(b_one, "y", 1)
-    b_two = sum_over(b_two, "seq", 0)
-    qkv_back = attention_backward(qkv, nb, saved, later, 3 * part, part, qkv_back)
-    qkv_back, b_one, b_two = tie((qkv_back, b_one, b_two))
-    b_own = sum_over(jnp.concatenate([b_one, b_two], 2), "z", 0)
+    block = jnp.concatenate([down, outer, side], 1)
+    block, a_one, a_two = tie((block, a_one, a_two))
+    own = w_query.shape[0]
+    z_parts = lax.axis_size("z")
+    one = total(a_one).reshape(z_parts, 2, 2, own, half)
+    two = total(a_two).reshape(seq_parts, z_parts, 2, own, half)
+    qkv_back, gate_up_pair, part = attention_backward(
+        qkv, nb, saved, later, one, two, block, own
+    )
     qkv_sent = weight_grad(normed, qkv_back, others, qkv_cols, qkv_cols, None, NT)
     qkv_come = swap_core(qkv_sent)
     c_all = weight_grad(normed, qkv_back, mine, qkv_cols, qkv_cols, qkv_come, NT)
-    c_cut = 128 * (qkv_cols // 256)
-    c_one = sum_over(as_pieces(c_all[:, :c_cut]), "seq", 0)
-    c_two = sum_over(as_pieces(c_all[:, c_cut:]), "y", 2)
-    qkv_back, c_all = tie((qkv_back, c_all))
-    split = rows // 2
-    early_part = input_gradient(qkv_back, flipped, inputs, resid_back, gain_one, 0, split)
-    early_part, c_one, c_two = tie((early_part, c_one, c_two))
-    c_one = sum_over(c_one, "y", 1)
-    c_two = sum_over(c_two, "seq", 0)
-    input_back = input_gradient(
-        qkv_back, flipped, inputs, resid_back, gain_one, split, split, early_part
-    )
-    input_back, c_one, c_two = tie((input_back, c_one, c_two))
-    c_own = sum_over(jnp.concatenate([c_one, c_two], 2), "z", 0)
-    own = w_query.shape[0]
-    gate_sum, up_sum = whole_rows(a_own.reshape(2, own, -1), core)
-    pair = whole_rows(b_own.reshape(2, own, -1), core)
-    down_sum = jnp.concatenate([pair[0][:, :half], pair[1][:, :half]], 1)
+    gate_sum, up_sum = gate_up_pair[0], gate_up_pair[1]
+    input_back, first_pair, pair = input_gradient(
+        qkv_back, flipped, inputs, resid_back, gain_rows, c_all, part, own
+    )
+    down_sum = jnp.concatenate([pair[0, :, :half], pair[1, :, :half]], 1)
     out_sum = jnp.concatenate(
-        [pair[0][:, half : half + out_half], pair[1][:, half : half + out_half]], 1
-    )
-    errors = pair[0][0, half + out_half : half + out_half + 3 * devices].astype(F32)
+        [pair[0, :, half : half + out_half], pair[1, :, half : half + out_half]], 1
+    )
+    errors = pair[:, 0, half + out_half : half + out_half + 3 * devices].astype(F32)
     loss = 2.0 * jnp.sum(errors) / (width * total_valid)
-    first, second = whole_rows(c_own.reshape(2, own, -1), core)
+    first, second = first_pair[0], first_pair[1]
     qkv_sum = jnp.concatenate([first, second], 1).astype(F32).reshape(own, HEADS, HROWS)
     grad_query = qkv_sum[:, :, :FEAT].reshape(own, lead)
     grad_key = qkv_sum[:, :, FEAT : 2 * FEAT].reshape(own, lead)

time: 571 us -> 522 us (0.914)
  starting transfers between devices: 49.6 us -> 12.7 us
  waiting for transfers between devices: 38 us -> 27.1 us
    ppermute x21 -> x2, starting transfers between devices: 41 us -> 5.68 us  [send(): lax.ppermute(piece, axis, [(i, (i + shift) % parts) for i in range(parts)])]
    ppermute x21 -> x2, waiting for transfers between devices: 26.3 us -> 0.67 us  [send(): lax.ppermute(piece, axis, [(i, (i + shift) % parts) for i in range(parts)])]
    pallas_call x1, Pallas kernels: 57 us -> 32.7 us  [gather_rows(): pl.pallas_call(functools.partial(gather_kernel, (seq_parts, z_parts), spl...]
    all_gather x1, waiting for transfers between devices: 0.01 us -> 23.7 us  [body(): late = lax.all_gather(late, everyone, axis=0, tiled=True)]
    pallas_call x6 -> x2, Pallas kernels: 83.8 us -> 107 us  [the longest x1 62 us: attention_backward(): pl.pallas_call(functools.partial(backward_kernel, sizes, blocks), grid=(H...]
    ppermute x3, waiting for transfers between devices: 10.9 us -> 1.99 us  [shifted_sum(): total = total + lax.ppermute(array, 'seq', pairs)]
    unnamed x45 -> x37, local copies, waits for them, and re-layouts: 9.05 us -> 12.8 us
  transfers between devices with their start and end apart: 33 -> 10, of which waited for: 10 -> 5; matrix products, arithmetic and copies ran while one was open for 6% -> 3% of each run, Pallas kernels for 47% -> 30%
where the time goes in v4:
time: 522 us; the launch traced here: 512 us
  Pallas kernels  407 us (78%)
  waiting for transfers between devices  27.1 us (5%)
  local copies, waits for them, and re-layouts  22.4 us (4%)
  other arithmetic  21.4 us (4%)
  between operations  21.4 us (4%)
  starting transfers between devices  12.7 us (2%)
    pallas_call x1, Pallas kernels, feed_forward(): pl.pallas_call(functools.partial(ffn_kernel, padded), grid_spec=pltpu.Pre...  102 us
    pallas_call x8, Pallas kernels, weight_grad(): pl.pallas_call(functools.partial(weight_grad_kernel, form), grid_spec=plt...  87.4 us
    pallas_call x1, Pallas kernels, attention_backward(): pl.pallas_call(functools.partial(backward_kernel, sizes, blocks), grid=(H...  62 us
    pallas_call x1, Pallas kernels, input_gradient(): pl.pallas_call(functools.partial(input_kernel, sizes), grid=(rows // tile...  44.8 us
    pallas_call x2, Pallas kernels, attention_forward(): pl.pallas_call(functools.partial(forward_kernel, blocks), grid=(count //...  39.7 us
    pallas_call x1, Pallas kernels, gather_rows(): pl.pallas_call(functools.partial(gather_kernel, (seq_parts, z_parts), spl...  32.7 us
    all_gather x1, waiting for transfers between devices, body(): late = lax.all_gather(late, everyone, axis=0, tiled=True)  23.7 us
    pallas_call x2, Pallas kernels, local_state(): pl.pallas_call(functools.partial(state_kernel, cols // CUT), grid=(count...  13.2 us
  transfers between devices with their start and end apart: 10, of which 5 were waited for; matrix products, arithmetic and copies ran while one was open for 3% of the time, Pallas kernels for 30%

profile of v4, /device:TPU:0, one launch (start us, length us, event | category | flops | bytes accessed | tf_op | source)
XLA Modules:
  0.0 512.3 jit_solution(16127888173982107777)
XLA Ops:
  7.2 2.0 fusion.6
  9.2 0.7 pad_maximum_fusion.2
  10.0 1.5 fusion.12.shard_ref
  11.5 32.7 %gather_rows.1 = bf16[2,4,2,2,32,1664]{5,4,3,2,1,0:T(8,128)(2,1)} custom-call(bf16[32,1664]{1,0:T(8,128)(2,1)} %fusion.12.shard_ref), custom_call_target="tpu_custom_call" | custom-call | flops 500000000 | tf_op jit(solution)/shard_map/gather_rows/pallas_call | solution.py:523
  44.2 13.1 %project.1 = (bf16[1536,2048]{1,0:T(8,128)(2,1)}, bf16[1024,2048]{1,0:T(8,128)(2,1)}, bf16[1536,1024]{1,0:T(8,128)(2,1)}, f32[8,1024]{1,0:T(8,128)}) custom-call(bf16[1,2048,1024]{2,1,0:T(8,128)(2,1)} %tokens_ref.5, bf16[1024,1664]{1,0:T(8,128)(2,1)} %bitcast.37), custom_call_target="tpu_custom_call" | custom-call | flops 128849016 | tf_op jit(solution)/shard_map/project/pallas_call | solution.py:567
  57.3 6.6 %key_state.2 = f32[4,3,72,128]{3,2,1,0:T(8,128)} custom-call(bf16[1536,2048]{1,0:T(8,128)(2,1)} %get-tuple-element.60.qkv_ref), custom_call_target="tpu_custom_call" | custom-call | flops 110000000 | tf_op jit(solution)/shard_map/key_state/pallas_call | solution.py:305
  63.9 3.3 collective-permute-start.1
  67.1 6.6 %key_state.3 = f32[4,3,72,128]{3,2,1,0:T(8,128)} custom-call(bf16[1536,2048]{1,0:T(8,128)(2,1)} %get-tuple-element.60.qkv_ref), custom_call_target="tpu_custom_call" | custom-call | flops 110000000 | tf_op jit(solution)/shard_map/key_state/pallas_call | solution.py:305
  73.8 1.5 collective-permute-start
  76.6 1.4 collective-permute-done.1.init_ref
  77.9 0.8 copy-done.6
  78.7 19.8 %attend.2 = (bf16[1024,2048]{1,0:T(8,128)(2,1)}, f32[4,4,2048]{2,1,0:T(4,128)}, bf16[16,8,160,176]{3,2,1,0:T(8,128)(2,1)}) custom-call(bf16[1536,2048]{1,0:T(8,128)(2,1)} %get-tuple-element.60.qkv_ref, f32[4,3,72,128]{3,2,1,0:T(8,128)} %copy-done.6), custom_call_target="tpu_custom_call" | custom-call | flops 360000000 | tf_op jit(solution)/shard_map/attend/pallas_call | solution.py:328
  98.5 0.8 copy-done.7
  99.3 19.9 %attend.3 = (bf16[1024,2048]{1,0:T(8,128)(2,1)}, f32[4,4,2048]{2,1,0:T(4,128)}, bf16[16,8,160,176]{3,2,1,0:T(8,128)(2,1)}) custom-call(bf16[1536,2048]{1,0:T(8,128)(2,1)} %get-tuple-element.60.qkv_ref, f32[4,3,72,128]{3,2,1,0:T(8,128)} %copy-done.7, ...), custom_call_target="tpu_custom_call", output_to_operand_aliasing={{0}: (2, {}), {1}: (3, {}), {2}: (4, {})} | custom-call | flops 360000000 | tf_op jit(solution)/shard_map/attend/pallas_call | solution.py:328
  119.2 23.7 %all-gather.2.cloned.1.call-done.late_ref = bf16[1024,9472]{1,0:T(8,128)(2,1)} async-done(((bf16[32,9472]{1,0:T(8,128)(2,1)}), bf16[1024,9472]{1,0:T(8,128)(2,1)}) %all-gather.2.cloned.1.call-update) | async-done | bytes 19398672 | tf_op jit(solution)/shard_map/all_gather | solution.py:1176
  142.9 101.6 %feed_forward.1 = (bf16[1,2048,1024]{2,1,0:T(8,128)(2,1)}, bf16[1024,2048]{1,0:T(8,128)(2,1)}, bf16[2048,2816]{1,0:T(8,128)(2,1)}, bf16[1024,2048]{1,0:T(8,128)(...) custom-call(s32[1]{0:T(128)} %bitcast.count_ref, ...), custom_call_target="tpu_custom_call" | custom-call | flops 1589137920 | tf_op jit(solution)/shard_map/feed_forward/pallas_call | solution.py:1006
  244.6 12.8 %query_state.1 = (bf16[16,80,2048]{2,1,0:T(8,128)(2,1)}, f32[8,3,72,128]{3,2,1,0:T(8,128)}) custom-call(bf16[1536,2048]{1,0:T(8,128)(2,1)} %get-tuple-element.60.qkv_ref, bf16[1024,2048]{1,0:T(8,128)(2,1)} %get-tuple-element.68.grad_ref, bf16[1024,2048]{1,0:T(8,128)(2,1)} %get-tuple-element.86.mixed_ref.left_ref, f32[4,4,2048]{2,1,0:T(4,128)} %get-tuple-element.69.den_ref), custom_call_target="tpu_custom_call" | custom-call | flops 260000000 | tf_op jit(solution)/shard_map/query_state/pallas_call | solution.py:353
  257.3 18.8 %weight_grad.8 = bf16[1024,2816]{1,0:T(8,128)(2,1)} custom-call(s32[1]{0:T(128)} %bitcast.5.pick_ref, bf16[1024,2048]{1,0:T(8,128)(2,1)} %get-tuple-element.78.left_ref, bf16[2048,5632]{1,0:T(8,128)(2,1)} %get-tuple-element.75.right_ref), custom_call_target="tpu_custom_call" | custom-call | flops 236223200 | tf_op jit(solution)/shard_map/weight_grad/pallas_call | solution.py:1078
  276.4 11.2 %weight_grad.9 = bf16[1024,1408]{1,0:T(8,128)(2,1)} custom-call(s32[1]{0:T(128)} %bitcast.5.pick_ref, bf16[1024,2048]{1,0:T(8,128)(2,1)} %get-tuple-element.83.left_ref, bf16[2048,2816]{1,0:T(8,128)(2,1)} %get-tuple-element.77.right_ref), custom_call_target="tpu_custom_call" | custom-call | flops 118111600 | tf_op jit(solution)/shard_map/weight_grad/pallas_call | solution.py:1078
  287.8 1.3 collective-permute-start.3
  289.1 19.4 %weight_grad.10 = bf16[1024,2816]{1,0:T(8,128)(2,1)} custom-call(s32[1]{0:T(128)} %bitcast.4.pick_ref, bf16[1024,2048]{1,0:T(8,128)(2,1)} %get-tuple-element.78.left_ref, bf16[2048,5632]{1,0:T(8,128)(2,1)} %get-tuple-element.75.right_ref, bf16[1024,2816]{1,0:T(8,128)(2,1)} %collective-permute-done.2.refs_0_), custom_call_target="tpu_custom_call" | custom-call | flops 236223200 | tf_op jit(solution)/shard_map/weight_grad/pallas_call | solution.py:1078
  308.5 3.1 fusion.15
  311.6 1.4 dynamic-slice_bitcast_fusion
  313.0 1.4 dynamic-slice_bitcast_fusion.2
  315.1 5.1 collective-permute-start.6
  320.8 5.5 %weight_grad.11 = bf16[1024,512]{1,0:T(8,128)(2,1)} custom-call(s32[1]{0:T(128)} %bitcast.5.pick_ref, bf16[1024,2048]{1,0:T(8,128)(2,1)} %get-tuple-element.86.mixed_ref.left_ref, bf16[2048,1024]{1,0:T(8,128)(2,1)} %get-tuple-element.82.right_ref), custom_call_target="tpu_custom_call" | custom-call | flops 42949672 | tf_op jit(solution)/shard_map/weight_grad/pallas_call | solution.py:1078
  331.1 1.3 select_convert_fusion
  332.4 11.7 %weight_grad.12 = bf16[1024,1408]{1,0:T(8,128)(2,1)} custom-call(s32[1]{0:T(128)} %bitcast.4.pick_ref, bf16[1024,2048]{1,0:T(8,128)(2,1)} %get-tuple-element.83.left_ref, bf16[2048,2816]{1,0:T(8,128)(2,1)} %get-tuple-element.77.right_ref, bf16[1024,1408]{1,0:T(8,128)(2,1)} %collective-permute-done.4.refs_0_), custom_call_target="tpu_custom_call" | custom-call | flops 118111600 | tf_op jit(solution)/shard_map/weight_grad/pallas_call | solution.py:1078
  344.1 5.9 %weight_grad.13 = bf16[1024,512]{1,0:T(8,128)(2,1)} custom-call(s32[1]{0:T(128)} %bitcast.4.pick_ref, bf16[1024,2048]{1,0:T(8,128)(2,1)} %get-tuple-element.86.mixed_ref.left_ref, bf16[2048,1024]{1,0:T(8,128)(2,1)} %get-tuple-element.82.right_ref, bf16[1024,512]{1,0:T(8,128)(2,1)} %collective-permute-done.5.refs_0_), custom_call_target="tpu_custom_call" | custom-call | flops 42949672 | tf_op jit(solution)/shard_map/weight_grad/pallas_call | solution.py:1078
  350.1 3.3 pad_maximum_fusion
  353.4 0.7 collective-permute-done.7
  354.0 2.8 add_convert_fusion
  356.9 2.8 add_convert_fusion.1
  359.7 62.0 %attend_back.1 = (bf16[1536,2048]{1,0:T(8,128)(2,1)}, bf16[2,32,2816]{2,1,0:T(8,128)(2,1)}, bf16[4,2,32,2048]{3,2,1,0:T(8,128)(2,1)}) custom-call(bf16[1536,2048]{1,0:T(8,128)(2,1)} %get-tuple-element.60.qkv_ref, bf16[16,80,2048]{2,1,0:T(8,128)(2,1)} %get-tuple-element.71.nb_ref, bf16[16,8,160,176]{3,2,1,0:T(8,128)(2,1)} %get-tuple-element.72.saved_ref, ...), custom_call_target="tpu_custom_call" | custom-call | flops 1060000000 | tf_op jit(solution)/shard_map/attend_back/pallas_call | solution.py:394
  421.8 7.4 %weight_grad.14 = bf16[1024,768]{1,0:T(8,128)(2,1)} custom-call(s32[1]{0:T(128)} %bitcast.5.pick_ref, bf16[1024,2048]{1,0:T(8,128)(2,1)} %get-tuple-element.100.left_ref, bf16[1536,2048]{1,0:T(8,128)(2,1)} %get-tuple-element.97.right_ref.back_ref), custom_call_target="tpu_custom_call" | custom-call | flops 64424508 | tf_op jit(solution)/shard_map/weight_grad/pallas_call | solution.py:1078
  430.6 1.1 multiply_reduce_fusion
  432.2 0.7 collective-permute-done.8.refs_0_
  432.9 1.2 copy-done.1
  434.1 7.4 %weight_grad.15 = bf16[1024,768]{1,0:T(8,128)(2,1)} custom-call(s32[1]{0:T(128)} %bitcast.4.pick_ref, bf16[1024,2048]{1,0:T(8,128)(2,1)} %get-tuple-element.100.left_ref, bf16[1536,2048]{1,0:T(8,128)(2,1)} %get-tuple-element.97.right_ref.back_ref, bf16[1024,768]{1,0:T(8,128)(2,1)} %copy-done.1), custom_call_target="tpu_custom_call" | custom-call | flops 64424508 | tf_op jit(solution)/shard_map/weight_grad/pallas_call | solution.py:1078
  441.5 44.8 %input_gradient.1 = (f32[1,2048,1024]{2,1,0:T(8,128)}, bf16[2,32,768]{2,1,0:T(8,128)(2,1)}, bf16[2,32,2048]{2,1,0:T(8,128)(2,1)}) custom-call(bf16[1536,2048]{1,0:T(8,128)(2,1)} %get-tuple-element.97.right_ref.back_ref, bf16[1536,1024]{1,0:T(8,128)(2,1)} %get-tuple-element.98.flipped_ref, bf16[1,2048,1024]{2,1,0:T(8,128)(2,1)} %tokens_ref.5, ...), custom_call_target="tpu_custom_call" | custom-call | flops 257698032 | tf_op jit(solution)/shard_map/input_gradient/pallas_call | solution.py:851
  486.3 1.0 slice_bitcast_fusion.3
  487.3 0.8 slice_bitcast_fusion.5
  488.1 0.8 fusion.17
  489.5 1.3 convert_reduce_fusion
  491.3 0.7 copy.43
  492.0 0.7 copy.44
  492.7 0.8 fusion.9
  495.4 8.4 %copy.49 = f32[1,2048,1024]{2,1,0:T(8,128)} copy(f32[1,2048,1024]{2,1,0:T(8,128)} %get-tuple-element.170) | data formatting | bytes 16777216
  (64 shorter events, 7.4 us)
Async XLA Ops:
  7.2 135.8 %all-gather.2.cloned.1.call-start = ((), (), s32[]{:S(2)}) async-start(), calls=%async_computation | async-start | bytes 20004864 | tf_op jit(solution)/shard_map/all_gather | solution.py:1176
  63.9 11.4 %copy-start.14 = (s32[16]{0:T(128)S(1)}, s32[16]{0:T(128)}, u32[]{:S(2)}) copy-start(s32[16]{0:T(128)} %param.14) | copy-start | bytes 196
  63.9 14.1 %collective-permute-start.1 = (f32[4,3,72,128]{3,2,1,0:T(8,128)}, f32[4,3,72,128]{3,2,1,0:T(8,128)S(1)}, u32[]{:S(2)}, u32[]{:S(2)}) collective-permute-start(f32[4,3,72,128]{3,2,1,0:T(8,128)} %key_state.2), channel_id=1, source_target_pairs={{0,16},{1,17},{2,18},{3,19},{4,20},{5,21},{6,22},{7,23},{8,24},{9,... | collective-permute-start | bytes 1327112 | tf_op jit(solution)/shard_map/ppermute | solution.py:1139
  73.8 24.8 %collective-permute-start = (f32[4,3,72,128]{3,2,1,0:T(8,128)}, f32[4,3,72,128]{3,2,1,0:T(8,128)S(1)}, u32[]{:S(2)}, u32[]{:S(2)}) collective-permute-start(f32[4,3,72,128]{3,2,1,0:T(8,128)} %key_state.3), channel_id=1, source_target_pairs={{0,16},{1,17},{2,18},{3,19},{4,20},{5,21},{6,22},{7,23},{8,24},{9,... | collective-permute-start | bytes 1327112 | tf_op jit(solution)/shard_map/ppermute | solution.py:1139
  77.9 0.8 copy-start.6
  98.5 0.8 copy-start.7
  276.1 13.0 %collective-permute-start.2 = (bf16[1024,2816]{1,0:T(8,128)(2,1)}, bf16[1024,2816]{1,0:T(8,128)(2,1)}, u32[]{:S(2)}, u32[]{:S(2)}) collective-permute-start(bf16[1024,2816]{1,0:T(8,128)(2,1)} %weight_grad.8), channel_id=1, source_target_pairs={{0,1},{1,0},{2,3},{3,2},{4,5},{5,4},{6,7},{7,6},{8,9},{9,8},{10,11... | collective-permute-start | bytes 17301512 | tf_op jit(solution)/shard_map/ppermute | solution.py:1094
  287.6 44.8 %collective-permute-start.4 = (bf16[1024,1408]{1,0:T(8,128)(2,1)}, bf16[1024,1408]{1,0:T(8,128)(2,1)}, u32[]{:S(2)}, u32[]{:S(2)}) collective-permute-start(bf16[1024,1408]{1,0:T(8,128)(2,1)} %weight_grad.9), channel_id=1, source_target_pairs={{0,1},{1,0},{2,3},{3,2},{4,5},{5,4},{6,7},{7,6},{8,9},{9,8},{10,11... | collective-permute-start | bytes 8650760 | tf_op jit(solution)/shard_map/ppermute | solution.py:1094
  287.8 27.3 %collective-permute-start.3 = (f32[8,3,72,128]{3,2,1,0:T(8,128)}, f32[8,3,72,128]{3,2,1,0:T(8,128)S(1)}, u32[]{:S(2)}, u32[]{:S(2)}) collective-permute-start(f32[8,3,72,128]{3,2,1,0:T(8,128)} %get-tuple-element.79), channel_id=1, source_target_pairs={{16,0},{17,1},{18,2},{19,3},{20,4},{21,5},{22,6},{23,7},{24,8},{25... | collective-permute-start | bytes 2654216 | tf_op jit(solution)/shard_map/ppermute | solution.py:1139
  315.1 11.2 %copy-start.2 = (f32[8,3,72,128]{3,2,1,0:T(8,128)}, f32[8,3,72,128]{3,2,1,0:T(8,128)S(1)}, u32[]{:S(2)}) copy-start(f32[8,3,72,128]{3,2,1,0:T(8,128)S(1)} %collective-permute-done.3.init_ref) | copy-start | bytes 2654212
  315.1 38.3 %collective-permute-start.6 = (bf16[4,2,64,1408]{3,2,1,0:T(8,128)(2,1)}, bf16[4,2,64,1408]{3,2,1,0:T(8,128)(2,1)}, u32[]{:S(2)}, u32[]{:S(2)}) collective-permute-start(bf16[4,2,64,1408]{3,2,1,0:T(8,128)(2,1)} %get-tuple-element.89), channel_id=1, source_target_pairs={{0,16},{16,0},{1,17},{17,1},{2,18},{18,2},{3,19},{19,3},{4,20},{20... | collective-permute-start | bytes 4325384 | tf_op jit(solution)/shard_map/ppermute | solution.py:1109
  320.2 33.9 %collective-permute-start.7 = (bf16[2,4,64,1408]{3,2,1,0:T(8,128)(2,1)}, bf16[2,4,64,1408]{3,2,1,0:T(8,128)(2,1)}, u32[]{:S(2)}, u32[]{:S(2)}) collective-permute-start(bf16[2,4,64,1408]{3,2,1,0:T(8,128)(2,1)} %get-tuple-element.91), channel_id=1, source_target_pairs={{0,2},{2,0},{1,3},{3,1},{4,6},{6,4},{5,7},{7,5},{8,10},{10,8},{9,1... | collective-permute-start | bytes 4325384 | tf_op jit(solution)/shard_map/ppermute | solution.py:1109
  320.7 5.6 %copy-start.12 = (f32[1,1024]{1,0:T(1,128)S(1)}, f32[1,1024]{1,0:T(1,128)}, u32[]{:S(2)}) copy-start(f32[1,1024]{1,0:T(1,128)} %get-tuple-element.87) | copy-start | bytes 12292
  326.3 17.9 %collective-permute-start.5 = (bf16[1024,512]{1,0:T(8,128)(2,1)}, bf16[1024,512]{1,0:T(8,128)(2,1)}, u32[]{:S(2)}, u32[]{:S(2)}) collective-permute-start(bf16[1024,512]{1,0:T(8,128)(2,1)} %weight_grad.11), channel_id=1, source_target_pairs={{0,1},{1,0},{2,3},{3,2},{4,5},{5,4},{6,7},{7,6},{8,9},{9,8},{10,11... | collective-permute-start | bytes 3145736 | tf_op jit(solution)/shard_map/ppermute | solution.py:1094
  344.1 5.9 %copy-start = (bf16[1024,1408]{1,0:T(8,128)(2,1)S(1)}, bf16[1024,1408]{1,0:T(8,128)(2,1)}, u32[]{:S(2)}) copy-start(bf16[1024,1408]{1,0:T(8,128)(2,1)} %weight_grad.12) | copy-start | bytes 8650756
  421.7 7.9 %copy-start.10 = (bf16[32,256]{1,0:T(8,128)(2,1)S(1)}, bf16[32,256]{1,0:T(8,128)(2,1)}, u32[]{:S(2)}) copy-start(bf16[32,256]{1,0:T(8,128)(2,1)} %param.16) | copy-start | bytes 49156
  421.8 8.0 %copy-start.11 = (bf16[32,256]{1,0:T(8,128)(2,1)S(1)}, bf16[32,256]{1,0:T(8,128)(2,1)}, u32[]{:S(2)}) copy-start(bf16[32,256]{1,0:T(8,128)(2,1)} %param.17) | copy-start | bytes 49156
  421.8 8.8 %copy-start.8 = (bf16[2,32,2816]{2,1,0:T(8,128)(2,1)S(1)}, bf16[2,32,2816]{2,1,0:T(8,128)(2,1)}, u32[]{:S(2)}) copy-start(bf16[2,32,2816]{2,1,0:T(8,128)(2,1)} %get-tuple-element.105) | copy-start | bytes 1081348
  421.8 8.8 %copy-start.3 = (bf16[32,2752]{1,0:T(8,128)(2,1)S(1)}, bf16[32,2752]{1,0:T(8,128)(2,1)}, u32[]{:S(2)}) copy-start(bf16[32,2752]{1,0:T(8,128)(2,1)} %param.22) | copy-start | bytes 528388
  421.8 8.8 %copy-start.4 = (bf16[32,2752]{1,0:T(8,128)(2,1)S(1)}, bf16[32,2752]{1,0:T(8,128)(2,1)}, u32[]{:S(2)}) copy-start(bf16[32,2752]{1,0:T(8,128)(2,1)} %param.21) | copy-start | bytes 528388
  421.8 9.9 %copy-start.15 = (bf16[32]{0:T(256)(128)(2,1)S(1)}, bf16[32]{0:T(256)(128)(2,1)}, u32[]{:S(2)}) copy-start(bf16[32]{0:T(256)(128)(2,1)} %param.20) | copy-start | bytes 196
  429.2 3.7 collective-permute-start.8
  432.9 1.2 copy-start.1
  486.3 4.9 copy-start.9
  486.3 8.6 %copy-start.13 = (bf16[32]{0:T(256)(128)(2,1)S(1)}, bf16[32]{0:T(256)(128)(2,1)}, u32[]{:S(2)}) copy-start(bf16[32]{0:T(256)(128)(2,1)} %param.15) | copy-start | bytes 196
  491.2 12.7 %copy-start.5 = (f32[32,1024]{1,0:T(8,128)}, f32[32,1024]{1,0:T(8,128)S(1)}, u32[]{:S(2)}) copy-start(f32[32,1024]{1,0:T(8,128)S(1)} %reshape.81) | copy-start | bytes 393220
Sparse Core Ops, SparseCore 0:
  11.4 131.4 all-gather.1

commit v5 on v4

--- a/solution.py
+++ b/solution.py
@@ -895,6 +895,157 @@
         block.reshape(sizes + (2, 2, own, cols)),
         part,
     )
+
+
+def last_kernel(
+    sizes,
+    normed_ref,
+    back_ref,
+    flipped_ref,
+    tokens_ref,
+    resid_ref,
+    gain_ref,
+    part_ref,
+    out_ref,
+    block_out,
+    part_out,
+    sent,
+    come,
+    block,
+    part_z_in,
+    part_sum,
+    part_swapped,
+    half_send,
+    half_recv,
+    z_send,
+    z_recv,
+    core_send,
+    core_recv,
+    *refs,
+):
+    step = pl.program_id(0)
+    c = positions()[3]
+    by_seq, by_z, by_y, by_core = neighbours(sizes)
+    sums = RowSums(sizes, block, refs, block_out)
+    part_along = along_z(sizes, part_ref, part_z_in, (z_send, z_recv))
+    part_across = remote(
+        part_sum.at[1 - c], part_swapped, (core_send, core_recv), 0, by_core
+    )
+    half = remote(sent, come, (half_send, half_recv), 0, by_core)
+    cols = sent.shape[1]
+    each = sent.shape[0] // sizes[0]
+    tile, width = tokens_ref.shape[1:]
+
+    def gradient(s, which):
+        rows = pl.ds(pl.multiple_of(which * cols, 16), cols)
+        return dot(normed_ref[s * each : (s + 1) * each, :], back_ref[rows, :], NT)
+
+    @pl.when(step == 0)
+    def _():
+        greet(by_seq + by_z + [by_y, by_core])
+        for copy in part_along:
+            copy.start()
+        for s in range(sizes[0]):
+            sent[s * each : (s + 1) * each, :] = gradient(s, 1 - c).astype(BF16)
+        half.start()
+
+    @pl.when(step == 2)
+    def _():
+        half.wait_recv()
+        for s in range(sizes[0]):
+            total = gradient(s, c) + come[s * each : (s + 1) * each, :].astype(F32)
+            block[s] = total.astype(BF16).reshape(block.shape[1:])
+        sums.start()
+
+    @pl.when((step == 1) | (step > 2))
+    def _():
+        at = pl.multiple_of(step // 3 * (step - 2) * tile, 128)
+        tokens = tokens_ref[0].astype(F32)
+        scale = lax.rsqrt(
+            jnp.sum(tokens * tokens, -1, keepdims=True) * (1.0 / width) + epsilon
+        )
+        unit = tokens * scale
+        normed_back = dot(back_ref[:, pl.ds(at, tile)], flipped_ref[...], TN)
+        scaled = normed_back * gain_ref[0:1]
+        middle = jnp.sum(scaled * unit, -1, keepdims=True) * (1.0 / width)
+        out_ref[0] = resid_ref[...] + scale * (scaled - unit * middle)
+
+    @pl.when(step == 4)
+    def _():
+        sums.second()
+
+    @pl.when(step == 5)
+    def _():
+        sums.third()
+        sum_z(part_along, part_ref, part_z_in, part_sum)
+        part_across.start()
+        part_out[c] = part_sum[c]
+        sums.fourth()
+        part_across.wait_recv()
+        part_out[1 - c] = part_swapped[...]
+        sums.finish()
+        for copy in part_along:
+            copy.wait_send()
+        part_across.wait_send()
+        half.wait_send()
+
+
+def last_gradients(normed, back, flipped, tokens, resid_back, gain, part, own):
+    rows, width = tokens.shape[1:]
+    tile = rows // 4
+    sizes = lax.axis_size("seq"), lax.axis_size("z")
+    cols, part_cols = HEADS * HROWS // 2, part.shape[-1]
+    cut = 128 * (cols // 256)
+    buffers, sems = row_sum_scratch(sizes, own, cut, cols - cut)
+    here = pl.BlockSpec(memory_space=pltpu.VMEM)
+
+    def place(i):
+        return i // 3 * (i - 2)
+
+    def low(*shape):
+        return pltpu.VMEM(shape, BF16)
+
+    one, many = pltpu.SemaphoreType.DMA((1,)), pltpu.SemaphoreType.DMA((sizes[1] - 1,))
+    return pl.pallas_call(
+        functools.partial(last_kernel, sizes),
+        grid=(6,),
+        in_specs=[
+            here,
+            here,
+            here,
+            pl.BlockSpec((1, tile, width), lambda i: (0, place(i), 0)),
+            pl.BlockSpec((tile, width), lambda i: (place(i), 0)),
+            pl.BlockSpec((8, width), lambda i: (0, 0)),
+            here,
+        ],
+        out_specs=[pl.BlockSpec((1, tile, width), lambda i: (0, place(i), 0)), here, here],
+        out_shape=[
+            jax.ShapeDtypeStruct((1, rows, width), F32),
+            jax.ShapeDtypeStruct((2, own, cols), BF16),
+            jax.ShapeDtypeStruct((2, own, part_cols), BF16),
+        ],
+        scratch_shapes=[
+            low(width, cols),
+            low(width, cols),
+            low(*sizes, 2, 2, own, cols),
+            low(sizes[1] - 1, 2, own, part_cols),
+            low(2, own, part_cols),
+            low(own, part_cols),
+            one,
+            one,
+            many,
+            many,
+            one,
+            one,
+        ]
+        + buffers
+        + sems,
+        compiler_params=pltpu.CompilerParams(
+            collective_id=3, has_side_effects=True, vmem_limit_bytes=56 * 1024 * 1024
+        ),
+        cost_estimate=cost(8 * HEADS * HROWS * rows * width),
+        name="last_gradients",
+    )(normed, back, flipped, tokens, resid_back, gain, part)
 
 
 def ffn_kernel(
@@ -1237,13 +1388,18 @@
     qkv_back, gate_up_pair, part = attention_backward(
         qkv, nb, saved, later, one, two, block, own
     )
-    qkv_sent = weight_grad(normed, qkv_back, others, qkv_cols, qkv_cols, None, NT)
-    qkv_come = swap_core(qkv_sent)
-    c_all = weight_grad(normed, qkv_back, mine, qkv_cols, qkv_cols, qkv_come, NT)
     gate_sum, up_sum = gate_up_pair[0], gate_up_pair[1]
-    input_back, first_pair, pair = input_gradient(
-        qkv_back, flipped, inputs, resid_back, gain_rows, c_all, part, own
-    )
+    if own % 16 == 0 and rows % 512 == 0:
+        input_back, first_pair, pair = last_gradients(
+            normed, qkv_back, flipped, inputs, resid_back, gain_rows, part, own
+        )
+    else:
+        qkv_sent = weight_grad(normed, qkv_back, others, qkv_cols, qkv_cols, None, NT)
+        qkv_come = swap_core(qkv_sent)
+        c_all = weight_grad(normed, qkv_back, mine, qkv_cols, qkv_cols, qkv_come, NT)
+        input_back, first_pair, pair = input_gradient(
+            qkv_back, flipped, inputs, resid_back, gain_rows, c_all, part, own
+        )
     down_sum = jnp.concatenate([pair[0, :, :half], pair[1, :, :half]], 1)
     out_sum = jnp.concatenate(
         [pair[0, :, half : half + out_half], pair[1, :, half : half + out_half]], 1

time: 522 us -> 505 us (0.967); the launches traced: 512 us -> 501 us
  Pallas kernels: 407 us -> 399 us
    pallas_call x8 -> x6, Pallas kernels: 87.4 us -> 72.8 us  [weight_grad(): pl.pallas_call(functools.partial(weight_grad_kernel, form), grid_spec=plt...]
    pallas_call x1, Pallas kernels: 44.8 us -> 50.8 us  [last_gradients(): pl.pallas_call(functools.partial(last_kernel, sizes), grid=(6,), in_specs...]
    unnamed x37 -> x35, local copies, waits for them, and re-layouts: 12.8 us -> 11.7 us
  transfers between devices with their start and end apart: 10 -> 9, of which waited for: 5 -> 3; matrix products, arithmetic and copies ran while one was open for 3% -> 3% of each run, Pallas kernels for 30% -> 30%
where the time goes in v5:
time: 505 us; the launch traced here: 501 us
  Pallas kernels  399 us (79%)
  waiting for transfers between devices  25.6 us (5%)
  other arithmetic  21.4 us (4%)
  local copies, waits for them, and re-layouts  21.3 us (4%)
  between operations  21.1 us (4%)
  starting transfers between devices  12.4 us (2%)
    pallas_call x1, Pallas kernels, feed_forward(): pl.pallas_call(functools.partial(ffn_kernel, padded), grid_spec=pltpu.Pre...  102 us
    pallas_call x6, Pallas kernels, weight_grad(): pl.pallas_call(functools.partial(weight_grad_kernel, form), grid_spec=plt...  72.8 us
    pallas_call x1, Pallas kernels, attention_backward(): pl.pallas_call(functools.partial(backward_kernel, sizes, blocks), grid=(H...  62.8 us
    pallas_call x1, Pallas kernels, last_gradients(): pl.pallas_call(functools.partial(last_kernel, sizes), grid=(6,), in_specs...  50.8 us
    pallas_call x2, Pallas kernels, attention_forward(): pl.pallas_call(functools.partial(forward_kernel, blocks), grid=(count //...  39.7 us
    pallas_call x1, Pallas kernels, gather_rows(): pl.pallas_call(functools.partial(gather_kernel, (seq_parts, z_parts), spl...  32.7 us
    all_gather x1, waiting for transfers between devices, body(): late = lax.all_gather(late, everyone, axis=0, tiled=True)  23.8 us
    pallas_call x2, Pallas kernels, local_state(): pl.pallas_call(functools.partial(state_kernel, cols // CUT), grid=(count...  13.2 us
  transfers between devices with their start and end apart: 9, of which 3 were waited for; matrix products, arithmetic and copies ran while one was open for 3% of the time, Pallas kernels for 30%

profile of v5, /device:TPU:0, one launch (start us, length us, event | category | flops | bytes accessed | tf_op | source)
XLA Modules:
  0.0 501.2 jit_solution(15368548637032695105)
XLA Ops:
  7.2 2.0 fusion.6
  9.2 0.7 pad_maximum_fusion.2
  10.0 1.5 fusion.12.shard_ref
  11.5 32.7 %gather_rows.1 = bf16[2,4,2,2,32,1664]{5,4,3,2,1,0:T(8,128)(2,1)} custom-call(bf16[32,1664]{1,0:T(8,128)(2,1)} %fusion.12.shard_ref), custom_call_target="tpu_custom_call" | custom-call | flops 500000000 | tf_op jit(solution)/shard_map/gather_rows/pallas_call | solution.py:523
  44.2 13.1 %project.1 = (bf16[1536,2048]{1,0:T(8,128)(2,1)}, bf16[1024,2048]{1,0:T(8,128)(2,1)}, bf16[1536,1024]{1,0:T(8,128)(2,1)}, f32[8,1024]{1,0:T(8,128)}) custom-call(bf16[1,2048,1024]{2,1,0:T(8,128)(2,1)} %tokens_ref.5, bf16[1024,1664]{1,0:T(8,128)(2,1)} %bitcast.36), custom_call_target="tpu_custom_call" | custom-call | flops 128849016 | tf_op jit(solution)/shard_map/project/pallas_call | solution.py:567
  57.3 6.6 %key_state.2 = f32[4,3,72,128]{3,2,1,0:T(8,128)} custom-call(bf16[1536,2048]{1,0:T(8,128)(2,1)} %get-tuple-element.60.qkv_ref), custom_call_target="tpu_custom_call" | custom-call | flops 110000000 | tf_op jit(solution)/shard_map/key_state/pallas_call | solution.py:305
  63.8 3.3 collective-permute-start.1
  67.1 6.6 %key_state.3 = f32[4,3,72,128]{3,2,1,0:T(8,128)} custom-call(bf16[1536,2048]{1,0:T(8,128)(2,1)} %get-tuple-element.60.qkv_ref), custom_call_target="tpu_custom_call" | custom-call | flops 110000000 | tf_op jit(solution)/shard_map/key_state/pallas_call | solution.py:305
  73.7 1.5 collective-permute-start
  75.3 0.6 fusion.14
  76.5 1.4 collective-permute-done.1.init_ref
  77.9 0.8 copy-done.5
  78.7 19.9 %attend.2 = (bf16[1024,2048]{1,0:T(8,128)(2,1)}, f32[4,4,2048]{2,1,0:T(4,128)}, bf16[16,8,160,176]{3,2,1,0:T(8,128)(2,1)}) custom-call(bf16[1536,2048]{1,0:T(8,128)(2,1)} %get-tuple-element.60.qkv_ref, f32[4,3,72,128]{3,2,1,0:T(8,128)} %copy-done.5), custom_call_target="tpu_custom_call" | custom-call | flops 360000000 | tf_op jit(solution)/shard_map/attend/pallas_call | solution.py:328
  98.6 0.8 copy-done.6
  99.3 19.9 %attend.3 = (bf16[1024,2048]{1,0:T(8,128)(2,1)}, f32[4,4,2048]{2,1,0:T(4,128)}, bf16[16,8,160,176]{3,2,1,0:T(8,128)(2,1)}) custom-call(bf16[1536,2048]{1,0:T(8,128)(2,1)} %get-tuple-element.60.qkv_ref, f32[4,3,72,128]{3,2,1,0:T(8,128)} %copy-done.6, ...), custom_call_target="tpu_custom_call", output_to_operand_aliasing={{0}: (2, {}), {1}: (3, {}), {2}: (4, {})} | custom-call | flops 360000000 | tf_op jit(solution)/shard_map/attend/pallas_call | solution.py:328
  119.2 23.8 %all-gather.2.cloned.1.call-done.late_ref = bf16[1024,9472]{1,0:T(8,128)(2,1)} async-done(((bf16[32,9472]{1,0:T(8,128)(2,1)}), bf16[1024,9472]{1,0:T(8,128)(2,1)}) %all-gather.2.cloned.1.call-update) | async-done | bytes 19398672 | tf_op jit(solution)/shard_map/all_gather | solution.py:1327
  143.0 101.6 %feed_forward.1 = (bf16[1,2048,1024]{2,1,0:T(8,128)(2,1)}, bf16[1024,2048]{1,0:T(8,128)(2,1)}, bf16[2048,2816]{1,0:T(8,128)(2,1)}, bf16[1024,2048]{1,0:T(8,128)(...) custom-call(s32[1]{0:T(128)} %bitcast.count_ref, ...), custom_call_target="tpu_custom_call" | custom-call | flops 1589137920 | tf_op jit(solution)/shard_map/feed_forward/pallas_call | solution.py:1157
  244.6 12.8 %query_state.1 = (bf16[16,80,2048]{2,1,0:T(8,128)(2,1)}, f32[8,3,72,128]{3,2,1,0:T(8,128)}) custom-call(bf16[1536,2048]{1,0:T(8,128)(2,1)} %get-tuple-element.60.qkv_ref, bf16[1024,2048]{1,0:T(8,128)(2,1)} %get-tuple-element.69.grad_ref, bf16[1024,2048]{1,0:T(8,128)(2,1)} %get-tuple-element.87.mixed_ref.left_ref, f32[4,4,2048]{2,1,0:T(4,128)} %get-tuple-element.70.den_ref), custom_call_target="tpu_custom_call" | custom-call | flops 260000000 | tf_op jit(solution)/shard_map/query_state/pallas_call | solution.py:353
  257.4 19.0 %weight_grad.6 = bf16[1024,2816]{1,0:T(8,128)(2,1)} custom-call(s32[1]{0:T(128)} %bitcast.5.pick_ref, bf16[1024,2048]{1,0:T(8,128)(2,1)} %get-tuple-element.79.left_ref, bf16[2048,5632]{1,0:T(8,128)(2,1)} %get-tuple-element.76.right_ref), custom_call_target="tpu_custom_call" | custom-call | flops 236223200 | tf_op jit(solution)/shard_map/weight_grad/pallas_call | solution.py:1229
  276.5 11.2 %weight_grad.7 = bf16[1024,1408]{1,0:T(8,128)(2,1)} custom-call(s32[1]{0:T(128)} %bitcast.5.pick_ref, bf16[1024,2048]{1,0:T(8,128)(2,1)} %get-tuple-element.84.left_ref, bf16[2048,2816]{1,0:T(8,128)(2,1)} %get-tuple-element.78.right_ref), custom_call_target="tpu_custom_call" | custom-call | flops 118111600 | tf_op jit(solution)/shard_map/weight_grad/pallas_call | solution.py:1229
  288.1 1.3 collective-permute-start.3
  289.4 19.3 %weight_grad.8 = bf16[1024,2816]{1,0:T(8,128)(2,1)} custom-call(s32[1]{0:T(128)} %bitcast.4.pick_ref, bf16[1024,2048]{1,0:T(8,128)(2,1)} %get-tuple-element.79.left_ref, bf16[2048,5632]{1,0:T(8,128)(2,1)} %get-tuple-element.76.right_ref, bf16[1024,2816]{1,0:T(8,128)(2,1)} %collective-permute-done.2.refs_0_), custom_call_target="tpu_custom_call" | custom-call | flops 236223200 | tf_op jit(solution)/shard_map/weight_grad/pallas_call | solution.py:1229
  308.8 3.1 fusion.15
  311.9 1.4 dynamic-slice_bitcast_fusion
  313.3 1.4 dynamic-slice_bitcast_fusion.2
  315.2 5.2 %collective-permute-start.6 = (bf16[4,2,64,1408]{3,2,1,0:T(8,128)(2,1)}, bf16[4,2,64,1408]{3,2,1,0:T(8,128)(2,1)}, u32[]{:S(2)}, u32[]{:S(2)}) collective-permute-start(bf16[4,2,64,1408]{3,2,1,0:T(8,128)(2,1)} %get-tuple-element.90), channel_id=1, source_target_pairs={{0,16},{16,0},{1,17},{17,1},{2,18},{18,2},{3,19},{19,3},{4,20},{20... | collective-permute-start | bytes 4325384 | tf_op jit(solution)/shard_map/ppermute | solution.py:1260
  320.4 0.6 collective-permute-start.7
  321.0 5.6 %weight_grad.9 = bf16[1024,512]{1,0:T(8,128)(2,1)} custom-call(s32[1]{0:T(128)} %bitcast.5.pick_ref, bf16[1024,2048]{1,0:T(8,128)(2,1)} %get-tuple-element.87.mixed_ref.left_ref, bf16[2048,1024]{1,0:T(8,128)(2,1)} %get-tuple-element.83.right_ref), custom_call_target="tpu_custom_call" | custom-call | flops 42949672 | tf_op jit(solution)/shard_map/weight_grad/pallas_call | solution.py:1229
  327.5 0.6 reduce_sum.82
  331.6 0.6 compare_select_fusion
  332.2 1.3 select_convert_fusion
  333.6 11.8 %weight_grad.10 = bf16[1024,1408]{1,0:T(8,128)(2,1)} custom-call(s32[1]{0:T(128)} %bitcast.4.pick_ref, bf16[1024,2048]{1,0:T(8,128)(2,1)} %get-tuple-element.84.left_ref, bf16[2048,2816]{1,0:T(8,128)(2,1)} %get-tuple-element.78.right_ref, bf16[1024,1408]{1,0:T(8,128)(2,1)} %collective-permute-done.4.refs_0_), custom_call_target="tpu_custom_call" | custom-call | flops 118111600 | tf_op jit(solution)/shard_map/weight_grad/pallas_call | solution.py:1229
  345.3 5.9 %weight_grad.11 = bf16[1024,512]{1,0:T(8,128)(2,1)} custom-call(s32[1]{0:T(128)} %bitcast.4.pick_ref, bf16[1024,2048]{1,0:T(8,128)(2,1)} %get-tuple-element.87.mixed_ref.left_ref, bf16[2048,1024]{1,0:T(8,128)(2,1)} %get-tuple-element.83.right_ref, bf16[1024,512]{1,0:T(8,128)(2,1)} %collective-permute-done.5.refs_0_), custom_call_target="tpu_custom_call" | custom-call | flops 42949672 | tf_op jit(solution)/shard_map/weight_grad/pallas_call | solution.py:1229
  351.2 3.3 pad_maximum_fusion
  354.5 2.8 add_convert_fusion
  357.4 2.8 add_convert_fusion.1
  360.2 62.8 %attend_back.1 = (bf16[1536,2048]{1,0:T(8,128)(2,1)}, bf16[2,32,2816]{2,1,0:T(8,128)(2,1)}, bf16[4,2,32,2048]{3,2,1,0:T(8,128)(2,1)}) custom-call(bf16[1536,2048]{1,0:T(8,128)(2,1)} %get-tuple-element.60.qkv_ref, bf16[16,80,2048]{2,1,0:T(8,128)(2,1)} %get-tuple-element.72.nb_ref, bf16[16,8,160,176]{3,2,1,0:T(8,128)(2,1)} %get-tuple-element.73.saved_ref, ...), custom_call_target="tpu_custom_call" | custom-call | flops 1060000000 | tf_op jit(solution)/shard_map/attend_back/pallas_call | solution.py:394
  423.0 50.8 %last_gradients.1 = (f32[1,2048,1024]{2,1,0:T(8,128)}, bf16[2,32,768]{2,1,0:T(8,128)(2,1)}, bf16[2,32,2048]{2,1,0:T(8,128)(2,1)}) custom-call(bf16[1024,2048]{1,0:T(8,128)(2,1)} %get-tuple-element.67.normed_ref, bf16[1536,2048]{1,0:T(8,128)(2,1)} %get-tuple-element.98.back_ref, bf16[1536,1024]{1,0:T(8,128)(2,1)} %get-tuple-element.99.flipped_ref, ...), custom_call_target="tpu_custom_call" | custom-call | flops 515396064 | tf_op jit(solution)/shard_map/last_gradients/pallas_call | solution.py:1009
  473.9 1.0 slice_bitcast_fusion.3
  474.9 0.8 slice_bitcast_fusion.5
  475.7 0.8 fusion.17
  477.1 1.3 convert_reduce_fusion
  479.0 0.7 copy.43
  479.7 0.7 copy.44
  480.4 0.8 fusion.9
  481.1 1.1 multiply_reduce_fusion
  482.7 0.7 maximum_convert_fusion.1
  484.6 8.4 %copy.49 = f32[1,2048,1024]{2,1,0:T(8,128)} copy(f32[1,2048,1024]{2,1,0:T(8,128)} %get-tuple-element.170) | data formatting | bytes 16777216
  (58 shorter events, 3.7 us)
Async XLA Ops:
  7.2 135.8 %all-gather.2.cloned.1.call-start = ((), (), s32[]{:S(2)}) async-start(), calls=%async_computation | async-start | bytes 20004864 | tf_op jit(solution)/shard_map/all_gather | solution.py:1327
  63.8 11.4 %copy-start.13 = (s32[16]{0:T(128)S(1)}, s32[16]{0:T(128)}, u32[]{:S(2)}) copy-start(s32[16]{0:T(128)} %param.14) | copy-start | bytes 196
  63.8 14.1 %collective-permute-start.1 = (f32[4,3,72,128]{3,2,1,0:T(8,128)}, f32[4,3,72,128]{3,2,1,0:T(8,128)S(1)}, u32[]{:S(2)}, u32[]{:S(2)}) collective-permute-start(f32[4,3,72,128]{3,2,1,0:T(8,128)} %key_state.2), channel_id=1, source_target_pairs={{0,16},{1,17},{2,18},{3,19},{4,20},{5,21},{6,22},{7,23},{8,24},{9,... | collective-permute-start | bytes 1327112 | tf_op jit(solution)/shard_map/ppermute | solution.py:1290
  73.7 24.8 %collective-permute-start = (f32[4,3,72,128]{3,2,1,0:T(8,128)}, f32[4,3,72,128]{3,2,1,0:T(8,128)S(1)}, u32[]{:S(2)}, u32[]{:S(2)}) collective-permute-start(f32[4,3,72,128]{3,2,1,0:T(8,128)} %key_state.3), channel_id=1, source_target_pairs={{0,16},{1,17},{2,18},{3,19},{4,20},{5,21},{6,22},{7,23},{8,24},{9,... | collective-permute-start | bytes 1327112 | tf_op jit(solution)/shard_map/ppermute | solution.py:1290
  77.9 0.8 copy-start.5
  98.5 0.8 copy-start.6
  276.4 13.1 %collective-permute-start.2 = (bf16[1024,2816]{1,0:T(8,128)(2,1)}, bf16[1024,2816]{1,0:T(8,128)(2,1)}, u32[]{:S(2)}, u32[]{:S(2)}) collective-permute-start(bf16[1024,2816]{1,0:T(8,128)(2,1)} %weight_grad.6), channel_id=1, source_target_pairs={{0,1},{1,0},{2,3},{3,2},{4,5},{5,4},{6,7},{7,6},{8,9},{9,8},{10,11... | collective-permute-start | bytes 17301512 | tf_op jit(solution)/shard_map/ppermute | solution.py:1245
  287.8 45.8 %collective-permute-start.4 = (bf16[1024,1408]{1,0:T(8,128)(2,1)}, bf16[1024,1408]{1,0:T(8,128)(2,1)}, u32[]{:S(2)}, u32[]{:S(2)}) collective-permute-start(bf16[1024,1408]{1,0:T(8,128)(2,1)} %weight_grad.7), channel_id=1, source_target_pairs={{0,1},{1,0},{2,3},{3,2},{4,5},{5,4},{6,7},{7,6},{8,9},{9,8},{10,11... | collective-permute-start | bytes 8650760 | tf_op jit(solution)/shard_map/ppermute | solution.py:1245
  288.1 27.0 %collective-permute-start.3 = (f32[8,3,72,128]{3,2,1,0:T(8,128)}, f32[8,3,72,128]{3,2,1,0:T(8,128)S(1)}, u32[]{:S(2)}, u32[]{:S(2)}) collective-permute-start(f32[8,3,72,128]{3,2,1,0:T(8,128)} %get-tuple-element.80), channel_id=1, source_target_pairs={{16,0},{17,1},{18,2},{19,3},{20,4},{21,5},{22,6},{23,7},{24,8},{25... | collective-permute-start | bytes 2654216 | tf_op jit(solution)/shard_map/ppermute | solution.py:1290
  315.2 11.4 %copy-start.1 = (f32[8,3,72,128]{3,2,1,0:T(8,128)}, f32[8,3,72,128]{3,2,1,0:T(8,128)S(1)}, u32[]{:S(2)}) copy-start(f32[8,3,72,128]{3,2,1,0:T(8,128)S(1)} %collective-permute-done.3.init_ref) | copy-start | bytes 2654212
  315.2 39.4 %collective-permute-start.6 = (bf16[4,2,64,1408]{3,2,1,0:T(8,128)(2,1)}, bf16[4,2,64,1408]{3,2,1,0:T(8,128)(2,1)}, u32[]{:S(2)}, u32[]{:S(2)}) collective-permute-start(bf16[4,2,64,1408]{3,2,1,0:T(8,128)(2,1)} %get-tuple-element.90), channel_id=1, source_target_pairs={{0,16},{16,0},{1,17},{17,1},{2,18},{18,2},{3,19},{19,3},{4,20},{20... | collective-permute-start | bytes 4325384 | tf_op jit(solution)/shard_map/ppermute | solution.py:1260
  320.4 34.2 %collective-permute-start.7 = (bf16[2,4,64,1408]{3,2,1,0:T(8,128)(2,1)}, bf16[2,4,64,1408]{3,2,1,0:T(8,128)(2,1)}, u32[]{:S(2)}, u32[]{:S(2)}) collective-permute-start(bf16[2,4,64,1408]{3,2,1,0:T(8,128)(2,1)} %get-tuple-element.92), channel_id=1, source_target_pairs={{0,2},{2,0},{1,3},{3,1},{4,6},{6,4},{5,7},{7,5},{8,10},{10,8},{9,1... | collective-permute-start | bytes 4325384 | tf_op jit(solution)/shard_map/ppermute | solution.py:1260
  321.0 5.6 %copy-start.9 = (bf16[32,256]{1,0:T(8,128)(2,1)S(1)}, bf16[32,256]{1,0:T(8,128)(2,1)}, u32[]{:S(2)}) copy-start(bf16[32,256]{1,0:T(8,128)(2,1)} %param.16) | copy-start | bytes 49156
  321.0 5.7 %copy-start.10 = (bf16[32,256]{1,0:T(8,128)(2,1)S(1)}, bf16[32,256]{1,0:T(8,128)(2,1)}, u32[]{:S(2)}) copy-start(bf16[32,256]{1,0:T(8,128)(2,1)} %param.17) | copy-start | bytes 49156
  321.0 6.5 %copy-start.11 = (f32[1,1024]{1,0:T(1,128)S(1)}, f32[1,1024]{1,0:T(1,128)}, u32[]{:S(2)}) copy-start(f32[1,1024]{1,0:T(1,128)} %get-tuple-element.88) | copy-start | bytes 12292
  326.5 18.8 %collective-permute-start.5 = (bf16[1024,512]{1,0:T(8,128)(2,1)}, bf16[1024,512]{1,0:T(8,128)(2,1)}, u32[]{:S(2)}, u32[]{:S(2)}) collective-permute-start(bf16[1024,512]{1,0:T(8,128)(2,1)} %weight_grad.9), channel_id=1, source_target_pairs={{0,1},{1,0},{2,3},{3,2},{4,5},{5,4},{6,7},{7,6},{8,9},{9,8},{10,11... | collective-permute-start | bytes 3145736 | tf_op jit(solution)/shard_map/ppermute | solution.py:1245
  345.3 5.9 %copy-start = (bf16[1024,1408]{1,0:T(8,128)(2,1)S(1)}, bf16[1024,1408]{1,0:T(8,128)(2,1)}, u32[]{:S(2)}) copy-start(bf16[1024,1408]{1,0:T(8,128)(2,1)} %weight_grad.10) | copy-start | bytes 8650756
  473.8 4.5 copy-start.7
  473.8 5.0 copy-start.8
  473.8 7.3 %copy-start.2 = (bf16[32,2752]{1,0:T(8,128)(2,1)S(1)}, bf16[32,2752]{1,0:T(8,128)(2,1)}, u32[]{:S(2)}) copy-start(bf16[32,2752]{1,0:T(8,128)(2,1)} %param.22) | copy-start | bytes 528388
  473.8 7.3 %copy-start.3 = (bf16[32,2752]{1,0:T(8,128)(2,1)S(1)}, bf16[32,2752]{1,0:T(8,128)(2,1)}, u32[]{:S(2)}) copy-start(bf16[32,2752]{1,0:T(8,128)(2,1)} %param.21) | copy-start | bytes 528388
  476.8 5.4 %copy-start.14 = (bf16[32]{0:T(256)(128)(2,1)S(1)}, bf16[32]{0:T(256)(128)(2,1)}, u32[]{:S(2)}) copy-start(bf16[32]{0:T(256)(128)(2,1)} %param.20) | copy-start | bytes 196
  476.9 7.2 %copy-start.12 = (bf16[32]{0:T(256)(128)(2,1)S(1)}, bf16[32]{0:T(256)(128)(2,1)}, u32[]{:S(2)}) copy-start(bf16[32]{0:T(256)(128)(2,1)} %param.15) | copy-start | bytes 196
  478.8 14.3 %copy-start.4 = (f32[32,1024]{1,0:T(8,128)}, f32[32,1024]{1,0:T(8,128)S(1)}, u32[]{:S(2)}) copy-start(f32[32,1024]{1,0:T(8,128)S(1)} %reshape.77) | copy-start | bytes 393220
Sparse Core Ops, SparseCore 0:
  11.4 131.4 all-gather.1

commit v6 on v5

--- a/solution.py
+++ b/solution.py
@@ -190,6 +190,7 @@
     nb_ref,
     saved_ref,
     init_ref,
+    wide_ref,
     one_ref,
     two_ref,
     block_ref,
@@ -209,8 +210,8 @@
     last = pl.num_programs(0) * halves - 1
     each = blocks // halves
     by_seq, by_z, by_y, by_core = neighbours(sizes)
-    count = 6 + 8
-    first = RowSums(sizes, (one_ref, two_ref), refs[:count], pair_out, summed=True)
+    count = 8 + 8
+    first = RowSums(sizes, wide_ref, refs[:count], pair_out, (one_ref, two_ref))
     refs = refs[count:]
     second = RowSums(sizes, block_ref, refs[:6] + (part_out,) + refs[6:])
 
@@ -370,13 +371,12 @@
     )(qkv, grad, mixed, den)
 
 
-def attention_backward(qkv, nb, saved, init, one, two, block, own):
+def attention_backward(qkv, nb, saved, init, wide, one, two, block, own):
     cols = qkv.shape[1]
     blocks = cols // CUT
     sizes = lax.axis_size("seq"), lax.axis_size("z")
     width = block.shape[-1]
     cut = 128 * (width // 256)
-    wide = one.shape[-1] + two.shape[-1]
     first_buffers, first_sems = row_sum_scratch(
         sizes, own, one.shape[-1], two.shape[-1], summed=True
     )
@@ -402,11 +402,12 @@
             here,
             here,
             here,
+            here,
         ],
         out_specs=[head_rows(HROWS), here, here],
         out_shape=[
             jax.ShapeDtypeStruct((HEADS * HROWS, cols), BF16),
-            jax.ShapeDtypeStruct((2, own, wide), BF16),
+            jax.ShapeDtypeStruct((2, own, wide.shape[-1]), BF16),
             jax.ShapeDtypeStruct((sizes[1], 2, own, width), BF16),
         ],
         scratch_shapes=[pltpu.VMEM((HG, VROWS, FROWS), F32)]
@@ -419,7 +420,16 @@
         ),
         cost_estimate=cost(53e9 * cols / 2048),
         name="attend_back",
-    )(qkv, nb, saved, init, one, two, block.reshape(sizes + (2, 2, own, width)))
+    )(
+        qkv,
+        nb,
+        saved,
+        init,
+        wide.reshape(sizes + (2, 2, own, wide.shape[-1])),
+        one,
+        two,
+        block.reshape(sizes + (2, 2, own, width)),
+    )
 
 
 MESH = pl.DeviceIdType.MESH
@@ -622,17 +632,18 @@
 
 
 class RowSums:
-    def __init__(self, sizes, source, refs, out_ref=None, summed=False):
+    def __init__(self, sizes, source, refs, out_ref=None, arrived=None):
         seq_parts, z_parts = self.sizes = sizes
         s, z, y, c = self.place = positions()
         by_seq, by_z, by_y, by_core = neighbours(sizes)
-        self.source, self.summed, self.out_ref = source, summed, out_ref
+        self.source, self.summed, self.out_ref = source, arrived is not None, out_ref
         refs = list(refs)
-        if summed:
-            self.x_sum, self.y_sum = source
-        else:
-            self.x_in, self.x_sum, self.y_in, self.y_sum = refs[:4]
-            del refs[:4]
+        self.x_sum, self.y_sum = refs[:2]
+        del refs[:2]
+        if arrived is None:
+            arrived = refs[:2]
+            del refs[:2]
+        self.x_in, self.y_in = arrived
         self.then_y_in, self.then_x_in, self.row_sum = refs[:3]
         del refs[:3]
         self.cut = self.x_sum.shape[-1]
@@ -643,7 +654,7 @@
         pairs = [refs[2 * i : 2 * i + 2] for i in range(len(refs) // 2)]
         others = range(1, seq_parts)
         self.first = []
-        if not summed:
+        if not self.summed:
             left, right = pl.ds(0, self.cut), pl.ds(self.cut, rest)
             self.first_x = [
                 remote(
@@ -683,15 +694,15 @@
         if not self.summed:
             for copy in self.first_x:
                 copy.wait_recv()
-            total = self.source[s, :, :, :, :, : self.cut].astype(F32)
-            for j in range(self.sizes[0] - 1):
-                total = total + self.x_in[j].astype(F32)
-            self.x_sum[...] = total.astype(BF16)
+        total = self.source[s, :, :, :, :, : self.cut].astype(F32)
+        for j in range(self.sizes[0] - 1):
+            total = total + self.x_in[j].astype(F32)
+        self.x_sum[...] = total.astype(BF16)
         self.then_y.start()
         if not self.summed:
             self.first_y.wait_recv()
-            total = self.source[:, :, y, :, :, self.cut :].astype(F32)
-            self.y_sum[...] = (total + self.y_in[...].astype(F32)).astype(BF16)
+        total = self.source[:, :, y, :, :, self.cut :].astype(F32)
+        self.y_sum[...] = (total + self.y_in[...].astype(F32)).astype(BF16)
         for copy in self.then_x:
             copy.start()
 
@@ -753,13 +764,12 @@
     def low(*shape):
         return pltpu.VMEM(shape, BF16)
 
-    first = [
-        low(seq_parts - 1, z_parts, 2, 2, own, cut),
-        low(z_parts, 2, 2, own, cut),
-        low(seq_parts, z_parts, 2, own, rest),
-        low(seq_parts, z_parts, 2, own, rest),
-    ]
-    buffers = [] if summed else first
+    buffers = [low(z_parts, 2, 2, own, cut), low(seq_parts, z_parts, 2, own, rest)]
+    if not summed:
+        buffers += [
+            low(seq_parts - 1, z_parts, 2, 2, own, cut),
+            low(seq_parts, z_parts, 2, own, rest),
+        ]
     buffers += [low(z_parts, 2, own, cut), low(seq_parts - 1, z_parts, 2, own, rest)]
     if keep:
         buffers += [low(z_parts, 2, own, cols)]
@@ -1064,6 +1074,7 @@
     attended_ref,
     resid_back_ref,
     mixed_back_ref,
+    side_ref,
     error_ref,
     w_out,
     w_gate,
@@ -1143,8 +1154,18 @@
     attended_ref[...] = attended
     mixed_back_ref[...] = dot(w_out[...], attended, NT).astype(BF16)
 
-
-def feed_forward(count, tokens, targets, mixed, gain, late, padded):
+    @pl.when(step == pl.num_programs(0) - 1)
+    def _():
+        error = 0.5 * jnp.sum(error_ref[...], -1, keepdims=True)
+        high = error.astype(BF16).astype(F32)
+        middle = (error - high).astype(BF16).astype(F32)
+        low = error - high - middle
+        column = lax.broadcasted_iota(jnp.int32, side_ref.shape, 1) - count_ref[1]
+        side = jnp.where(column == 0, high, jnp.where(column == 1, middle, 0.0))
+        side_ref[...] = jnp.where(column == 2, low, side).astype(BF16)
+
+
+def feed_forward(count, tokens, targets, mixed, gain, late, padded, extra):
     rows, width = tokens.shape[1:]
     tile = min(rows, 256)
     token_spec = pl.BlockSpec((1, tile, width), lambda i, c: (0, i, 0))
@@ -1153,7 +1174,6 @@
         return pl.BlockSpec((tile, cols), lambda i, c: (i, 0))
 
     tall = pl.BlockSpec((width, tile), lambda i, c: (0, i))
-    line = pl.BlockSpec((1, width), lambda i, c: (0, 0))
     return pl.pallas_call(
         functools.partial(ffn_kernel, padded),
         grid_spec=pltpu.PrefetchScalarGridSpec(
@@ -1175,9 +1195,10 @@
                 flat(width),
                 flat(width),
                 tall,
-                line,
+                pl.BlockSpec((width, extra), lambda i, c: (0, 0)),
             ],
             scratch_shapes=[
+                pltpu.VMEM((1, width), F32),
                 pltpu.VMEM((width, width), BF16),
                 pltpu.VMEM((width, padded), BF16),
                 pltpu.VMEM((width, padded), BF16),
@@ -1196,7 +1217,7 @@
             jax.ShapeDtypeStruct((rows, width), BF16),
             jax.ShapeDtypeStruct((rows, width), F32),
             jax.ShapeDtypeStruct((width, rows), BF16),
-            jax.ShapeDtypeStruct((1, width), F32),
+            jax.ShapeDtypeStruct((width, extra), BF16),
         ],
         compiler_params=pltpu.CompilerParams(vmem_limit_bytes=60 * 1024 * 1024),
         cost_estimate=cost(4 * rows * width * (width + 3 * padded)),
@@ -1250,21 +1271,16 @@
     index = lax.axis_index(axis)
     return [
         lax.dynamic_index_in_dim(pieces, lax.rem(index + shift, parts), dim, keepdims=False)
-        for shift in range(parts)
+        for shift in range(1, parts)
     ]
 
 
 def send(pieces, axis):
     parts = lax.axis_size(axis)
-    return pieces[:1] + [
+    return [
         lax.ppermute(piece, axis, [(i, (i + shift) % parts) for i in range(parts)])
-        for shift, piece in enumerate(pieces)
-        if shift
+        for shift, piece in enumerate(pieces, 1)
     ]
-
-
-def total(pieces):
-    return sum(piece.astype(F32) for piece in pieces).astype(BF16)
 
 
 def as_pieces(block):
@@ -1317,7 +1333,9 @@
     owners = jnp.arange(valid_count.shape[0])
     count = jnp.sum(jnp.where(owners == batch_index, valid_count, 0))
     total_valid = jnp.sum(valid_count).astype(F32)
-    valid_here = jnp.reshape(count - seq_index * rows, (1,))
+    place = 3 * lax.axis_index(everyone)
+    valid_here = jnp.stack([count - seq_index * rows, place]).astype(jnp.int32)
+    extra = -(-3 * devices // 128) * 128
     gains = jnp.pad(jnp.stack([gain_mix, gain_ffn], 1), ((0, 0), (0, 126)))
     early = gather_rows(jnp.concatenate([gains, w_query, w_key, w_value], 1))
     fill = ((0, 0), (0, padded - hidden_units))
@@ -1344,20 +1362,10 @@
         attended_back,
         resid_back,
         mixed_back,
-        squares,
-    ) = feed_forward(valid_here, inputs, targets, mixed, gain_rows, late, padded)
-    local_error = 0.5 * jnp.sum(squares)
+        side,
+    ) = feed_forward(valid_here, inputs, targets, mixed, gain_rows, late, padded, extra)
     mine, others = jnp.reshape(core, (1,)), jnp.reshape(1 - core, (1,))
     half, out_half, qkv_cols = padded // 2, width // 2, HEADS * HROWS // 2
-
-    high = lax.reduce_precision(local_error, 8, 7)
-    middle = lax.reduce_precision(local_error - high, 8, 7)
-    low = lax.reduce_precision(local_error - high - middle, 8, 7)
-    column = lax.broadcasted_iota(jnp.int32, (width, -(-3 * devices // 128) * 128), 1)
-    place = 3 * lax.axis_index(everyone)
-    side = jnp.where(column == place, high, 0.0)
-    side = jnp.where(column == place + 1, middle, side)
-    side = jnp.where(column == place + 2, low, side).astype(BF16)
 
     nb, back = local_back_state(qkv, mixed_back, mixed, den)
     later = shifted_sum(back, seq_parts, -1)
@@ -1383,10 +1391,10 @@
     block, a_one, a_two = tie((block, a_one, a_two))
     own = w_query.shape[0]
     z_parts = lax.axis_size("z")
-    one = total(a_one).reshape(z_parts, 2, 2, own, half)
-    two = total(a_two).reshape(seq_parts, z_parts, 2, own, half)
+    one = jnp.stack(a_one).reshape(seq_parts - 1, z_parts, 2, 2, own, half)
+    two = a_two[0].reshape(seq_parts, z_parts, 2, own, half)
     qkv_back, gate_up_pair, part = attention_backward(
-        qkv, nb, saved, later, one, two, block, own
+        qkv, nb, saved, later, gate_up, one, two, block, own
     )
     gate_sum, up_sum = gate_up_pair[0], gate_up_pair[1]
     if own % 16 == 0 and rows % 512 == 0:

time: 505 us -> 501 us (level)
  other arithmetic: 21.4 us -> 13.7 us
    convert_element_type x3 -> x0, other arithmetic: 7 us -> none  [the longest x2 5.68 us: total(): return sum((piece.astype(F32) for piece in pieces)).astype(BF16)]
    unnamed x35 -> x37, local copies, waits for them, and re-layouts: 11.7 us -> 13.2 us
  transfers between devices with their start and end apart: 9 -> 9, of which waited for: 3 -> 5; matrix products, arithmetic and copies ran while one was open for 3% -> 3% of each run, Pallas kernels for 30% -> 31%
where the time goes in v6:
time: 501 us; the launch traced here: 497 us
  Pallas kernels  401 us (80%)
  waiting for transfers between devices  29.7 us (6%)
  local copies, waits for them, and re-layouts  22.6 us (5%)
  between operations  17.9 us (4%)
  other arithmetic  13.7 us (3%)
  starting transfers between devices  12 us (2%)
    pallas_call x1, Pallas kernels, feed_forward(): pl.pallas_call(functools.partial(ffn_kernel, padded), grid_spec=pltpu.Pre...  103 us
    pallas_call x6, Pallas kernels, weight_grad(): pl.pallas_call(functools.partial(weight_grad_kernel, form), grid_spec=plt...  72.5 us
    pallas_call x1, Pallas kernels, attention_backward(): pl.pallas_call(functools.partial(backward_kernel, sizes, blocks), grid=(H...  63.1 us
    pallas_call x1, Pallas kernels, last_gradients(): pl.pallas_call(functools.partial(last_kernel, sizes), grid=(6,), in_specs...  51.4 us
    pallas_call x2, Pallas kernels, attention_forward(): pl.pallas_call(functools.partial(forward_kernel, blocks), grid=(count //...  39.7 us
    pallas_call x1, Pallas kernels, gather_rows(): pl.pallas_call(functools.partial(gather_kernel, (seq_parts, z_parts), spl...  32.7 us
    all_gather x1, waiting for transfers between devices, body(): late = lax.all_gather(late, everyone, axis=0, tiled=True)  23.8 us
    unnamed x37, local copies, waits for them, and re-layouts  13.2 us
  transfers between devices with their start and end apart: 9, of which 5 were waited for; matrix products, arithmetic and copies ran while one was open for 3% of the time, Pallas kernels for 31%

profile of v6, /device:TPU:0, one launch (start us, length us, event | category | flops | bytes accessed | tf_op | source)
XLA Modules:
  0.0 497.3 jit_solution(9656422140203210603)
XLA Ops:
  7.2 2.0 fusion.6
  9.2 0.7 pad_maximum_fusion.2
  10.0 1.5 fusion.12.shard_ref
  11.5 32.7 %gather_rows.1 = bf16[2,4,2,2,32,1664]{5,4,3,2,1,0:T(8,128)(2,1)} custom-call(bf16[32,1664]{1,0:T(8,128)(2,1)} %fusion.12.shard_ref), custom_call_target="tpu_custom_call" | custom-call | flops 500000000 | tf_op jit(solution)/shard_map/gather_rows/pallas_call | solution.py:533
  44.2 13.1 %project.1 = (bf16[1536,2048]{1,0:T(8,128)(2,1)}, bf16[1024,2048]{1,0:T(8,128)(2,1)}, bf16[1536,1024]{1,0:T(8,128)(2,1)}, f32[8,1024]{1,0:T(8,128)}) custom-call(bf16[1,2048,1024]{2,1,0:T(8,128)(2,1)} %tokens_ref.5, bf16[1024,1664]{1,0:T(8,128)(2,1)} %bitcast.35), custom_call_target="tpu_custom_call" | custom-call | flops 128849016 | tf_op jit(solution)/shard_map/project/pallas_call | solution.py:577
  57.3 6.6 %key_state.2 = f32[4,3,72,128]{3,2,1,0:T(8,128)} custom-call(bf16[1536,2048]{1,0:T(8,128)(2,1)} %get-tuple-element.56.qkv_ref), custom_call_target="tpu_custom_call" | custom-call | flops 110000000 | tf_op jit(solution)/shard_map/key_state/pallas_call | solution.py:306
  63.9 3.3 collective-permute-start.1
  67.1 6.6 %key_state.3 = f32[4,3,72,128]{3,2,1,0:T(8,128)} custom-call(bf16[1536,2048]{1,0:T(8,128)(2,1)} %get-tuple-element.56.qkv_ref), custom_call_target="tpu_custom_call" | custom-call | flops 110000000 | tf_op jit(solution)/shard_map/key_state/pallas_call | solution.py:306
  73.8 1.5 collective-permute-start
  75.3 0.6 fusion.14
  76.6 0.6 pad_add_fusion.count_ref
  77.1 0.8 collective-permute-done.1.init_ref
  77.9 0.8 copy-done.6
  78.7 19.8 %attend.2 = (bf16[1024,2048]{1,0:T(8,128)(2,1)}, f32[4,4,2048]{2,1,0:T(4,128)}, bf16[16,8,160,176]{3,2,1,0:T(8,128)(2,1)}) custom-call(bf16[1536,2048]{1,0:T(8,128)(2,1)} %get-tuple-element.56.qkv_ref, f32[4,3,72,128]{3,2,1,0:T(8,128)} %copy-done.6), custom_call_target="tpu_custom_call" | custom-call | flops 360000000 | tf_op jit(solution)/shard_map/attend/pallas_call | solution.py:329
  98.5 0.8 copy-done.7
  99.3 19.9 %attend.3 = (bf16[1024,2048]{1,0:T(8,128)(2,1)}, f32[4,4,2048]{2,1,0:T(4,128)}, bf16[16,8,160,176]{3,2,1,0:T(8,128)(2,1)}) custom-call(bf16[1536,2048]{1,0:T(8,128)(2,1)} %get-tuple-element.56.qkv_ref, f32[4,3,72,128]{3,2,1,0:T(8,128)} %copy-done.7, ...), custom_call_target="tpu_custom_call", output_to_operand_aliasing={{0}: (2, {}), {1}: (3, {}), {2}: (4, {})} | custom-call | flops 360000000 | tf_op jit(solution)/shard_map/attend/pallas_call | solution.py:329
  119.2 23.8 %all-gather.2.cloned.1.call-done.late_ref = bf16[1024,9472]{1,0:T(8,128)(2,1)} async-done(((bf16[32,9472]{1,0:T(8,128)(2,1)}), bf16[1024,9472]{1,0:T(8,128)(2,1)}) %all-gather.2.cloned.1.call-update) | async-done | bytes 19398672 | tf_op jit(solution)/shard_map/all_gather | solution.py:1345
  143.0 103.0 %feed_forward.1 = (bf16[1,2048,1024]{2,1,0:T(8,128)(2,1)}, bf16[1024,2048]{1,0:T(8,128)(2,1)}, bf16[2048,2816]{1,0:T(8,128)(2,1)}, bf16[1024,2048]{1,0:T(8,128)(...) custom-call(s32[2]{0:T(128)} %pad_add_fusion.count_ref, ...), custom_call_target="tpu_custom_call" | custom-call | flops 1589137920 | tf_op jit(solution)/shard_map/feed_forward/pallas_call | solution.py:1177
  246.0 12.8 %query_state.1 = (bf16[16,80,2048]{2,1,0:T(8,128)(2,1)}, f32[8,3,72,128]{3,2,1,0:T(8,128)}) custom-call(bf16[1536,2048]{1,0:T(8,128)(2,1)} %get-tuple-element.56.qkv_ref, bf16[1024,2048]{1,0:T(8,128)(2,1)} %get-tuple-element.65.grad_ref, bf16[1024,2048]{1,0:T(8,128)(2,1)} %get-tuple-element.83.mixed_ref.left_ref, f32[4,4,2048]{2,1,0:T(4,128)} %get-tuple-element.66.den_ref), custom_call_target="tpu_custom_call" | custom-call | flops 260000000 | tf_op jit(solution)/shard_map/query_state/pallas_call | solution.py:354
  258.8 18.7 %weight_grad.6 = bf16[1024,2816]{1,0:T(8,128)(2,1)} custom-call(s32[1]{0:T(128)} %bitcast.6.pick_ref, bf16[1024,2048]{1,0:T(8,128)(2,1)} %get-tuple-element.75.left_ref, bf16[2048,5632]{1,0:T(8,128)(2,1)} %get-tuple-element.72.right_ref), custom_call_target="tpu_custom_call" | custom-call | flops 236223200 | tf_op jit(solution)/shard_map/weight_grad/pallas_call | solution.py:1250
  277.8 11.2 %weight_grad.7 = bf16[1024,1408]{1,0:T(8,128)(2,1)} custom-call(s32[1]{0:T(128)} %bitcast.6.pick_ref, bf16[1024,2048]{1,0:T(8,128)(2,1)} %get-tuple-element.80.left_ref, bf16[2048,2816]{1,0:T(8,128)(2,1)} %get-tuple-element.74.right_ref), custom_call_target="tpu_custom_call" | custom-call | flops 118111600 | tf_op jit(solution)/shard_map/weight_grad/pallas_call | solution.py:1250
  289.3 1.3 collective-permute-start.3
  290.6 19.4 %weight_grad.8 = bf16[1024,2816]{1,0:T(8,128)(2,1)} custom-call(s32[1]{0:T(128)} %bitcast.5.pick_ref, bf16[1024,2048]{1,0:T(8,128)(2,1)} %get-tuple-element.75.left_ref, bf16[2048,5632]{1,0:T(8,128)(2,1)} %get-tuple-element.72.right_ref, bf16[1024,2816]{1,0:T(8,128)(2,1)} %collective-permute-done.2.refs_0_), custom_call_target="tpu_custom_call" | custom-call | flops 236223200 | tf_op jit(solution)/shard_map/weight_grad/pallas_call | solution.py:1250
  310.0 3.1 fusion.15
  313.1 1.3 dynamic-slice_bitcast_fusion
  314.4 1.2 dynamic-slice_bitcast_fusion.1
  315.6 0.8 collective-permute-done.3.init_ref
  316.5 4.8 collective-permute-start.6
  321.2 0.6 collective-permute-start.7
  321.8 5.5 %weight_grad.9 = bf16[1024,512]{1,0:T(8,128)(2,1)} custom-call(s32[1]{0:T(128)} %bitcast.6.pick_ref, bf16[1024,2048]{1,0:T(8,128)(2,1)} %get-tuple-element.83.mixed_ref.left_ref, bf16[2048,1024]{1,0:T(8,128)(2,1)} %get-tuple-element.79.right_ref), custom_call_target="tpu_custom_call" | custom-call | flops 42949672 | tf_op jit(solution)/shard_map/weight_grad/pallas_call | solution.py:1250
  328.3 1.5 copy-done.1
  329.9 11.7 %weight_grad.10 = bf16[1024,1408]{1,0:T(8,128)(2,1)} custom-call(s32[1]{0:T(128)} %bitcast.5.pick_ref, bf16[1024,2048]{1,0:T(8,128)(2,1)} %get-tuple-element.80.left_ref, bf16[2048,2816]{1,0:T(8,128)(2,1)} %get-tuple-element.74.right_ref, bf16[1024,1408]{1,0:T(8,128)(2,1)} %copy-done.1), custom_call_target="tpu_custom_call" | custom-call | flops 118111600 | tf_op jit(solution)/shard_map/weight_grad/pallas_call | solution.py:1250
  341.6 5.9 %weight_grad.11 = bf16[1024,512]{1,0:T(8,128)(2,1)} custom-call(s32[1]{0:T(128)} %bitcast.5.pick_ref, bf16[1024,2048]{1,0:T(8,128)(2,1)} %get-tuple-element.83.mixed_ref.left_ref, bf16[2048,1024]{1,0:T(8,128)(2,1)} %get-tuple-element.79.right_ref, bf16[1024,512]{1,0:T(8,128)(2,1)} %collective-permute-done.5.refs_0_), custom_call_target="tpu_custom_call" | custom-call | flops 42949672 | tf_op jit(solution)/shard_map/weight_grad/pallas_call | solution.py:1250
  347.5 3.3 pad_maximum_fusion
  350.7 2.8 collective-permute-done.6
  353.5 1.5 collective-permute-done.7
  355.0 63.1 %attend_back.1 = (bf16[1536,2048]{1,0:T(8,128)(2,1)}, bf16[2,32,2816]{2,1,0:T(8,128)(2,1)}, bf16[4,2,32,2048]{3,2,1,0:T(8,128)(2,1)}) custom-call(bf16[1536,2048]{1,0:T(8,128)(2,1)} %get-tuple-element.56.qkv_ref, bf16[16,80,2048]{2,1,0:T(8,128)(2,1)} %get-tuple-element.68.nb_ref, bf16[16,8,160,176]{3,2,1,0:T(8,128)(2,1)} %get-tuple-element.69.saved_ref, ...), custom_call_target="tpu_custom_call" | custom-call | flops 1060000000 | tf_op jit(solution)/shard_map/attend_back/pallas_call | solution.py:394
  418.1 51.4 %last_gradients.1 = (f32[1,2048,1024]{2,1,0:T(8,128)}, bf16[2,32,768]{2,1,0:T(8,128)(2,1)}, bf16[2,32,2048]{2,1,0:T(8,128)(2,1)}) custom-call(bf16[1024,2048]{1,0:T(8,128)(2,1)} %get-tuple-element.63.normed_ref, bf16[1536,2048]{1,0:T(8,128)(2,1)} %get-tuple-element.90.back_ref, bf16[1536,1024]{1,0:T(8,128)(2,1)} %get-tuple-element.91.flipped_ref, ...), custom_call_target="tpu_custom_call" | custom-call | flops 515396064 | tf_op jit(solution)/shard_map/last_gradients/pallas_call | solution.py:1019
  469.6 1.0 slice_bitcast_fusion.3
  470.6 0.8 slice_bitcast_fusion.5
  471.4 0.8 fusion.17
  472.8 1.3 convert_reduce_fusion
  474.7 0.7 copy.43
  475.4 0.7 copy.44
  476.1 0.8 fusion.9
  476.9 1.1 multiply_reduce_fusion
  478.5 0.7 maximum_convert_fusion.1
  480.4 8.4 %copy.49 = f32[1,2048,1024]{2,1,0:T(8,128)} copy(f32[1,2048,1024]{2,1,0:T(8,128)} %get-tuple-element.158) | data formatting | bytes 16777216
  (54 shorter events, 3.2 us)
Async XLA Ops:
  7.2 135.8 %all-gather.2.cloned.1.call-start = ((), (), s32[]{:S(2)}) async-start(), calls=%async_computation | async-start | bytes 20004864 | tf_op jit(solution)/shard_map/all_gather | solution.py:1345
  63.9 11.4 %copy-start.14 = (s32[16]{0:T(128)S(1)}, s32[16]{0:T(128)}, u32[]{:S(2)}) copy-start(s32[16]{0:T(128)} %param.14) | copy-start | bytes 196
  63.9 14.1 %collective-permute-start.1 = (f32[4,3,72,128]{3,2,1,0:T(8,128)}, f32[4,3,72,128]{3,2,1,0:T(8,128)S(1)}, u32[]{:S(2)}, u32[]{:S(2)}) collective-permute-start(f32[4,3,72,128]{3,2,1,0:T(8,128)} %key_state.2), channel_id=1, source_target_pairs={{0,16},{1,17},{2,18},{3,19},{4,20},{5,21},{6,22},{7,23},{8,24},{9,... | collective-permute-start | bytes 1327112 | tf_op jit(solution)/shard_map/ppermute | solution.py:1306
  73.8 24.8 %collective-permute-start = (f32[4,3,72,128]{3,2,1,0:T(8,128)}, f32[4,3,72,128]{3,2,1,0:T(8,128)S(1)}, u32[]{:S(2)}, u32[]{:S(2)}) collective-permute-start(f32[4,3,72,128]{3,2,1,0:T(8,128)} %key_state.3), channel_id=1, source_target_pairs={{0,16},{1,17},{2,18},{3,19},{4,20},{5,21},{6,22},{7,23},{8,24},{9,... | collective-permute-start | bytes 1327112 | tf_op jit(solution)/shard_map/ppermute | solution.py:1306
  77.9 0.8 copy-start.6
  98.5 0.8 copy-start.7
  277.5 13.0 %collective-permute-start.2 = (bf16[1024,2816]{1,0:T(8,128)(2,1)}, bf16[1024,2816]{1,0:T(8,128)(2,1)}, u32[]{:S(2)}, u32[]{:S(2)}) collective-permute-start(bf16[1024,2816]{1,0:T(8,128)(2,1)} %weight_grad.6), channel_id=1, source_target_pairs={{0,1},{1,0},{2,3},{3,2},{4,5},{5,4},{6,7},{7,6},{8,9},{9,8},{10,11... | collective-permute-start | bytes 17301512 | tf_op jit(solution)/shard_map/ppermute | solution.py:1266
  289.1 39.2 %collective-permute-start.4 = (bf16[1024,1408]{1,0:T(8,128)(2,1)}, bf16[1024,1408]{1,0:T(8,128)(2,1)S(1)}, u32[]{:S(2)}, u32[]{:S(2)}) collective-permute-start(bf16[1024,1408]{1,0:T(8,128)(2,1)} %weight_grad.7), channel_id=1, source_target_pairs={{0,1},{1,0},{2,3},{3,2},{4,5},{5,4},{6,7},{7,6},{8,9},{9,8},{10,11... | collective-permute-start | bytes 8650760 | tf_op jit(solution)/shard_map/ppermute | solution.py:1266
  289.3 27.2 %collective-permute-start.3 = (f32[8,3,72,128]{3,2,1,0:T(8,128)}, f32[8,3,72,128]{3,2,1,0:T(8,128)S(1)}, u32[]{:S(2)}, u32[]{:S(2)}) collective-permute-start(f32[8,3,72,128]{3,2,1,0:T(8,128)} %get-tuple-element.76), channel_id=1, source_target_pairs={{16,0},{17,1},{18,2},{19,3},{20,4},{21,5},{22,6},{23,7},{24,8},{25... | collective-permute-start | bytes 2654216 | tf_op jit(solution)/shard_map/ppermute | solution.py:1306
  316.4 10.9 %copy-start.2 = (f32[8,3,72,128]{3,2,1,0:T(8,128)}, f32[8,3,72,128]{3,2,1,0:T(8,128)S(1)}, u32[]{:S(2)}) copy-start(f32[8,3,72,128]{3,2,1,0:T(8,128)S(1)} %collective-permute-done.3.init_ref) | copy-start | bytes 2654212
  316.5 37.1 %collective-permute-start.6 = (bf16[4,2,64,1408]{3,2,1,0:T(8,128)(2,1)}, bf16[4,2,64,1408]{3,2,1,0:T(8,128)(2,1)}, u32[]{:S(2)}, u32[]{:S(2)}) collective-permute-start(bf16[4,2,64,1408]{3,2,1,0:T(8,128)(2,1)} %dynamic-slice_bitcast_fusion.1), channel_id=1, source_target_pairs={{0,16},{16,0},{1,17},{17,1},{2,18},{18,2},{3,19},{19,3},{4,20},{20... | collective-permute-start | bytes 4325384 | tf_op jit(solution)/shard_map/ppermute | solution.py:1281
  321.2 33.8 %collective-permute-start.7 = (bf16[2,4,64,1408]{3,2,1,0:T(8,128)(2,1)}, bf16[2,4,64,1408]{3,2,1,0:T(8,128)(2,1)}, u32[]{:S(2)}, u32[]{:S(2)}) collective-permute-start(bf16[2,4,64,1408]{3,2,1,0:T(8,128)(2,1)} %dynamic-slice_bitcast_fusion), channel_id=1, source_target_pairs={{0,2},{2,0},{1,3},{3,1},{4,6},{6,4},{5,7},{7,5},{8,10},{10,8},{9,1... | collective-permute-start | bytes 4325384 | tf_op jit(solution)/shard_map/ppermute | solution.py:1281
  321.8 5.6 %copy-start.11 = (bf16[32,256]{1,0:T(8,128)(2,1)S(1)}, bf16[32,256]{1,0:T(8,128)(2,1)}, u32[]{:S(2)}) copy-start(bf16[32,256]{1,0:T(8,128)(2,1)} %param.16) | copy-start | bytes 49156
  321.8 5.7 %copy-start.12 = (bf16[32,256]{1,0:T(8,128)(2,1)S(1)}, bf16[32,256]{1,0:T(8,128)(2,1)}, u32[]{:S(2)}) copy-start(bf16[32,256]{1,0:T(8,128)(2,1)} %param.17) | copy-start | bytes 49156
  327.4 14.2 %collective-permute-start.5 = (bf16[1024,512]{1,0:T(8,128)(2,1)}, bf16[1024,512]{1,0:T(8,128)(2,1)}, u32[]{:S(2)}, u32[]{:S(2)}) collective-permute-start(bf16[1024,512]{1,0:T(8,128)(2,1)} %weight_grad.9), channel_id=1, source_target_pairs={{0,1},{1,0},{2,3},{3,2},{4,5},{5,4},{6,7},{7,6},{8,9},{9,8},{10,11... | collective-permute-start | bytes 3145736 | tf_op jit(solution)/shard_map/ppermute | solution.py:1266
  328.3 1.5 copy-start.1
  341.6 5.9 %copy-start = (bf16[1024,1408]{1,0:T(8,128)(2,1)S(1)}, bf16[1024,1408]{1,0:T(8,128)(2,1)}, u32[]{:S(2)}) copy-start(bf16[1024,1408]{1,0:T(8,128)(2,1)} %weight_grad.10) | copy-start | bytes 8650756
  341.6 5.9 %copy-start.9 = (bf16[1024,128]{1,0:T(8,128)(2,1)S(1)}, bf16[1024,128]{1,0:T(8,128)(2,1)}, u32[]{:S(2)}) copy-start(bf16[1024,128]{1,0:T(8,128)(2,1)} %get-tuple-element.84) | copy-start | bytes 786436
  418.1 56.0 %copy-start.8 = (bf16[2,32,2816]{2,1,0:T(8,128)(2,1)S(1)}, bf16[2,32,2816]{2,1,0:T(8,128)(2,1)}, u32[]{:S(2)}) copy-start(bf16[2,32,2816]{2,1,0:T(8,128)(2,1)} %get-tuple-element.97) | copy-start | bytes 1081348
  469.6 5.0 %copy-start.10 = (bf16[32,1024]{1,0:T(8,128)(2,1)S(1)}, bf16[32,1024]{1,0:T(8,128)(2,1)}, u32[]{:S(2)}) copy-start(bf16[32,1024]{1,0:T(8,128)(2,1)} %param.18) | copy-start | bytes 196612
  469.6 7.3 %copy-start.3 = (bf16[32,2752]{1,0:T(8,128)(2,1)S(1)}, bf16[32,2752]{1,0:T(8,128)(2,1)}, u32[]{:S(2)}) copy-start(bf16[32,2752]{1,0:T(8,128)(2,1)} %param.22) | copy-start | bytes 528388
  469.6 7.3 %copy-start.4 = (bf16[32,2752]{1,0:T(8,128)(2,1)S(1)}, bf16[32,2752]{1,0:T(8,128)(2,1)}, u32[]{:S(2)}) copy-start(bf16[32,2752]{1,0:T(8,128)(2,1)} %param.21) | copy-start | bytes 528388
  469.6 8.3 %copy-start.15 = (bf16[32]{0:T(256)(128)(2,1)S(1)}, bf16[32]{0:T(256)(128)(2,1)}, u32[]{:S(2)}) copy-start(bf16[32]{0:T(256)(128)(2,1)} %param.20) | copy-start | bytes 196
  469.6 10.3 %copy-start.13 = (bf16[32]{0:T(256)(128)(2,1)S(1)}, bf16[32]{0:T(256)(128)(2,1)}, u32[]{:S(2)}) copy-start(bf16[32]{0:T(256)(128)(2,1)} %param.15) | copy-start | bytes 196
  474.6 14.3 %copy-start.5 = (f32[32,1024]{1,0:T(8,128)}, f32[32,1024]{1,0:T(8,128)S(1)}, u32[]{:S(2)}) copy-start(f32[32,1024]{1,0:T(8,128)S(1)} %reshape.73) | copy-start | bytes 393220
Sparse Core Ops, SparseCore 0:
  11.4 131.5 all-gather.1

commit v7 on v6

--- a/solution.py
+++ b/solution.py
@@ -19,8 +19,8 @@
 VROWS = HEAD_DIM + 16
 PAIR = 2 * VROWS
 SENT = HEAD_DIM + 8
-HG = 4
-FIRST_BACK, SECOND_BACK = 4, 2
+HG = 8
+FIRST_BACK, SECOND_BACK = 2, 1
 
 epsilon = 1e-05
 F32 = jnp.float32

time: 501 us -> 503 us (level)
  no operation moved by 1% of the time
where the time goes in v7:
time: 503 us; the launch traced here: 496 us
  Pallas kernels  401 us (80%)
  waiting for transfers between devices  29.8 us (6%)
  local copies, waits for them, and re-layouts  22.6 us (4%)
  between operations  17.9 us (4%)
  other arithmetic  13.7 us (3%)
  starting transfers between devices  11.8 us (2%)
    pallas_call x1, Pallas kernels, feed_forward(): pl.pallas_call(functools.partial(ffn_kernel, padded), grid_spec=pltpu.Pre...  103 us
    pallas_call x6, Pallas kernels, weight_grad(): pl.pallas_call(functools.partial(weight_grad_kernel, form), grid_spec=plt...  72.5 us
    pallas_call x1, Pallas kernels, attention_backward(): pl.pallas_call(functools.partial(backward_kernel, sizes, blocks), grid=(H...  64.8 us
    pallas_call x1, Pallas kernels, last_gradients(): pl.pallas_call(functools.partial(last_kernel, sizes), grid=(6,), in_specs...  49.3 us
    pallas_call x2, Pallas kernels, attention_forward(): pl.pallas_call(functools.partial(forward_kernel, blocks), grid=(count //...  40.2 us
    pallas_call x1, Pallas kernels, gather_rows(): pl.pallas_call(functools.partial(gather_kernel, (seq_parts, z_parts), spl...  32.7 us
    all_gather x1, waiting for transfers between devices, body(): late = lax.all_gather(late, everyone, axis=0, tiled=True)  23.8 us
    unnamed x37, local copies, waits for them, and re-layouts  13.2 us
  transfers between devices with their start and end apart: 9, of which 5 were waited for; matrix products, arithmetic and copies ran while one was open for 3% of the time, Pallas kernels for 31%

profile of v7, /device:TPU:0, one launch (start us, length us, event | category | flops | bytes accessed | tf_op | source)
XLA Modules:
  0.0 496.5 jit_solution(13977272732053199370)
XLA Ops:
  7.2 2.0 fusion.6
  9.2 0.7 pad_maximum_fusion.2
  10.0 1.5 fusion.12.shard_ref
  11.5 32.7 %gather_rows.1 = bf16[2,4,2,2,32,1664]{5,4,3,2,1,0:T(8,128)(2,1)} custom-call(bf16[32,1664]{1,0:T(8,128)(2,1)} %fusion.12.shard_ref), custom_call_target="tpu_custom_call" | custom-call | flops 500000000 | tf_op jit(solution)/shard_map/gather_rows/pallas_call | solution.py:533
  44.2 13.1 %project.1 = (bf16[1536,2048]{1,0:T(8,128)(2,1)}, bf16[1024,2048]{1,0:T(8,128)(2,1)}, bf16[1536,1024]{1,0:T(8,128)(2,1)}, f32[8,1024]{1,0:T(8,128)}) custom-call(bf16[1,2048,1024]{2,1,0:T(8,128)(2,1)} %tokens_ref.5, bf16[1024,1664]{1,0:T(8,128)(2,1)} %bitcast.35), custom_call_target="tpu_custom_call" | custom-call | flops 128849016 | tf_op jit(solution)/shard_map/project/pallas_call | solution.py:577
  57.3 6.2 %key_state.2 = f32[4,3,72,128]{3,2,1,0:T(8,128)} custom-call(bf16[1536,2048]{1,0:T(8,128)(2,1)} %get-tuple-element.56.qkv_ref), custom_call_target="tpu_custom_call" | custom-call | flops 110000000 | tf_op jit(solution)/shard_map/key_state/pallas_call | solution.py:306
  63.5 3.3 collective-permute-start.1
  66.7 6.2 %key_state.3 = f32[4,3,72,128]{3,2,1,0:T(8,128)} custom-call(bf16[1536,2048]{1,0:T(8,128)(2,1)} %get-tuple-element.56.qkv_ref), custom_call_target="tpu_custom_call" | custom-call | flops 110000000 | tf_op jit(solution)/shard_map/key_state/pallas_call | solution.py:306
  73.0 1.3 collective-permute-start
  74.3 0.6 fusion.14
  75.6 0.6 pad_add_fusion.count_ref
  76.2 1.3 collective-permute-done.1.init_ref
  77.5 0.8 copy-done.6
  78.3 20.2 %attend.2 = (bf16[1024,2048]{1,0:T(8,128)(2,1)}, f32[2,8,2048]{2,1,0:T(8,128)}, bf16[16,8,160,176]{3,2,1,0:T(8,128)(2,1)}) custom-call(bf16[1536,2048]{1,0:T(8,128)(2,1)} %get-tuple-element.56.qkv_ref, f32[4,3,72,128]{3,2,1,0:T(8,128)} %copy-done.6), custom_call_target="tpu_custom_call" | custom-call | flops 360000000 | tf_op jit(solution)/shard_map/attend/pallas_call | solution.py:329
  98.5 0.8 copy-done.7
  99.2 20.1 %attend.3 = (bf16[1024,2048]{1,0:T(8,128)(2,1)}, f32[2,8,2048]{2,1,0:T(8,128)}, bf16[16,8,160,176]{3,2,1,0:T(8,128)(2,1)}) custom-call(bf16[1536,2048]{1,0:T(8,128)(2,1)} %get-tuple-element.56.qkv_ref, f32[4,3,72,128]{3,2,1,0:T(8,128)} %copy-done.7, ...), custom_call_target="tpu_custom_call", output_to_operand_aliasing={{0}: (2, {}), {1}: (3, {}), {2}: (4, {})} | custom-call | flops 360000000 | tf_op jit(solution)/shard_map/attend/pallas_call | solution.py:329
  119.3 23.8 %all-gather.2.cloned.1.call-done.late_ref = bf16[1024,9472]{1,0:T(8,128)(2,1)} async-done(((bf16[32,9472]{1,0:T(8,128)(2,1)}), bf16[1024,9472]{1,0:T(8,128)(2,1)}) %all-gather.2.cloned.1.call-update) | async-done | bytes 19398672 | tf_op jit(solution)/shard_map/all_gather | solution.py:1345
  143.1 103.2 %feed_forward.1 = (bf16[1,2048,1024]{2,1,0:T(8,128)(2,1)}, bf16[1024,2048]{1,0:T(8,128)(2,1)}, bf16[2048,2816]{1,0:T(8,128)(2,1)}, bf16[1024,2048]{1,0:T(8,128)(...) custom-call(s32[2]{0:T(128)} %pad_add_fusion.count_ref, ...), custom_call_target="tpu_custom_call" | custom-call | flops 1589137920 | tf_op jit(solution)/shard_map/feed_forward/pallas_call | solution.py:1177
  246.3 12.6 %query_state.1 = (bf16[16,80,2048]{2,1,0:T(8,128)(2,1)}, f32[8,3,72,128]{3,2,1,0:T(8,128)}) custom-call(bf16[1536,2048]{1,0:T(8,128)(2,1)} %get-tuple-element.56.qkv_ref, bf16[1024,2048]{1,0:T(8,128)(2,1)} %get-tuple-element.65.grad_ref, bf16[1024,2048]{1,0:T(8,128)(2,1)} %get-tuple-element.83.mixed_ref.left_ref, f32[2,8,2048]{2,1,0:T(8,128)} %get-tuple-element.66.den_ref), custom_call_target="tpu_custom_call" | custom-call | flops 260000000 | tf_op jit(solution)/shard_map/query_state/pallas_call | solution.py:354
  258.9 18.5 %weight_grad.6 = bf16[1024,2816]{1,0:T(8,128)(2,1)} custom-call(s32[1]{0:T(128)} %bitcast.6.pick_ref, bf16[1024,2048]{1,0:T(8,128)(2,1)} %get-tuple-element.75.left_ref, bf16[2048,5632]{1,0:T(8,128)(2,1)} %get-tuple-element.72.right_ref), custom_call_target="tpu_custom_call" | custom-call | flops 236223200 | tf_op jit(solution)/shard_map/weight_grad/pallas_call | solution.py:1250
  277.8 11.4 %weight_grad.7 = bf16[1024,1408]{1,0:T(8,128)(2,1)} custom-call(s32[1]{0:T(128)} %bitcast.6.pick_ref, bf16[1024,2048]{1,0:T(8,128)(2,1)} %get-tuple-element.80.left_ref, bf16[2048,2816]{1,0:T(8,128)(2,1)} %get-tuple-element.74.right_ref), custom_call_target="tpu_custom_call" | custom-call | flops 118111600 | tf_op jit(solution)/shard_map/weight_grad/pallas_call | solution.py:1250
  289.4 1.3 collective-permute-start.3
  290.7 19.4 %weight_grad.8 = bf16[1024,2816]{1,0:T(8,128)(2,1)} custom-call(s32[1]{0:T(128)} %bitcast.5.pick_ref, bf16[1024,2048]{1,0:T(8,128)(2,1)} %get-tuple-element.75.left_ref, bf16[2048,5632]{1,0:T(8,128)(2,1)} %get-tuple-element.72.right_ref, bf16[1024,2816]{1,0:T(8,128)(2,1)} %collective-permute-done.2.refs_0_), custom_call_target="tpu_custom_call" | custom-call | flops 236223200 | tf_op jit(solution)/shard_map/weight_grad/pallas_call | solution.py:1250
  310.1 3.1 fusion.15
  313.2 1.3 dynamic-slice_bitcast_fusion
  314.5 1.2 dynamic-slice_bitcast_fusion.1
  316.1 4.8 collective-permute-start.6
  320.9 0.6 collective-permute-start.7
  321.5 5.5 %weight_grad.9 = bf16[1024,512]{1,0:T(8,128)(2,1)} custom-call(s32[1]{0:T(128)} %bitcast.6.pick_ref, bf16[1024,2048]{1,0:T(8,128)(2,1)} %get-tuple-element.83.mixed_ref.left_ref, bf16[2048,1024]{1,0:T(8,128)(2,1)} %get-tuple-element.79.right_ref), custom_call_target="tpu_custom_call" | custom-call | flops 42949672 | tf_op jit(solution)/shard_map/weight_grad/pallas_call | solution.py:1250
  327.9 1.5 copy-done.1
  329.5 11.7 %weight_grad.10 = bf16[1024,1408]{1,0:T(8,128)(2,1)} custom-call(s32[1]{0:T(128)} %bitcast.5.pick_ref, bf16[1024,2048]{1,0:T(8,128)(2,1)} %get-tuple-element.80.left_ref, bf16[2048,2816]{1,0:T(8,128)(2,1)} %get-tuple-element.74.right_ref, bf16[1024,1408]{1,0:T(8,128)(2,1)} %copy-done.1), custom_call_target="tpu_custom_call" | custom-call | flops 118111600 | tf_op jit(solution)/shard_map/weight_grad/pallas_call | solution.py:1250
  341.2 5.9 %weight_grad.11 = bf16[1024,512]{1,0:T(8,128)(2,1)} custom-call(s32[1]{0:T(128)} %bitcast.5.pick_ref, bf16[1024,2048]{1,0:T(8,128)(2,1)} %get-tuple-element.83.mixed_ref.left_ref, bf16[2048,1024]{1,0:T(8,128)(2,1)} %get-tuple-element.79.right_ref, bf16[1024,512]{1,0:T(8,128)(2,1)} %collective-permute-done.5.refs_0_), custom_call_target="tpu_custom_call" | custom-call | flops 42949672 | tf_op jit(solution)/shard_map/weight_grad/pallas_call | solution.py:1250
  347.1 3.3 pad_maximum_fusion
  350.4 2.8 collective-permute-done.6
  353.2 1.5 collective-permute-done.7
  354.6 64.8 %attend_back.1 = (bf16[1536,2048]{1,0:T(8,128)(2,1)}, bf16[2,32,2816]{2,1,0:T(8,128)(2,1)}, bf16[4,2,32,2048]{3,2,1,0:T(8,128)(2,1)}) custom-call(bf16[1536,2048]{1,0:T(8,128)(2,1)} %get-tuple-element.56.qkv_ref, bf16[16,80,2048]{2,1,0:T(8,128)(2,1)} %get-tuple-element.68.nb_ref, bf16[16,8,160,176]{3,2,1,0:T(8,128)(2,1)} %get-tuple-element.69.saved_ref, ...), custom_call_target="tpu_custom_call" | custom-call | flops 1060000000 | tf_op jit(solution)/shard_map/attend_back/pallas_call | solution.py:394
  419.5 49.3 %last_gradients.1 = (f32[1,2048,1024]{2,1,0:T(8,128)}, bf16[2,32,768]{2,1,0:T(8,128)(2,1)}, bf16[2,32,2048]{2,1,0:T(8,128)(2,1)}) custom-call(bf16[1024,2048]{1,0:T(8,128)(2,1)} %get-tuple-element.63.normed_ref, bf16[1536,2048]{1,0:T(8,128)(2,1)} %get-tuple-element.90.back_ref, bf16[1536,1024]{1,0:T(8,128)(2,1)} %get-tuple-element.91.flipped_ref, ...), custom_call_target="tpu_custom_call" | custom-call | flops 515396064 | tf_op jit(solution)/shard_map/last_gradients/pallas_call | solution.py:1019
  468.8 1.0 slice_bitcast_fusion.3
  469.8 0.8 slice_bitcast_fusion.5
  470.6 0.8 fusion.17
  472.0 1.3 convert_reduce_fusion
  473.9 0.7 copy.43
  474.6 0.7 copy.44
  475.3 0.8 fusion.9
  476.1 1.1 multiply_reduce_fusion
  477.1 0.5 convert_divide_fusion
  477.7 0.7 maximum_convert_fusion.1
  479.6 8.4 %copy.49 = f32[1,2048,1024]{2,1,0:T(8,128)} copy(f32[1,2048,1024]{2,1,0:T(8,128)} %get-tuple-element.158) | data formatting | bytes 16777216
  (54 shorter events, 3.0 us)
Async XLA Ops:
  7.2 135.9 %all-gather.2.cloned.1.call-start = ((), (), s32[]{:S(2)}) async-start(), calls=%async_computation | async-start | bytes 20004864 | tf_op jit(solution)/shard_map/all_gather | solution.py:1345
  63.5 10.9 %copy-start.14 = (s32[16]{0:T(128)S(1)}, s32[16]{0:T(128)}, u32[]{:S(2)}) copy-start(s32[16]{0:T(128)} %param.14) | copy-start | bytes 196
  63.5 14.1 %collective-permute-start.1 = (f32[4,3,72,128]{3,2,1,0:T(8,128)}, f32[4,3,72,128]{3,2,1,0:T(8,128)S(1)}, u32[]{:S(2)}, u32[]{:S(2)}) collective-permute-start(f32[4,3,72,128]{3,2,1,0:T(8,128)} %key_state.2), channel_id=1, source_target_pairs={{0,16},{1,17},{2,18},{3,19},{4,20},{5,21},{6,22},{7,23},{8,24},{9,... | collective-permute-start | bytes 1327112 | tf_op jit(solution)/shard_map/ppermute | solution.py:1306
  73.0 25.5 %collective-permute-start = (f32[4,3,72,128]{3,2,1,0:T(8,128)}, f32[4,3,72,128]{3,2,1,0:T(8,128)S(1)}, u32[]{:S(2)}, u32[]{:S(2)}) collective-permute-start(f32[4,3,72,128]{3,2,1,0:T(8,128)} %key_state.3), channel_id=1, source_target_pairs={{0,16},{1,17},{2,18},{3,19},{4,20},{5,21},{6,22},{7,23},{8,24},{9,... | collective-permute-start | bytes 1327112 | tf_op jit(solution)/shard_map/ppermute | solution.py:1306
  77.5 0.8 copy-start.6
  98.5 0.8 copy-start.7
  277.4 13.3 %collective-permute-start.2 = (bf16[1024,2816]{1,0:T(8,128)(2,1)}, bf16[1024,2816]{1,0:T(8,128)(2,1)}, u32[]{:S(2)}, u32[]{:S(2)}) collective-permute-start(bf16[1024,2816]{1,0:T(8,128)(2,1)} %weight_grad.6), channel_id=1, source_target_pairs={{0,1},{1,0},{2,3},{3,2},{4,5},{5,4},{6,7},{7,6},{8,9},{9,8},{10,11... | collective-permute-start | bytes 17301512 | tf_op jit(solution)/shard_map/ppermute | solution.py:1266
  289.2 38.7 %collective-permute-start.4 = (bf16[1024,1408]{1,0:T(8,128)(2,1)}, bf16[1024,1408]{1,0:T(8,128)(2,1)S(1)}, u32[]{:S(2)}, u32[]{:S(2)}) collective-permute-start(bf16[1024,1408]{1,0:T(8,128)(2,1)} %weight_grad.7), channel_id=1, source_target_pairs={{0,1},{1,0},{2,3},{3,2},{4,5},{5,4},{6,7},{7,6},{8,9},{9,8},{10,11... | collective-permute-start | bytes 8650760 | tf_op jit(solution)/shard_map/ppermute | solution.py:1266
  289.4 26.7 %collective-permute-start.3 = (f32[8,3,72,128]{3,2,1,0:T(8,128)}, f32[8,3,72,128]{3,2,1,0:T(8,128)S(1)}, u32[]{:S(2)}, u32[]{:S(2)}) collective-permute-start(f32[8,3,72,128]{3,2,1,0:T(8,128)} %get-tuple-element.76), channel_id=1, source_target_pairs={{16,0},{17,1},{18,2},{19,3},{20,4},{21,5},{22,6},{23,7},{24,8},{25... | collective-permute-start | bytes 2654216 | tf_op jit(solution)/shard_map/ppermute | solution.py:1306
  316.1 10.9 %copy-start.2 = (f32[8,3,72,128]{3,2,1,0:T(8,128)}, f32[8,3,72,128]{3,2,1,0:T(8,128)S(1)}, u32[]{:S(2)}) copy-start(f32[8,3,72,128]{3,2,1,0:T(8,128)S(1)} %collective-permute-done.3.init_ref) | copy-start | bytes 2654212
  316.1 37.1 %collective-permute-start.6 = (bf16[4,2,64,1408]{3,2,1,0:T(8,128)(2,1)}, bf16[4,2,64,1408]{3,2,1,0:T(8,128)(2,1)}, u32[]{:S(2)}, u32[]{:S(2)}) collective-permute-start(bf16[4,2,64,1408]{3,2,1,0:T(8,128)(2,1)} %dynamic-slice_bitcast_fusion.1), channel_id=1, source_target_pairs={{0,16},{16,0},{1,17},{17,1},{2,18},{18,2},{3,19},{19,3},{4,20},{20... | collective-permute-start | bytes 4325384 | tf_op jit(solution)/shard_map/ppermute | solution.py:1281
  320.9 33.8 %collective-permute-start.7 = (bf16[2,4,64,1408]{3,2,1,0:T(8,128)(2,1)}, bf16[2,4,64,1408]{3,2,1,0:T(8,128)(2,1)}, u32[]{:S(2)}, u32[]{:S(2)}) collective-permute-start(bf16[2,4,64,1408]{3,2,1,0:T(8,128)(2,1)} %dynamic-slice_bitcast_fusion), channel_id=1, source_target_pairs={{0,2},{2,0},{1,3},{3,1},{4,6},{6,4},{5,7},{7,5},{8,10},{10,8},{9,1... | collective-permute-start | bytes 4325384 | tf_op jit(solution)/shard_map/ppermute | solution.py:1281
  321.5 5.6 %copy-start.11 = (bf16[32,256]{1,0:T(8,128)(2,1)S(1)}, bf16[32,256]{1,0:T(8,128)(2,1)}, u32[]{:S(2)}) copy-start(bf16[32,256]{1,0:T(8,128)(2,1)} %param.16) | copy-start | bytes 49156
  321.5 5.7 %copy-start.12 = (bf16[32,256]{1,0:T(8,128)(2,1)S(1)}, bf16[32,256]{1,0:T(8,128)(2,1)}, u32[]{:S(2)}) copy-start(bf16[32,256]{1,0:T(8,128)(2,1)} %param.17) | copy-start | bytes 49156
  327.0 14.2 %collective-permute-start.5 = (bf16[1024,512]{1,0:T(8,128)(2,1)}, bf16[1024,512]{1,0:T(8,128)(2,1)}, u32[]{:S(2)}, u32[]{:S(2)}) collective-permute-start(bf16[1024,512]{1,0:T(8,128)(2,1)} %weight_grad.9), channel_id=1, source_target_pairs={{0,1},{1,0},{2,3},{3,2},{4,5},{5,4},{6,7},{7,6},{8,9},{9,8},{10,11... | collective-permute-start | bytes 3145736 | tf_op jit(solution)/shard_map/ppermute | solution.py:1266
  327.9 1.5 copy-start.1
  341.2 5.9 %copy-start = (bf16[1024,1408]{1,0:T(8,128)(2,1)S(1)}, bf16[1024,1408]{1,0:T(8,128)(2,1)}, u32[]{:S(2)}) copy-start(bf16[1024,1408]{1,0:T(8,128)(2,1)} %weight_grad.10) | copy-start | bytes 8650756
  341.2 5.9 %copy-start.9 = (bf16[1024,128]{1,0:T(8,128)(2,1)S(1)}, bf16[1024,128]{1,0:T(8,128)(2,1)}, u32[]{:S(2)}) copy-start(bf16[1024,128]{1,0:T(8,128)(2,1)} %get-tuple-element.84) | copy-start | bytes 786436
  419.5 53.9 %copy-start.8 = (bf16[2,32,2816]{2,1,0:T(8,128)(2,1)S(1)}, bf16[2,32,2816]{2,1,0:T(8,128)(2,1)}, u32[]{:S(2)}) copy-start(bf16[2,32,2816]{2,1,0:T(8,128)(2,1)} %get-tuple-element.97) | copy-start | bytes 1081348
  468.8 5.0 %copy-start.10 = (bf16[32,1024]{1,0:T(8,128)(2,1)S(1)}, bf16[32,1024]{1,0:T(8,128)(2,1)}, u32[]{:S(2)}) copy-start(bf16[32,1024]{1,0:T(8,128)(2,1)} %param.18) | copy-start | bytes 196612
  468.8 7.3 %copy-start.3 = (bf16[32,2752]{1,0:T(8,128)(2,1)S(1)}, bf16[32,2752]{1,0:T(8,128)(2,1)}, u32[]{:S(2)}) copy-start(bf16[32,2752]{1,0:T(8,128)(2,1)} %param.22) | copy-start | bytes 528388
  468.8 7.3 %copy-start.4 = (bf16[32,2752]{1,0:T(8,128)(2,1)S(1)}, bf16[32,2752]{1,0:T(8,128)(2,1)}, u32[]{:S(2)}) copy-start(bf16[32,2752]{1,0:T(8,128)(2,1)} %param.21) | copy-start | bytes 528388
  468.8 8.3 %copy-start.15 = (bf16[32]{0:T(256)(128)(2,1)S(1)}, bf16[32]{0:T(256)(128)(2,1)}, u32[]{:S(2)}) copy-start(bf16[32]{0:T(256)(128)(2,1)} %param.20) | copy-start | bytes 196
  468.8 10.3 %copy-start.13 = (bf16[32]{0:T(256)(128)(2,1)S(1)}, bf16[32]{0:T(256)(128)(2,1)}, u32[]{:S(2)}) copy-start(bf16[32]{0:T(256)(128)(2,1)} %param.15) | copy-start | bytes 196
  473.8 14.3 %copy-start.5 = (f32[32,1024]{1,0:T(8,128)}, f32[32,1024]{1,0:T(8,128)S(1)}, u32[]{:S(2)}) copy-start(f32[32,1024]{1,0:T(8,128)S(1)} %reshape.73) | copy-start | bytes 393220
Sparse Core Ops, SparseCore 0:
  11.4 131.6 all-gather.1
